TPU v7x, 32 devices: a whole 2x2x4 slice. The times are simulated.
32 devices in a mesh: ra: 4 (over z), dec: 4 (over y, x), band: 2 (over core).
Axes of the slice: x: 2, y: 2, z: 4, core: 2. Of those that a mesh axis runs over, the one named last changes fastest.
Arguments:
- morphology: bfloat16 [4, 4, 128, 4096], P('ra', 'dec'), may hold values from 0 to 1
- sed_amps: float32 [4, 4, 6, 128], P('ra', 'dec', 'band'), may hold values from 0.1 to 2
- slot_lists: int32 [4, 4, 5, 128], P('ra', 'dec'), may hold values from 0 to 16, as said below
- morph_step: float32 [4, 4, 128], P('ra', 'dec'), may hold values from 0.01 to 0.04
- sed_step: float32 [4, 4, 128], P('ra', 'dec'), may hold values from 9.765625e-06 to 3.90625e-05
- psf_kernels: bfloat16 [6, 32, 4096], P('band', 'ra'), may hold values from -0.75 to 0.75
- observed: bfloat16 [4, 4, 6, 16, 4096], P('ra', 'dec', 'band'), may hold values from -16 to 16
Outputs:
- morph_out: float32 [4, 4, 128, 4096], P('ra', 'dec', None, 'band')
- sed_out: float32 [4, 4, 6, 128], P('ra', 'dec', 'band')
Inputs may be any that keep to these rules, and one draw needn't show every extreme that they name: `slot_lists`: in each home tile the sources 0 to some count - 1 are live (the count at least 32, and 128 in some tile); a live source has a slot below 16 in row 0; every other entry of a dead source is 16. No source lands beyond the declination edges. Each of rows 1 to 4 of a home tile holds at most 32 entries below 16, and some tile's row 1 holds exactly 32.
All inputs are finite; a program needn't handle non-finite values.
Results may differ from a plain program's by a relative error of at most 0.015.
Values may be sent and summed in bfloat16 or wider, within the bound.
No kernel may reach another device: no remote copies, remote signals or barrier semaphores. Data moves between devices by JAX's collectives and lax.ppermute only.
A program may use at most 256 MiB of HBM per device.

v0:
```python
import functools

import jax
import jax.numpy as jnp
from jax import lax
from jax.experimental import pallas as pl
from jax.experimental.pallas import tpu as pltpu
from jax.sharding import PartitionSpec as P

SIDE = 64
KERN = 32
ITERS = 2
CAP = 32
LANES = 128
ROWS = SIDE * SIDE // LANES
HALF = ROWS // 2
WIDE = 4 * SIDE
ORDER, KERNEL_OF, SLOT_OF, COUNT = range(4)
NEAR = 4
GROUP = 4
STRIDE = 4
F32 = jnp.float32
BF16 = jnp.bfloat16


def dot(a, b):
    return lax.dot_general(a, b, (((1,), (0,)), ((), ())), preferred_element_type=F32)


def dot_nt(a, b):
    return lax.dot_general(a, b, (((1,), (1,)), ((), ())), preferred_element_type=F32)


def iota(shape, dim):
    return lax.broadcasted_iota(jnp.int32, shape, dim)


def low_lanes(rows, dtype=F32):
    return (iota((rows, LANES), 1) < SIDE).astype(F32).astype(dtype)


def lane_sums(rows):
    coarse = rows.astype(BF16)
    fine = (rows - coarse.astype(F32)).astype(BF16)
    ones = jnp.ones((8, rows.shape[1]), BF16)
    return dot_nt(ones, coarse) + dot_nt(ones, fine)


def half_masks(rows):
    low = iota((rows, LANES), 1) < SIDE
    return low, jnp.logical_not(low)


def turned(value):
    return pltpu.roll(value, SIDE, 1)


def twofold(packed):
    low, flip = half_masks(ROWS)[0], turned(packed)
    return jnp.concatenate([jnp.where(low, packed, flip), jnp.where(low, flip, packed)], axis=0)


def half_rows():
    return pl.multiple_of(lax.axis_index("band") * HALF, HALF)


def by_core(mine, theirs):
    first = lax.axis_index("band") == 0
    return jnp.where(first, mine, theirs), jnp.where(first, theirs, mine)


def lists_kernel(num_slots, slots_ref, hots, places):
    slots = slots_ref[...]
    sources = slots.shape[1]
    valid = (slots < num_slots).astype(F32)
    upper = (iota((sources, sources), 0) <= iota((sources, sources), 1)).astype(F32)
    rank = dot(valid.astype(BF16), upper.astype(BF16))
    place = iota((LANES, sources), 0).astype(F32)
    names = iota((8, sources), 1).astype(F32).astype(BF16)
    for near in range(NEAR):
        row = slice(near + 1, near + 2)
        hot = ((place == rank[row] - 1.0).astype(F32) * valid[row]).astype(BF16)
        hots[near] = hot
        places[near : near + 1, :] = dot_nt(names, hot)[:1].astype(jnp.int32)
        count = jnp.broadcast_to(rank[row, sources - 1 :], (1, LANES))
        places[NEAR + near : NEAR + near + 1, :] = count.astype(jnp.int32)


def write_messages(messages, slots, amps, hots, places, stamps):
    first = lax.axis_index("band") == 0
    row = iota((ROWS, slots.shape[1]), 0)
    for turn in range(2):
        near = 2 * turn + lax.axis_index("band")

        def pick(n, carry, near=near, turn=turn):
            messages[turn][n] = stamps[places[near, n]]
            return carry

        lax.fori_loop(0, CAP, pick, 0, unroll=8)
        slot = jnp.where(first, slots[2 * turn + 1 : 2 * turn + 2], slots[2 * turn + 2 : 2 * turn + 3]).astype(F32)
        meta = jnp.where(row == 0, slot + 1.0, 0.0)
        meta = jnp.where(row == 1, slots[0:1].astype(F32), meta)
        for band in range(amps.shape[0]):
            meta = jnp.where(row == 2 + band, amps[band : band + 1], meta)
        hot = jnp.where(first, hots[2 * turn].astype(F32), hots[2 * turn + 1].astype(F32)).astype(BF16)
        messages[turn][CAP] = dot_nt(meta.astype(BF16), hot).astype(BF16)


def pack_kernel(places, slots_ref, amps_mine, amps_theirs, hots, morph, *out):
    messages, amps_out, amps_q = out[:2], out[2], out[3]
    amps = jnp.concatenate(by_core(amps_mine[...], amps_theirs[...]), axis=0)
    write_messages(messages, slots_ref[...], amps, hots, places, morph)
    amps_out[...] = amps
    amps_q[...] = amps.astype(BF16).astype(F32)


def order_kernel(num_slots, *refs):
    plan, amps = refs[NEAR:]
    none = NEAR * CAP
    bands = amps.shape[0]
    meta = jnp.zeros((ROWS, LANES), F32)
    for turn in range(2):
        pair = by_core(refs[turn][CAP].astype(F32), refs[2 + turn][CAP].astype(F32))
        for core in range(2):
            meta = meta + pltpu.roll(pair[core], (2 * turn + core) * CAP, 1)
    slot, kernel = meta[0:1], meta[1:2]
    amps[...] = by_core(meta[2 : 2 + bands], meta[2 + bands : 2 + 2 * bands])[0]
    plan[SLOT_OF : SLOT_OF + 1, :LANES] = jnp.maximum(slot - 1.0, 0.0).astype(jnp.int32)
    live = (slot > 0.0).astype(F32)
    hot = (iota((num_slots, none), 0).astype(F32) == kernel).astype(F32) * live
    upto = (iota((none, none), 0) <= iota((none, none), 1)).astype(F32).astype(BF16)
    rank = dot(hot.astype(BF16), upto)
    size = jnp.max(rank, axis=1, keepdims=True)
    filled = ((size.astype(jnp.int32) + (GROUP - 1)) // GROUP).astype(F32)
    before = (iota((num_slots, num_slots), 1) < iota((num_slots, num_slots), 0)).astype(F32).astype(BF16)
    start = dot(before, jnp.broadcast_to(filled, (num_slots, none)).astype(BF16))
    place = jnp.sum(hot * (GROUP * start + rank), axis=0, keepdims=True) - 1.0
    eight = iota((8, none), 0)
    names = jnp.where(eight == 0, iota((8, none), 1).astype(F32) - none, 0.0).astype(BF16)
    for part in range(plan.shape[1] // LANES):
        at = (iota((LANES, none), 0) + part * LANES).astype(F32)
        hit = (at == place).astype(F32) * live
        found = dot_nt(names, hit.astype(BF16))[:1] + none
        plan[ORDER : ORDER + 1, part * LANES : (part + 1) * LANES] = found.astype(jnp.int32)
    chunk = iota((num_slots, LANES), 1).astype(F32)
    row = iota((num_slots, LANES), 0).astype(F32)
    inside = (chunk >= start[:, :LANES]) & (chunk < start[:, :LANES] + filled)
    kernels = jnp.sum(jnp.where(inside, row, 0.0), axis=0, keepdims=True)
    plan[KERNEL_OF : KERNEL_OF + 1, :LANES] = kernels.astype(jnp.int32)
    total = jnp.sum(filled, axis=0, keepdims=True)
    plan[COUNT : COUNT + 1, :LANES] = jnp.broadcast_to(total, (1, LANES)).astype(jnp.int32)


def quarter_start(quarter, held):
    parity, line = lax.axis_index("ra") % 2, lax.axis_index("dec") % 2
    shard = parity if quarter % 2 == 0 else 1 - parity
    half = line if quarter < 2 else 1 - line
    return (2 * shard + half) * held


def tables_kernel(bands, earlier, *refs):
    shards, (first_t, left, left_t, right, packed) = refs[: len(refs) - 5 - 4 * earlier], refs[-5:]
    held = shards[0].shape[1]
    for turn, ref in enumerate(shards):
        for band in range(bands):
            for r in range(ROWS):
                rows = pl.ds(turn * held * ROWS + r, held, stride=ROWS)
                packed[band, rows, :] = ref[band, :, r * LANES : (r + 1) * LANES].astype(F32)
    starts = [quarter_start(2 + turn, held) if earlier else turn * held for turn in range(len(shards))]
    if earlier:
        old_first, old_left, old_left_t, old_right = refs[len(shards) : len(shards) + 4]
        for turn in range(2):
            old, new = pl.ds(turn * held, held), pl.ds(quarter_start(turn, held), held)
            first_t[new] = old_first[old]
            right[new] = old_right[old]
            for band in range(bands):
                left[band, new] = old_left[band, old]
                left_t[band, new] = old_left_t[band, old]
    eye = (iota((SIDE, SIDE), 0) == iota((SIDE, SIDE), 1)).astype(F32).astype(BF16)
    row, col = iota((SIDE, SIDE), 0), iota((SIDE, SIDE), 1)
    even = (col == 2 * (row % ROWS) + row // ROWS).astype(F32).astype(BF16)
    even_t = (row == 2 * (col % ROWS) + col // ROWS).astype(F32).astype(BF16)
    rest = [jnp.zeros((SIDE * (4 - bands), SIDE), BF16)] if bands < 4 else []
    for turn, start in enumerate(starts):

        def step(place, carry, turn=turn, start=start):
            k = start + place
            at = pl.multiple_of((turn * held + place) * ROWS, ROWS)
            parts = [twofold(packed[band, pl.ds(at, ROWS), :]).astype(BF16) for band in range(bands)]
            lefts = dot_nt(jnp.concatenate([part[:, :SIDE] for part in parts], axis=0), even).astype(BF16)
            natural = []
            for band, part in enumerate(parts):
                rows = slice(band * SIDE, (band + 1) * SIDE)
                left[band, k] = lefts[rows]
                left_t[band, k] = dot_nt(eye, lefts[rows]).astype(BF16)
                both = dot(even_t, part).astype(BF16)
                right[k, rows, :] = both
                natural.append(both[:, :SIDE])
            if rest:
                right[k, bands * SIDE :, :] = jnp.zeros((SIDE * (4 - bands), LANES), BF16)
            first_t[k] = dot_nt(eye, jnp.concatenate(natural + rest, axis=0)).astype(BF16)
            return carry

        lax.fori_loop(0, held, step, 0, unroll=min(held, 4))


def make_tables(shards, bands, earlier=()):
    count = sum(x.shape[1] for x in shards)
    total = count + sum(x.shape[0] for x in earlier[:1])
    square = ((bands, total, SIDE, SIDE), BF16, False)
    return call(
        functools.partial(tables_kernel, bands, bool(earlier)),
        "tables",
        (*shards, *earlier),
        0,
        [((total, SIDE, WIDE), BF16, False), square, square, ((total, WIDE, LANES), BF16, False)],
        [((bands, count * ROWS, LANES), F32)],
        flops=2 * 10**9,
        moved=5 * 2**20,
    )


def home_sums_kernel(bands, lists, amps, morph, sums):
    first = lax.axis_index("band") * bands
    sums[...] = jnp.zeros_like(sums)

    def add(s, carry):
        q = lists[0, s]
        stamp = morph[s].astype(F32)
        for band in range(bands):
            sums[band, q] += amps[first + band, s] * stamp
        return carry

    lax.fori_loop(0, lists.shape[1], add, 0, unroll=4)


def home_forward_kernel(bands, sums, first_t, left, total, inner_all):
    num_slots = total.shape[1]
    masks = half_masks(SIDE)

    def inner_products(q, carry):
        images = []
        for band in range(bands):
            both = sums[band, q]
            images += [both[:, :SIDE], turned(both)[:, :SIDE]]
        inners = dot(jnp.concatenate(images, axis=0).astype(BF16), first_t[q])
        for band in range(bands):
            lanes = slice(band // 2 * LANES, (band // 2 + 1) * LANES)
            inner_all[band, q] = inners[band * SIDE : (band + 1) * SIDE, lanes].astype(BF16)
        return carry

    def slot(q, carry):
        for band in range(bands):
            total[band, q] = jnp.where(masks[band % 2], dot(left[band, q], inner_all[band, q]), 0.0)
        return carry

    lax.fori_loop(0, num_slots, inner_products, 0, unroll=4)
    lax.fori_loop(0, num_slots, slot, 0, unroll=4)


def chunk_reader(bands, plan, amps):
    none = NEAR * CAP

    def read(c):
        members = [plan[ORDER, c * GROUP + u] for u in range(GROUP)]
        held = [jnp.minimum(v, none - 1) for v in members]
        values = [[jnp.where(v < none, amps[band, h], 0.0) for v, h in zip(members, held)] for band in range(bands)]
        return plan[KERNEL_OF, c], members, [plan[SLOT_OF, h] for h in held], values

    return read, (plan[COUNT, 0] + STRIDE - 1) // STRIDE


def forward_kernel(bands, plan, amps, *refs):
    home, observed, first_t, left = refs[NEAR : NEAR + 4]
    residual, inner_all, stamps, *totals = refs[NEAR + 4 :]
    totals = [totals[2 * band : 2 * band + 2] for band in range(bands)]
    num_slots = home.shape[1]
    none = NEAR * CAP
    core = lax.axis_index("band")
    for source, near in enumerate((core, 2 + core, 1 - core, 3 - core)):
        group = pl.ds(near * CAP, CAP)
        even = refs[source][pl.ds(0, CAP)].astype(F32)
        odd = turned(even.reshape(CAP * ROWS, LANES)).reshape(CAP, ROWS, LANES)
        stamps[group, pl.ds(0, ROWS), :] = even.astype(BF16)
        stamps[group, pl.ds(ROWS, ROWS), :] = odd.astype(BF16)
    stamps[none] = jnp.zeros((SIDE, LANES), BF16)
    for band in range(bands):
        totals[band][band % 2][...] = home[band]
        totals[band][1 - band % 2][...] = jnp.zeros_like(home[band])
    masks, row_masks = half_masks(SIDE), half_masks(1)
    read, rounds = chunk_reader(bands, plan, amps)

    def inner_products(turn, carry):
        for c in [STRIDE * turn + i for i in range(STRIDE)]:
            k, members, _, _ = read(c)
            stack = jnp.concatenate([stamps[v] for v in members], axis=0)
            inners = dot(stack[:, :SIDE], first_t[k])
            for band in range(bands):
                lanes = slice(band // 2 * LANES, (band // 2 + 1) * LANES)
                pairs = []
                for u in range(0, GROUP, 2):
                    x = inners[u * SIDE : (u + 1) * SIDE, lanes]
                    y = inners[(u + 1) * SIDE : (u + 2) * SIDE, lanes]
                    x, y = (x, turned(y)) if band % 2 == 0 else (turned(x), y)
                    pairs.append(jnp.where(masks[0], x, y))
                inner_all[c, band] = jnp.concatenate(pairs, axis=1).astype(BF16)
        return carry

    def images(turn, carry):
        for c in [STRIDE * turn + i for i in range(STRIDE)]:
            k, _, slots, values = read(c)
            for band in range(bands):
                image = dot(left[band, k], inner_all[c, band])
                for u in range(0, GROUP, 2):
                    lanes = slice(u // 2 * LANES, (u // 2 + 1) * LANES)
                    scale = jnp.where(row_masks[0], values[band][u], values[band][u + 1])
                    pair = image[:, lanes] * scale
                    for part in (0, 1):
                        totals[band][part][slots[u + part]] += pair
        return carry

    lax.fori_loop(0, rounds, inner_products, 0)
    lax.fori_loop(0, rounds, images, 0)

    def slot(q, carry):
        for band in range(bands):
            model = jnp.where(masks[0], totals[band][0][q], totals[band][1][q])
            seen = twofold(observed[band, q].astype(F32))
            residual[band, q] = (model + turned(model) - seen).astype(BF16)
        return carry

    lax.fori_loop(0, num_slots, slot, 0, unroll=8)


def backward_kernel(bands, plan, amps, *refs):
    residual, inner_all, left_t, right, keep, send, stacks, sums = refs
    none = NEAR * CAP
    sums[...] = jnp.zeros_like(sums)
    masks, row_masks, packed_low = half_masks(SIDE), half_masks(1), half_masks(ROWS)[0]
    read, rounds = chunk_reader(bands, plan, amps)
    spare = none // 2
    core = lax.axis_index("band")

    def outer_products(turn, carry):
        for c in [STRIDE * turn + i for i in range(STRIDE)]:
            k, members, slots, values = read(c)
            outers = []
            for band in range(bands):
                pairs = [
                    jnp.where(masks[0], residual[band, slots[u]], residual[band, slots[u + 1]])
                    for u in range(0, GROUP, 2)
                ]
                outer = dot(left_t[band, k], jnp.concatenate(pairs, axis=1))
                along = jnp.sum(inner_all[c, band].astype(F32) * outer, axis=0, keepdims=True)
                scaled = []
                for u in range(0, GROUP, 2):
                    lanes = slice(u // 2 * LANES, (u // 2 + 1) * LANES)
                    for part in (0, 1):
                        row = jnp.where(row_masks[part], along[:, lanes], 0.0)
                        sums[band, pl.ds(members[u + part], 1), :] = row
                    scale = jnp.where(row_masks[0], values[band][u], values[band][u + 1])
                    scaled.append(outer[:, lanes] * scale)
                outers.append(scaled)
            outers += [[jnp.zeros((SIDE, LANES), F32)] * (GROUP // 2)] * (4 - bands)
            for pair in range(GROUP // 2):
                b0, b1, b2, b3 = [outers[band][pair] for band in range(4)]
                if bands > 3:
                    last = [jnp.where(masks[0], b2, turned(b3)), jnp.where(masks[0], turned(b2), b3)]
                else:
                    last = [b2, turned(b2)]
                first = [jnp.where(masks[0], b0, turned(b1)), jnp.where(masks[0], turned(b0), b1)]
                for part in (0, 1):
                    rows = slice((2 * pair + part) * SIDE, (2 * pair + part + 1) * SIDE)
                    stacks[c, rows, :] = jnp.concatenate([first[part], last[part]], axis=1).astype(BF16)
        return carry

    def gradients(turn, carry):
        for c in [STRIDE * turn + i for i in range(STRIDE)]:
            k, members, _, _ = read(c)
            grads = dot(stacks[c], right[k])
            for u, v in enumerate(members):
                top = grads[u * SIDE : u * SIDE + ROWS]
                low = grads[u * SIDE + ROWS : (u + 1) * SIDE]
                stamp = jnp.where(packed_low, top, low).astype(BF16)
                side, place = v // CAP % 2, v // (2 * CAP) * CAP + v % CAP
                keep[jnp.where(side == core, place, spare)] = stamp
                send[jnp.where(side == 1 - core, place, spare)] = stamp
        return carry

    lax.fori_loop(0, rounds, outer_products, 0)
    lax.fori_loop(0, rounds, gradients, 0)
    meta = amp_rows([lane_sums(sums[band, :none, :]) for band in range(bands)])
    keep[spare] = meta
    send[spare] = meta


def home_slots_kernel(bands, residual, left_t, right, back):
    num_slots = residual.shape[1]
    back[:, num_slots] = jnp.zeros((bands, ROWS, LANES), BF16)
    packed_low = half_masks(ROWS)[0]

    def slot(q, carry):
        for band in range(bands):
            outer = dot(left_t[band, q], residual[band, q]).astype(BF16)
            grad = dot(outer[:, :SIDE], right[q, band * SIDE : (band + 1) * SIDE, :])
            back[band, q] = jnp.where(packed_low, grad[:ROWS], grad[ROWS:]).astype(BF16)
        return carry

    lax.fori_loop(0, num_slots, slot, 0, unroll=8)


def home_gather_kernel(bands, last, lists, amps, morph, back, received, keep, grad_a, sums):
    core = lax.axis_index("band")
    mine = pl.ds(half_rows(), HALF) if last else pl.ds(0, ROWS)

    def gather(s, carry):
        q = lists[0, s]
        stamp = morph[s].astype(F32)
        grad = jnp.zeros((HALF if last else ROWS, LANES), F32)
        for ref, side in ((back, core), (received, 1 - core)):
            for band in range(bands):
                amp = amps[side * bands + band, s]
                if last:
                    grad = grad + amp * ref[band, q, mine, :].astype(F32)
                    if ref is received:
                        continue
                seen = ref[band, q].astype(F32)
                if not last:
                    grad = grad + amp * seen
                along = jnp.sum(seen * stamp, axis=0, keepdims=True)
                sums[side * bands + band, pl.ds(s, 1), :] = along
        keep[s] = grad
        return carry

    lax.fori_loop(0, lists.shape[1], gather, 0, unroll=4)
    for band in range(grad_a.shape[0]):
        rows = sums[core * bands + band] if last else sums[band]
        grad_a[band : band + 1, :] = lane_sums(rows)[:1]


def amp_rows(sums):
    eight = iota((8, LANES), 0)
    total = jnp.zeros((8, LANES), F32)
    for band, row in enumerate(sums):
        total = jnp.where(eight == band, row, total)
    coarse = total.astype(BF16).astype(F32)
    return jnp.concatenate([coarse, total - coarse, jnp.zeros((HALF, LANES), F32)], axis=0).astype(BF16)


def reduce_kernel(keep, received, *messages):
    for turn in range(2):
        part = pl.ds(turn * CAP, CAP)
        total = keep[part].astype(F32) + received[part].astype(F32)
        messages[turn][pl.ds(0, CAP)] = total.astype(BF16)
        pair = by_core(keep[2 * CAP].astype(F32), received[2 * CAP].astype(F32))
        meta = jnp.concatenate([pair[0][:HALF], pair[1][:HALF]], axis=0)
        messages[turn][CAP] = meta.astype(BF16)


def update_kernel(first, last, places, eta_m, slots_ref, eta_a, hots, amps_ref, grad_a, morph, home, *refs):
    grads, out = refs[:NEAR], refs[NEAR:]
    state, amps_out, work = out[0], out[1], out[-1]
    sources = slots_ref.shape[1]
    core = lax.axis_index("band")
    mine = pl.ds(half_rows(), HALF) if last else pl.ds(0, ROWS)
    nears = (core, 2 + core, 1 - core, 3 - core)
    work[...] = home[...]
    for ref, near in zip(grads, nears):

        def add(n, carry, ref=ref, near=near):
            work[places[near, n]] += ref[n, mine, :].astype(F32)
            return carry

        lax.fori_loop(0, places[NEAR + near, 0], add, 0)

    def step(s, carry):
        new = jnp.maximum(morph[s, mine, :].astype(F32) - eta_m[0, s] * work[s], 0.0)
        if last:
            work[s] = new
        else:
            state[s] = new
            out[2][s] = new.astype(BF16)
        return carry

    lax.fori_loop(0, sources, step, 0, unroll=8)
    if last:
        for r in range(HALF):
            state[:, r * LANES : (r + 1) * LANES] = work[:, r, :]
    lane = iota((ROWS, LANES), 1) // CAP
    meta = jnp.zeros((ROWS, LANES), F32)
    for ref, near in zip(grads, nears):
        meta = jnp.where(lane == near, ref[CAP].astype(F32), meta)
    all_hots = jnp.concatenate([hots[near, :CAP] for near in range(NEAR)], axis=0)
    from_near = dot(meta.astype(BF16), all_hots)
    bands = amps_ref.shape[0] // 2
    sides = [from_near[r : r + bands] + from_near[r + 8 : r + 8 + bands] for r in (0, HALF)]
    if last:
        amps = by_core(amps_ref[:bands], amps_ref[bands:])[0]
        total = grad_a[...] + by_core(sides[0], sides[1])[0]
    else:
        amps = amps_ref[...]
        total = grad_a[...] + jnp.concatenate(sides, axis=0)
    amps = jnp.maximum(amps - eta_a[...] * total, 0.0)
    amps_out[...] = amps
    if last:
        return
    stamps, amps_q, messages = out[2], out[3], out[4:6]
    amps_q[...] = amps.astype(BF16).astype(F32)
    write_messages(messages, slots_ref[...], amps, hots, places, stamps)


def call(body, name, operands, scalars, outs, scratch=(), smem_scratch=(), flops=0, moved=0):
    vmem, smem = pl.BlockSpec(memory_space=pltpu.VMEM), pl.BlockSpec(memory_space=pltpu.SMEM)
    return pl.pallas_call(
        body,
        out_shape=[jax.ShapeDtypeStruct(shape, dtype) for shape, dtype, _ in outs],
        in_specs=[smem if i < scalars else vmem for i in range(len(operands))],
        out_specs=[smem if flag else vmem for _, _, flag in outs],
        scratch_shapes=[pltpu.VMEM(shape, dtype) for shape, dtype in scratch]
        + [pltpu.SMEM(shape, dtype) for shape, dtype in smem_scratch],
        compiler_params=pltpu.CompilerParams(vmem_limit_bytes=40 * 2**20),
        cost_estimate=pl.CostEstimate(flops=flops, bytes_accessed=moved, transcendentals=0),
        name=name,
    )(*operands)


def stepped(value, axis, step):
    shape = [lax.axis_size(name) for name in ("ra", "dec", "band")]

    def device(ra, dec, band):
        return (ra * shape[1] + dec) * shape[2] + band

    pairs = []
    for ra in range(shape[0]):
        for dec in range(shape[1]):
            for band, by in ((0, step), (1, -step)):
                if axis == "ra":
                    pairs.append((device(ra, dec, band), device((ra + by) % shape[0], dec, band)))
                elif 0 <= dec + by < shape[1]:
                    pairs.append((device(ra, dec, band), device(ra, dec + by, band)))
    return lax.ppermute(value, ("ra", "dec", "band"), pairs)


def swapped(value):
    return lax.ppermute(value, "band", [(0, 1), (1, 0)])


def all_tables(psf, num_slots, messages, morph):
    bands, held = psf.shape[:2]
    lines = lax.axis_size("dec")
    if lax.axis_size("ra") == 4 and 2 * held == num_slots and held % 2 == 0 and lines % 2 == 0:
        across = [(i, i + 1 - 2 * (i % 2)) for i in range(lines)]
        along = [(0, 1), (1, 0), (2, 3), (3, 2)]
        mine = jnp.where(lax.axis_index("dec") % 2 == 0, psf[:, : held // 2], psf[:, held // 2 :])
        far = lax.ppermute(mine, "ra", [(0, 2), (1, 3)])
        here = jnp.where(lax.axis_index("ra") < 2, mine, far)
        here, *messages = lax.optimization_barrier((here, *messages))
        near = lax.ppermute(here, "ra", along)
        near, morph, messages[1] = lax.optimization_barrier((near, morph, messages[1]))
        halves = make_tables((here, near), bands)
        others = (lax.ppermute(here, "dec", across), lax.ppermute(near, "dec", across))
        return make_tables(others, bands, halves), messages, morph
    return make_tables((lax.all_gather(psf, "ra", axis=1, tiled=True)[:, :num_slots],), bands), messages, morph


def shards(morphology, sed_amps, slot_lists, morph_step, sed_step, psf_kernels, observed):
    bands, num_slots, sources = sed_amps.shape[2], observed.shape[3], morphology.shape[2]
    lists, amps = slot_lists[0, 0], sed_amps[0, 0]
    eta_m, eta_a = morph_step[0], sed_step[0]
    full = morphology[0, 0].reshape(sources, ROWS, LANES)
    seen = observed[0, 0].reshape(bands, num_slots, ROWS, LANES)
    stamp = ((CAP + 1, ROWS, LANES), BF16, False)
    all_stamps = (sources, ROWS, LANES)
    near_all = NEAR * CAP
    chunks = -(-(near_all // GROUP + num_slots) // STRIDE) * STRIDE
    amps_theirs = swapped(amps)
    hots, places = call(
        functools.partial(lists_kernel, num_slots),
        "lists",
        (lists,),
        0,
        [
            ((NEAR, LANES, sources), BF16, False),
            ((2 * NEAR, LANES), jnp.int32, False),
        ],
        moved=2**20,
    )
    *messages, amps, amps_q = call(
        pack_kernel,
        "pack",
        (places, lists, amps, amps_theirs, hots, full),
        1,
        [stamp] * 2 + [((2 * bands, sources), F32, False)] * 2,
        moved=2**20,
    )
    (first_t, left, left_t, right), messages, morph = all_tables(psf_kernels, num_slots, messages, full)
    state = full
    for sweep in range(ITERS):
        last = sweep == ITERS - 1
        own = [stepped(messages[0], "ra", 1), stepped(messages[1], "dec", 1)]
        sums = call(
            functools.partial(home_sums_kernel, bands),
            "home_sums",
            (lists, amps_q, morph),
            2,
            [((bands, num_slots + 1, ROWS, LANES), F32, False)],
            moved=4 * 2**20,
        )[0]
        home = call(
            functools.partial(home_forward_kernel, bands),
            "home_forward",
            (sums, first_t, left),
            0,
            [((bands, num_slots, SIDE, LANES), F32, False)],
            [((bands, num_slots, SIDE, LANES), BF16)],
            flops=2 * 10**9,
            moved=4 * 2**20,
        )[0]
        home, *own = lax.optimization_barrier((home, *own))
        other = [swapped(x) for x in own]
        order = call(
            functools.partial(order_kernel, num_slots),
            "order",
            (*own, *other),
            0,
            [
                ((8, -(-chunks * GROUP // LANES) * LANES), jnp.int32, False),
                ((bands, LANES), F32, False),
            ],
            moved=2**20,
        )
        residual, inner_all = call(
            functools.partial(forward_kernel, bands),
            "forward",
            (*order, *own, *other, home, seen, first_t, left),
            2,
            [
                ((bands, num_slots, SIDE, LANES), BF16, False),
                ((chunks, bands, SIDE, WIDE), BF16, False),
            ],
            [((near_all + 1, SIDE, LANES), BF16)] + [((num_slots, SIDE, LANES), F32)] * (2 * bands),
            flops=3 * 10**9,
            moved=8 * 2**20,
        )
        half_of_near = ((near_all // 2 + 1, ROWS, LANES), BF16, False)
        keep, send = call(
            functools.partial(backward_kernel, bands),
            "backward",
            (*order, residual, inner_all, left_t, right),
            2,
            [half_of_near] * 2,
            [((chunks, WIDE, WIDE), BF16), ((bands, near_all + 8, LANES), F32)],
            flops=3 * 10**9,
            moved=8 * 2**20,
        )
        received = swapped(send)
        back = call(
            functools.partial(home_slots_kernel, bands),
            "home_slots",
            (residual, left_t, right),
            0,
            [((bands, num_slots + 1, ROWS, LANES), BF16, False)],
            flops=2 * 10**9,
            moved=4 * 2**20,
        )[0]
        back_received = swapped(back)
        received, back_received = lax.optimization_barrier((received, back_received))
        grads = call(reduce_kernel, "reduce", (keep, received), 0, [stamp] * 2, moved=2 * 2**20)
        grads = [stepped(grads[0], "ra", -1), stepped(grads[1], "dec", -1)]
        bands_here = bands if last else 2 * bands
        part = (sources, HALF, LANES) if last else all_stamps
        home_grad, grad_a = call(
            functools.partial(home_gather_kernel, bands, last),
            "home_gather",
            (lists, amps_q, morph, back, back_received),
            2,
            [(part, F32, False), ((bands_here, sources), F32, False)],
            [((2 * bands, sources, LANES), F32)],
            moved=4 * 2**20,
        )
        home_grad, *grads = lax.optimization_barrier((home_grad, *grads))
        grads += [swapped(x) for x in grads]
        outs = [((sources, HALF * LANES) if last else all_stamps, F32, False), ((bands_here, sources), F32, False)]
        if not last:
            outs += [(all_stamps, BF16, False), ((bands_here, sources), F32, False)] + [stamp] * 2
        state, amps, *more = call(
            functools.partial(update_kernel, sweep == 0, last),
            "update",
            (places, eta_m, lists, eta_a, hots, amps, grad_a, state, home_grad, *grads),
            2,
            outs,
            [(part, F32)],
            moved=3 * 2**20,
        )
        if not last:
            morph, amps_q, *messages = more
    return state[None, None], amps[None, None]


def solution(mesh):
    in_specs = (
        P("ra", "dec", None, None),
        P("ra", "dec", "band", None),
        P("ra", "dec", None, None),
        P("ra", "dec", None),
        P("ra", "dec", None),
        P("band", "ra", None),
        P("ra", "dec", "band", None, None),
    )
    out_specs = (P("ra", "dec", None, "band"), P("ra", "dec", "band", None))
    return jax.shard_map(shards, mesh=mesh, in_specs=in_specs, out_specs=out_specs, check_vma=False)
```

profile of v0, /device:TPU:5, one launch (start us, length us, event | category | flops | bytes accessed | tf_op | source)
XLA Modules:
  0.0 113.2 jit_solution(15897141135422084658)
XLA Ops:
  1.8 4.2 %collective-permute-start.1 = (bf16[3,4,4096]{2,1,0:T(4,128)(2,1)S(1)}, bf16[3,4,4096]{2,1,0:T(4,128)(2,1)S(1)}, u32[]{:S(2)}, u32[]{:S(2)}) collective-permute-start(bf16[3,4,4096]{2,1,0:T(4,128)(2,1)S(1)} %slice_select_fusion), channel_id=1, source_target_pairs={{0,16},{8,24},{1,17},{9,25},{2,18},{10,26},{3,19},{11,27},{4,20},{... | collective-permute-start | bytes 294920 | tf_op jit(solution)/shard_map/ppermute | solution.py:555
  13.9 2.2 %collective-permute-start.5 = (bf16[33,32,128]{2,1,0:T(8,128)(2,1)S(1)}, bf16[33,32,128]{2,1,0:T(8,128)(2,1)S(1)}, u32[]{:S(2)}, u32[]{:S(2)}) collective-permute-start(bf16[33,32,128]{2,1,0:T(8,128)(2,1)S(1)} %get-tuple-element.82), channel_id=1, source_target_pairs={{0,8},{1,25},{2,10},{3,27},{4,12},{5,29},{6,14},{7,31},{8,16},{9,1... | collective-permute-start | bytes 811016 | tf_op jit(solution)/shard_map/ppermute | solution.py:541
  17.0 2.3 %collective-permute-start.6 = (bf16[33,32,128]{2,1,0:T(8,128)(2,1)S(1)}, bf16[33,32,128]{2,1,0:T(8,128)(2,1)S(1)}, u32[]{:S(2)}, u32[]{:S(2)}) collective-permute-start(bf16[33,32,128]{2,1,0:T(8,128)(2,1)S(1)} %get-tuple-element.83), channel_id=1, source_target_pairs={{0,2},{2,4},{3,1},{4,6},{5,3},{7,5},{8,10},{10,12},{11,9},{12,14},... | collective-permute-start | bytes 811016 | tf_op jit(solution)/shard_map/ppermute | solution.py:541
  21.2 2.0 %tables.2 = (bf16[8,64,256]{2,1,0:T(8,128)(2,1)S(1)}, bf16[3,8,64,64]{3,2,1,0:T(8,128)(2,1)S(1)}, bf16[3,8,64,64]{3,2,1,0:T(8,128)(2,1)S(1)}, bf16[8,256,128]{2,1,0:T(8,128)(2,1)S(1)}) custom-call(bf16[3,4,4096]{2,1,0:T(4,128)(2,1)S(1)} %broadcast_select_fusion.refs_0_, bf16[3,4,4096]{2,1,0:T(4,128)(2,1)S(1)} %collective-permute-done.2.refs_1_), custom_call_target="tpu_custom_call" | custom-call | flops 2000000000 | bytes 5242880 | tf_op jit(solution)/shard_map/tables/pallas_call | solution.py:514
  23.2 2.0 %tables.3 = (bf16[16,64,256]{2,1,0:T(8,128)(2,1)S(1)}, bf16[3,16,64,64]{3,2,1,0:T(8,128)(2,1)S(1)}, bf16[3,16,64,64]{3,2,1,0:T(8,128)(2,1)S(1)}, bf16[16,256,128]{2,1,0:T(8,128)(2,1)S(1)}) custom-call(bf16[3,4,4096]{2,1,0:T(4,128)(2,1)S(1)} %collective-permute-done.3.refs_0_, bf16[3,4,4096]{2,1,0:T(4,128)(2,1)S(1)} %collective-permute-done.4.refs_1_, ...), custom_call_target="tpu_custom_call" | custom-call | flops 2000000000 | bytes 5242880 | tf_op jit(solution)/shard_map/tables/pallas_call | solution.py:514
  25.2 2.0 %home_forward.2.refs_4_ = f32[3,16,64,128]{3,2,1,0:T(8,128)S(1)} custom-call(f32[3,17,32,128]{3,2,1,0:T(8,128)S(1)} %home_sums.2.sums, bf16[16,64,256]{2,1,0:T(8,128)(2,1)S(1)} %get-tuple-element.80.first_t.refs_6_, bf16[3,16,64,64]{3,2,1,0:T(8,128)(2,1)S(1)} %get-tuple-element.81.left.refs_7_), custom_call_target="tpu_custom_call" | custom-call | flops 2000000000 | bytes 4194304 | tf_op jit(solution)/shard_map/home_forward/pallas_call | solution.py:514
  30.6 5.7 %forward.2 = (bf16[3,16,64,128]{3,2,1,0:T(8,128)(2,1)S(1)}, bf16[48,3,64,256]{3,2,1,0:T(8,128)(2,1)S(1)}) custom-call(s32[8,256]{1,0:T(8,128)S(1)} %get-tuple-element.86.plan, f32[3,128]{1,0:T(4,128)S(1)} %get-tuple-element.87.amps, bf16[33,32,128]{2,1,0:T(8,128)(2,1)S(1)} %collective-permute-done.5.refs_0_, ...), custom_call_target="tpu_custom_call" | custom-call | flops 3000000000 | bytes 8388608 | tf_op jit(solution)/shard_map/forward/pallas_call | solution.py:514
  36.3 5.4 %backward.2 = (bf16[65,32,128]{2,1,0:T(8,128)(2,1)S(1)}, bf16[65,32,128]{2,1,0:T(8,128)(2,1)S(1)}) custom-call(s32[8,256]{1,0:T(8,128)S(1)} %get-tuple-element.86.plan, f32[3,128]{1,0:T(4,128)S(1)} %get-tuple-element.87.amps, bf16[3,16,64,128]{3,2,1,0:T(8,128)(2,1)S(1)} %get-tuple-element.89.residual.refs_0_, ...), custom_call_target="tpu_custom_call" | custom-call | flops 3000000000 | bytes 8388608 | tf_op jit(solution)/shard_map/backward/pallas_call | solution.py:514
  45.0 2.8 %collective-permute-start.11 = (bf16[33,32,128]{2,1,0:T(8,128)(2,1)S(1)}, bf16[33,32,128]{2,1,0:T(8,128)(2,1)S(1)}, u32[]{:S(2)}, u32[]{:S(2)}) collective-permute-start(bf16[33,32,128]{2,1,0:T(8,128)(2,1)S(1)} %get-tuple-element.99), channel_id=1, source_target_pairs={{0,24},{1,9},{2,26},{3,11},{4,28},{5,13},{6,30},{7,15},{8,0},{9,17... | collective-permute-start | bytes 811016 | tf_op jit(solution)/shard_map/ppermute | solution.py:541
  47.8 1.9 %collective-permute-start.12 = (bf16[33,32,128]{2,1,0:T(8,128)(2,1)S(1)}, bf16[33,32,128]{2,1,0:T(8,128)(2,1)S(1)}, u32[]{:S(2)}, u32[]{:S(2)}) collective-permute-start(bf16[33,32,128]{2,1,0:T(8,128)(2,1)S(1)} %get-tuple-element.100), channel_id=1, source_target_pairs={{1,3},{2,0},{3,5},{4,2},{5,7},{6,4},{9,11},{10,8},{11,13},{12,10},... | collective-permute-start | bytes 811016 | tf_op jit(solution)/shard_map/ppermute | solution.py:541
  49.7 4.3 %home_gather.2 = (f32[128,32,128]{2,1,0:T(8,128)S(1)}, f32[6,128]{1,0:T(8,128)S(1)}) custom-call(s32[5,128]{1,0:T(8,128)S(1)} %bitcast.28, f32[6,128]{1,0:T(8,128)S(1)} %get-tuple-element.69.amps, bf16[128,32,128]{2,1,0:T(8,128)(2,1)S(1)} %bitcast.21, bf16[3,17,32,128]{3,2,1,0:T(8,128)(2,1)S(1)} %home_slots.2.back, ...), custom_call_target="tpu_custom_call" | custom-call | bytes 4194304 | tf_op jit(solution)/shard_map/home_gather/pallas_call | solution.py:514
  54.0 3.7 %collective-permute-done.11.refs_0_ = bf16[33,32,128]{2,1,0:T(8,128)(2,1)S(1)} collective-permute-done((bf16[33,32,128]{2,1,0:T(8,128)(2,1)S(1)}, bf16[33,32,128]{2,1,0:T(8,128)(2,1)S(1)}, u32[]{:S(2)}, u32[]{:S(2)}) %collective-permute-start.11) | collective-permute-done | bytes 270368 | tf_op jit(solution)/shard_map/ppermute | solution.py:541
  61.6 2.9 %update.2 = (f32[128,32,128]{2,1,0:T(8,128)S(1)}, f32[6,128]{1,0:T(8,128)S(1)}, bf16[128,32,128]{2,1,0:T(8,128)(2,1)S(1)}, f32[6,128]{1,0:T(8,128)S(1)}, bf16[33...) custom-call(s32[8,128]{1,0:T(8,128)S(1)} %get-tuple-element.66.places, f32[1,128]{1,0:T(1,128)S(1)} %bitcast.36, ...), custom_call_target="tpu_custom_call" | custom-call | bytes 3145728 | tf_op jit(solution)/shard_map/update/pallas_call | solution.py:514
  64.4 2.6 %collective-permute-start.15 = (bf16[33,32,128]{2,1,0:T(8,128)(2,1)S(1)}, bf16[33,32,128]{2,1,0:T(8,128)(2,1)S(1)}, u32[]{:S(2)}, u32[]{:S(2)}) collective-permute-start(bf16[33,32,128]{2,1,0:T(8,128)(2,1)S(1)} %get-tuple-element.107), channel_id=1, source_target_pairs={{0,8},{1,25},{2,10},{3,27},{4,12},{5,29},{6,14},{7,31},{8,16},{9,1... | collective-permute-start | bytes 811016 | tf_op jit(solution)/shard_map/ppermute | solution.py:541
  67.0 4.1 %collective-permute-start.16 = (bf16[33,32,128]{2,1,0:T(8,128)(2,1)S(1)}, bf16[33,32,128]{2,1,0:T(8,128)(2,1)S(1)}, u32[]{:S(2)}, u32[]{:S(2)}) collective-permute-start(bf16[33,32,128]{2,1,0:T(8,128)(2,1)S(1)} %get-tuple-element.108), channel_id=1, source_target_pairs={{0,2},{2,4},{3,1},{4,6},{5,3},{7,5},{8,10},{10,12},{11,9},{12,14},... | collective-permute-start | bytes 811016 | tf_op jit(solution)/shard_map/ppermute | solution.py:541
  72.9 2.0 %home_forward.3.refs_4_ = f32[3,16,64,128]{3,2,1,0:T(8,128)S(1)} custom-call(f32[3,17,32,128]{3,2,1,0:T(8,128)S(1)} %home_sums.3.sums, bf16[16,64,256]{2,1,0:T(8,128)(2,1)S(1)} %get-tuple-element.80.first_t.refs_6_, bf16[3,16,64,64]{3,2,1,0:T(8,128)(2,1)S(1)} %get-tuple-element.81.left.refs_7_), custom_call_target="tpu_custom_call" | custom-call | flops 2000000000 | bytes 4194304 | tf_op jit(solution)/shard_map/home_forward/pallas_call | solution.py:514
  75.4 3.5 %collective-permute-start.17 = (bf16[33,32,128]{2,1,0:T(8,128)(2,1)S(1)}, bf16[33,32,128]{2,1,0:T(8,128)(2,1)S(1)}, u32[]{:S(2)}, u32[]{:S(2)}) collective-permute-start(bf16[33,32,128]{2,1,0:T(8,128)(2,1)S(1)} %collective-permute-done.15.refs_0_), channel_id=1, source_target_pairs={{0,1},{1,0},{2,3},{3,2},{4,5},{5,4},{6,7},{7,6},{8,9},{9,8},{10,11... | collective-permute-start | bytes 811016 | tf_op jit(solution)/shard_map/ppermute | solution.py:545
  81.0 5.6 %forward.3 = (bf16[3,16,64,128]{3,2,1,0:T(8,128)(2,1)S(1)}, bf16[48,3,64,256]{3,2,1,0:T(8,128)(2,1)S(1)}) custom-call(s32[8,256]{1,0:T(8,128)S(1)} %get-tuple-element.111.plan, f32[3,128]{1,0:T(4,128)S(1)} %get-tuple-element.112.amps, bf16[33,32,128]{2,1,0:T(8,128)(2,1)S(1)} %collective-permute-done.15.refs_0_, ...), custom_call_target="tpu_custom_call" | custom-call | flops 3000000000 | bytes 8388608 | tf_op jit(solution)/shard_map/forward/pallas_call | solution.py:514
  86.7 5.5 %backward.3 = (bf16[65,32,128]{2,1,0:T(8,128)(2,1)S(1)}, bf16[65,32,128]{2,1,0:T(8,128)(2,1)S(1)}) custom-call(s32[8,256]{1,0:T(8,128)S(1)} %get-tuple-element.111.plan, f32[3,128]{1,0:T(4,128)S(1)} %get-tuple-element.112.amps, bf16[3,16,64,128]{3,2,1,0:T(8,128)(2,1)S(1)} %get-tuple-element.114.residual.refs_0_, ...), custom_call_target="tpu_custom_call" | custom-call | flops 3000000000 | bytes 8388608 | tf_op jit(solution)/shard_map/backward/pallas_call | solution.py:514
  95.7 1.9 %collective-permute-start.22 = (bf16[33,32,128]{2,1,0:T(8,128)(2,1)S(1)}, bf16[33,32,128]{2,1,0:T(8,128)(2,1)S(1)}, u32[]{:S(2)}, u32[]{:S(2)}) collective-permute-start(bf16[33,32,128]{2,1,0:T(8,128)(2,1)S(1)} %get-tuple-element.124), channel_id=1, source_target_pairs={{1,3},{2,0},{3,5},{4,2},{5,7},{6,4},{9,11},{10,8},{11,13},{12,10},... | collective-permute-start | bytes 811016 | tf_op jit(solution)/shard_map/ppermute | solution.py:541
  97.6 2.8 %home_gather.3 = (f32[128,16,128]{2,1,0:T(8,128)S(1)}, f32[3,128]{1,0:T(4,128)S(1)}) custom-call(s32[5,128]{1,0:T(8,128)S(1)} %bitcast.31, f32[6,128]{1,0:T(8,128)S(1)} %get-tuple-element.105.amps, bf16[128,32,128]{2,1,0:T(8,128)(2,1)S(1)} %get-tuple-element.106.morph, bf16[3,17,32,128]{3,2,1,0:T(8,128)(2,1)S(1)} %home_slots.3.back, ...), custom_call_target="tpu_custom_call" | custom-call | bytes 4194304 | tf_op jit(solution)/shard_map/home_gather/pallas_call | solution.py:514
  100.4 4.8 %collective-permute-done.21.refs_0_ = bf16[33,32,128]{2,1,0:T(8,128)(2,1)S(1)} collective-permute-done((bf16[33,32,128]{2,1,0:T(8,128)(2,1)S(1)}, bf16[33,32,128]{2,1,0:T(8,128)(2,1)S(1)}, u32[]{:S(2)}, u32[]{:S(2)}) %collective-permute-start.21) | collective-permute-done | bytes 270368 | tf_op jit(solution)/shard_map/ppermute | solution.py:541
  105.2 1.9 %collective-permute-done.22.refs_1_ = bf16[33,32,128]{2,1,0:T(8,128)(2,1)S(1)} collective-permute-done((bf16[33,32,128]{2,1,0:T(8,128)(2,1)S(1)}, bf16[33,32,128]{2,1,0:T(8,128)(2,1)S(1)}, u32[]{:S(2)}, u32[]{:S(2)}) %collective-permute-start.22) | collective-permute-done | bytes 270368 | tf_op jit(solution)/shard_map/ppermute | solution.py:541
  109.1 3.5 %update.3 = (f32[128,2048]{1,0:T(8,128)}, f32[3,128]{1,0:T(4,128)S(1)}) custom-call(s32[8,128]{1,0:T(8,128)S(1)} %get-tuple-element.66.places, f32[1,128]{1,0:T(1,128)S(1)} %bitcast.37, s32[5,128]{1,0:T(8,128)S(1)} %bitcast.32, f32[1,128]{1,0:T(1,128)S(1)} %bitcast.39, bf16[4,128,128]{2,1,0:T(8,128)(2,1)S(1)} %get-tuple-element.67.hots, ...), custom_call_target="tpu_custom_call" | custom-call | bytes 3145728 | tf_op jit(solution)/shard_map/update/pallas_call | solution.py:514
  (63 shorter events, 32.7 us)
Async XLA Ops:
  1.8 9.4 %collective-permute-start.1 = (bf16[3,4,4096]{2,1,0:T(4,128)(2,1)S(1)}, bf16[3,4,4096]{2,1,0:T(4,128)(2,1)S(1)}, u32[]{:S(2)}, u32[]{:S(2)}) collective-permute-start(bf16[3,4,4096]{2,1,0:T(4,128)(2,1)S(1)} %slice_select_fusion), channel_id=1, source_target_pairs={{0,16},{8,24},{1,17},{9,25},{2,18},{10,26},{3,19},{11,27},{4,20},{... | collective-permute-start | bytes 294920 | tf_op jit(solution)/shard_map/ppermute | solution.py:555
  6.7 3.4 %collective-permute-start = (f32[3,128]{1,0:T(4,128)S(1)}, f32[3,128]{1,0:T(4,128)S(1)}, u32[]{:S(2)}, u32[]{:S(2)}) collective-permute-start(f32[3,128]{1,0:T(4,128)S(1)} %bitcast.33), channel_id=1, source_target_pairs={{0,1},{1,0},{2,3},{3,2},{4,5},{5,4},{6,7},{7,6},{8,9},{9,8},{10,11... | collective-permute-start | bytes 4616 | tf_op jit(solution)/shard_map/ppermute | solution.py:545
  11.3 4.7 %collective-permute-start.2 = (bf16[3,4,4096]{2,1,0:T(4,128)(2,1)S(1)}, bf16[3,4,4096]{2,1,0:T(4,128)(2,1)S(1)}, u32[]{:S(2)}, u32[]{:S(2)}) collective-permute-start(bf16[3,4,4096]{2,1,0:T(4,128)(2,1)S(1)} %broadcast_select_fusion.refs_0_), channel_id=1, source_target_pairs={{0,8},{8,0},{16,24},{24,16},{1,9},{9,1},{17,25},{25,17},{2,10},{10... | collective-permute-start | bytes 294920 | tf_op jit(solution)/shard_map/ppermute | solution.py:558
  12.7 10.5 %collective-permute-start.3 = (bf16[3,4,4096]{2,1,0:T(4,128)(2,1)S(1)}, bf16[3,4,4096]{2,1,0:T(4,128)(2,1)S(1)}, u32[]{:S(2)}, u32[]{:S(2)}) collective-permute-start(bf16[3,4,4096]{2,1,0:T(4,128)(2,1)S(1)} %broadcast_select_fusion.refs_0_), channel_id=1, source_target_pairs={{0,2},{2,0},{4,6},{6,4},{1,3},{3,1},{5,7},{7,5},{8,10},{10,8},{12,... | collective-permute-start | bytes 294920 | tf_op jit(solution)/shard_map/ppermute | solution.py:561
  13.9 13.3 %collective-permute-start.5 = (bf16[33,32,128]{2,1,0:T(8,128)(2,1)S(1)}, bf16[33,32,128]{2,1,0:T(8,128)(2,1)S(1)}, u32[]{:S(2)}, u32[]{:S(2)}) collective-permute-start(bf16[33,32,128]{2,1,0:T(8,128)(2,1)S(1)} %get-tuple-element.82), channel_id=1, source_target_pairs={{0,8},{1,25},{2,10},{3,27},{4,12},{5,29},{6,14},{7,31},{8,16},{9,1... | collective-permute-start | bytes 811016 | tf_op jit(solution)/shard_map/ppermute | solution.py:541
  16.1 7.1 %collective-permute-start.4 = (bf16[3,4,4096]{2,1,0:T(4,128)(2,1)S(1)}, bf16[3,4,4096]{2,1,0:T(4,128)(2,1)S(1)}, u32[]{:S(2)}, u32[]{:S(2)}) collective-permute-start(bf16[3,4,4096]{2,1,0:T(4,128)(2,1)S(1)} %collective-permute-done.2.refs_1_), channel_id=1, source_target_pairs={{0,2},{2,0},{4,6},{6,4},{1,3},{3,1},{5,7},{7,5},{8,10},{10,8},{12,... | collective-permute-start | bytes 294920 | tf_op jit(solution)/shard_map/ppermute | solution.py:561
  17.0 10.2 %collective-permute-start.6 = (bf16[33,32,128]{2,1,0:T(8,128)(2,1)S(1)}, bf16[33,32,128]{2,1,0:T(8,128)(2,1)S(1)}, u32[]{:S(2)}, u32[]{:S(2)}) collective-permute-start(bf16[33,32,128]{2,1,0:T(8,128)(2,1)S(1)} %get-tuple-element.83), channel_id=1, source_target_pairs={{0,2},{2,4},{3,1},{4,6},{5,3},{7,5},{8,10},{10,12},{11,9},{12,14},... | collective-permute-start | bytes 811016 | tf_op jit(solution)/shard_map/ppermute | solution.py:541
  27.3 2.4 %collective-permute-start.7 = (bf16[33,32,128]{2,1,0:T(8,128)(2,1)S(1)}, bf16[33,32,128]{2,1,0:T(8,128)(2,1)S(1)}, u32[]{:S(2)}, u32[]{:S(2)}) collective-permute-start(bf16[33,32,128]{2,1,0:T(8,128)(2,1)S(1)} %collective-permute-done.5.refs_0_), channel_id=1, source_target_pairs={{0,1},{1,0},{2,3},{3,2},{4,5},{5,4},{6,7},{7,6},{8,9},{9,8},{10,11... | collective-permute-start | bytes 811016 | tf_op jit(solution)/shard_map/ppermute | solution.py:545
  28.5 1.6 %collective-permute-start.8 = (bf16[33,32,128]{2,1,0:T(8,128)(2,1)S(1)}, bf16[33,32,128]{2,1,0:T(8,128)(2,1)S(1)}, u32[]{:S(2)}, u32[]{:S(2)}) collective-permute-start(bf16[33,32,128]{2,1,0:T(8,128)(2,1)S(1)} %collective-permute-done.6.refs_1_), channel_id=1, source_target_pairs={{0,1},{1,0},{2,3},{3,2},{4,5},{5,4},{6,7},{7,6},{8,9},{9,8},{10,11... | collective-permute-start | bytes 811016 | tf_op jit(solution)/shard_map/ppermute | solution.py:545
  41.7 3.2 %collective-permute-start.9 = (bf16[65,32,128]{2,1,0:T(8,128)(2,1)S(1)}, bf16[65,32,128]{2,1,0:T(8,128)(2,1)S(1)}, u32[]{:S(2)}, u32[]{:S(2)}) collective-permute-start(bf16[65,32,128]{2,1,0:T(8,128)(2,1)S(1)} %get-tuple-element.93), channel_id=1, source_target_pairs={{0,1},{1,0},{2,3},{3,2},{4,5},{5,4},{6,7},{7,6},{8,9},{9,8},{10,11... | collective-permute-start | bytes 1597448 | tf_op jit(solution)/shard_map/ppermute | solution.py:545
  43.0 1.8 %collective-permute-start.10 = (bf16[3,17,32,128]{3,2,1,0:T(8,128)(2,1)S(1)}, bf16[3,17,32,128]{3,2,1,0:T(8,128)(2,1)S(1)}, u32[]{:S(2)}, u32[]{:S(2)}) collective-permute-start(bf16[3,17,32,128]{3,2,1,0:T(8,128)(2,1)S(1)} %home_slots.2.back), channel_id=1, source_target_pairs={{0,1},{1,0},{2,3},{3,2},{4,5},{5,4},{6,7},{7,6},{8,9},{9,8},{10,11... | collective-permute-start | bytes 1253384 | tf_op jit(solution)/shard_map/ppermute | solution.py:545
  45.0 12.7 %collective-permute-start.11 = (bf16[33,32,128]{2,1,0:T(8,128)(2,1)S(1)}, bf16[33,32,128]{2,1,0:T(8,128)(2,1)S(1)}, u32[]{:S(2)}, u32[]{:S(2)}) collective-permute-start(bf16[33,32,128]{2,1,0:T(8,128)(2,1)S(1)} %get-tuple-element.99), channel_id=1, source_target_pairs={{0,24},{1,9},{2,26},{3,11},{4,28},{5,13},{6,30},{7,15},{8,0},{9,17... | collective-permute-start | bytes 811016 | tf_op jit(solution)/shard_map/ppermute | solution.py:541
  47.8 10.8 %collective-permute-start.12 = (bf16[33,32,128]{2,1,0:T(8,128)(2,1)S(1)}, bf16[33,32,128]{2,1,0:T(8,128)(2,1)S(1)}, u32[]{:S(2)}, u32[]{:S(2)}) collective-permute-start(bf16[33,32,128]{2,1,0:T(8,128)(2,1)S(1)} %get-tuple-element.100), channel_id=1, source_target_pairs={{1,3},{2,0},{3,5},{4,2},{5,7},{6,4},{9,11},{10,8},{11,13},{12,10},... | collective-permute-start | bytes 811016 | tf_op jit(solution)/shard_map/ppermute | solution.py:541
  58.5 2.7 %collective-permute-start.13 = (bf16[33,32,128]{2,1,0:T(8,128)(2,1)S(1)}, bf16[33,32,128]{2,1,0:T(8,128)(2,1)S(1)}, u32[]{:S(2)}, u32[]{:S(2)}) collective-permute-start(bf16[33,32,128]{2,1,0:T(8,128)(2,1)S(1)} %collective-permute-done.11.refs_0_), channel_id=1, source_target_pairs={{0,1},{1,0},{2,3},{3,2},{4,5},{5,4},{6,7},{7,6},{8,9},{9,8},{10,11... | collective-permute-start | bytes 811016 | tf_op jit(solution)/shard_map/ppermute | solution.py:545
  64.4 10.5 %collective-permute-start.15 = (bf16[33,32,128]{2,1,0:T(8,128)(2,1)S(1)}, bf16[33,32,128]{2,1,0:T(8,128)(2,1)S(1)}, u32[]{:S(2)}, u32[]{:S(2)}) collective-permute-start(bf16[33,32,128]{2,1,0:T(8,128)(2,1)S(1)} %get-tuple-element.107), channel_id=1, source_target_pairs={{0,8},{1,25},{2,10},{3,27},{4,12},{5,29},{6,14},{7,31},{8,16},{9,1... | collective-permute-start | bytes 811016 | tf_op jit(solution)/shard_map/ppermute | solution.py:541
  67.0 8.4 %collective-permute-start.16 = (bf16[33,32,128]{2,1,0:T(8,128)(2,1)S(1)}, bf16[33,32,128]{2,1,0:T(8,128)(2,1)S(1)}, u32[]{:S(2)}, u32[]{:S(2)}) collective-permute-start(bf16[33,32,128]{2,1,0:T(8,128)(2,1)S(1)} %get-tuple-element.108), channel_id=1, source_target_pairs={{0,2},{2,4},{3,1},{4,6},{5,3},{7,5},{8,10},{10,12},{11,9},{12,14},... | collective-permute-start | bytes 811016 | tf_op jit(solution)/shard_map/ppermute | solution.py:541
  75.4 4.6 %collective-permute-start.17 = (bf16[33,32,128]{2,1,0:T(8,128)(2,1)S(1)}, bf16[33,32,128]{2,1,0:T(8,128)(2,1)S(1)}, u32[]{:S(2)}, u32[]{:S(2)}) collective-permute-start(bf16[33,32,128]{2,1,0:T(8,128)(2,1)S(1)} %collective-permute-done.15.refs_0_), channel_id=1, source_target_pairs={{0,1},{1,0},{2,3},{3,2},{4,5},{5,4},{6,7},{7,6},{8,9},{9,8},{10,11... | collective-permute-start | bytes 811016 | tf_op jit(solution)/shard_map/ppermute | solution.py:545
  78.9 1.6 %collective-permute-start.18 = (bf16[33,32,128]{2,1,0:T(8,128)(2,1)S(1)}, bf16[33,32,128]{2,1,0:T(8,128)(2,1)S(1)}, u32[]{:S(2)}, u32[]{:S(2)}) collective-permute-start(bf16[33,32,128]{2,1,0:T(8,128)(2,1)S(1)} %collective-permute-done.16.refs_1_), channel_id=1, source_target_pairs={{0,1},{1,0},{2,3},{3,2},{4,5},{5,4},{6,7},{7,6},{8,9},{9,8},{10,11... | collective-permute-start | bytes 811016 | tf_op jit(solution)/shard_map/ppermute | solution.py:545
  92.1 3.2 %collective-permute-start.19 = (bf16[65,32,128]{2,1,0:T(8,128)(2,1)S(1)}, bf16[65,32,128]{2,1,0:T(8,128)(2,1)S(1)}, u32[]{:S(2)}, u32[]{:S(2)}) collective-permute-start(bf16[65,32,128]{2,1,0:T(8,128)(2,1)S(1)} %get-tuple-element.116), channel_id=1, source_target_pairs={{0,1},{1,0},{2,3},{3,2},{4,5},{5,4},{6,7},{7,6},{8,9},{9,8},{10,11... | collective-permute-start | bytes 1597448 | tf_op jit(solution)/shard_map/ppermute | solution.py:545
  93.5 1.8 %collective-permute-start.20 = (bf16[3,17,32,128]{3,2,1,0:T(8,128)(2,1)S(1)}, bf16[3,17,32,128]{3,2,1,0:T(8,128)(2,1)S(1)}, u32[]{:S(2)}, u32[]{:S(2)}) collective-permute-start(bf16[3,17,32,128]{3,2,1,0:T(8,128)(2,1)S(1)} %home_slots.3.back), channel_id=1, source_target_pairs={{0,1},{1,0},{2,3},{3,2},{4,5},{5,4},{6,7},{7,6},{8,9},{9,8},{10,11... | collective-permute-start | bytes 1253384 | tf_op jit(solution)/shard_map/ppermute | solution.py:545
  95.4 9.8 %collective-permute-start.21 = (bf16[33,32,128]{2,1,0:T(8,128)(2,1)S(1)}, bf16[33,32,128]{2,1,0:T(8,128)(2,1)S(1)}, u32[]{:S(2)}, u32[]{:S(2)}) collective-permute-start(bf16[33,32,128]{2,1,0:T(8,128)(2,1)S(1)} %get-tuple-element.123), channel_id=1, source_target_pairs={{0,24},{1,9},{2,26},{3,11},{4,28},{5,13},{6,30},{7,15},{8,0},{9,17... | collective-permute-start | bytes 811016 | tf_op jit(solution)/shard_map/ppermute | solution.py:541
  95.7 11.4 %collective-permute-start.22 = (bf16[33,32,128]{2,1,0:T(8,128)(2,1)S(1)}, bf16[33,32,128]{2,1,0:T(8,128)(2,1)S(1)}, u32[]{:S(2)}, u32[]{:S(2)}) collective-permute-start(bf16[33,32,128]{2,1,0:T(8,128)(2,1)S(1)} %get-tuple-element.124), channel_id=1, source_target_pairs={{1,3},{2,0},{3,5},{4,2},{5,7},{6,4},{9,11},{10,8},{11,13},{12,10},... | collective-permute-start | bytes 811016 | tf_op jit(solution)/shard_map/ppermute | solution.py:541
  107.1 1.6 %collective-permute-start.23 = (bf16[33,32,128]{2,1,0:T(8,128)(2,1)S(1)}, bf16[33,32,128]{2,1,0:T(8,128)(2,1)S(1)}, u32[]{:S(2)}, u32[]{:S(2)}) collective-permute-start(bf16[33,32,128]{2,1,0:T(8,128)(2,1)S(1)} %collective-permute-done.21.refs_0_), channel_id=1, source_target_pairs={{0,1},{1,0},{2,3},{3,2},{4,5},{5,4},{6,7},{7,6},{8,9},{9,8},{10,11... | collective-permute-start | bytes 811016 | tf_op jit(solution)/shard_map/ppermute | solution.py:545
  107.5 1.6 %collective-permute-start.24 = (bf16[33,32,128]{2,1,0:T(8,128)(2,1)S(1)}, bf16[33,32,128]{2,1,0:T(8,128)(2,1)S(1)}, u32[]{:S(2)}, u32[]{:S(2)}) collective-permute-start(bf16[33,32,128]{2,1,0:T(8,128)(2,1)S(1)} %collective-permute-done.22.refs_1_), channel_id=1, source_target_pairs={{0,1},{1,0},{2,3},{3,2},{4,5},{5,4},{6,7},{7,6},{8,9},{9,8},{10,11... | collective-permute-start | bytes 811016 | tf_op jit(solution)/shard_map/ppermute | solution.py:545
  (5 other events, 52.6 us)
where the time goes:
time: 115 us; the launch traced here: 113 us
  Pallas kernels  51.8 us (45%)
  starting transfers between devices  34.7 us (30%)
  waiting for transfers between devices  21 us (18%)
  local copies, waits for them, and re-layouts  3.51 us (3%)
  other arithmetic  1.24 us (1%)
    pallas_call x22, Pallas kernels, call(): pl.pallas_call(body, out_shape=[jax.ShapeDtypeStruct(shape, dtype) for sh...  51.8 us
    ppermute x8, starting transfers between devices, stepped(): return lax.ppermute(value, ('ra', 'dec', 'band'), pairs)  18.1 us
    ppermute x8, waiting for transfers between devices, stepped(): return lax.ppermute(value, ('ra', 'dec', 'band'), pairs)  11.8 us
    ppermute x13, waiting for transfers between devices, swapped(): return lax.ppermute(value, 'band', [(0, 1), (1, 0)])  9.22 us
    ppermute x13, starting transfers between devices, swapped(): return lax.ppermute(value, 'band', [(0, 1), (1, 0)])  8.9 us
    ppermute x1, starting transfers between devices, all_tables(): far = lax.ppermute(mine, 'ra', [(0, 2), (1, 3)])  4.22 us
    unnamed x13, local copies, waits for them, and re-layouts  3.51 us
  transfers between devices with their start and end apart: 25, of which 15 were waited for; matrix products, arithmetic and copies ran while one was open for 3% of the time, Pallas kernels for 19%

commit v1 on v0

--- a/solution.py
+++ b/solution.py
@@ -64,13 +64,17 @@
     return pl.multiple_of(lax.axis_index("band") * HALF, HALF)
 
 
+def rows_of(ref):
+    return jnp.concatenate([ref[i] for i in range(ref.shape[0])], axis=0)
+
+
 def by_core(mine, theirs):
     first = lax.axis_index("band") == 0
     return jnp.where(first, mine, theirs), jnp.where(first, theirs, mine)
 
 
 def lists_kernel(num_slots, slots_ref, hots, places):
-    slots = slots_ref[...]
+    slots = rows_of(slots_ref)
     sources = slots.shape[1]
     valid = (slots < num_slots).astype(F32)
     upper = (iota((sources, sources), 0) <= iota((sources, sources), 1)).astype(F32)
@@ -108,8 +112,8 @@
 
 def pack_kernel(places, slots_ref, amps_mine, amps_theirs, hots, morph, *out):
     messages, amps_out, amps_q = out[:2], out[2], out[3]
-    amps = jnp.concatenate(by_core(amps_mine[...], amps_theirs[...]), axis=0)
-    write_messages(messages, slots_ref[...], amps, hots, places, morph)
+    amps = jnp.concatenate(by_core(rows_of(amps_mine), rows_of(amps_theirs)), axis=0)
+    write_messages(messages, rows_of(slots_ref), amps, hots, places, morph)
     amps_out[...] = amps
     amps_q[...] = amps.astype(BF16).astype(F32)
 
@@ -207,13 +211,13 @@
 def make_tables(shards, bands, earlier=()):
     count = sum(x.shape[1] for x in shards)
     total = count + sum(x.shape[0] for x in earlier[:1])
-    square = ((bands, total, SIDE, SIDE), BF16, False)
+    square = ((bands, total, SIDE, SIDE), BF16)
     return call(
         functools.partial(tables_kernel, bands, bool(earlier)),
         "tables",
         (*shards, *earlier),
         0,
-        [((total, SIDE, WIDE), BF16, False), square, square, ((total, WIDE, LANES), BF16, False)],
+        [((total, SIDE, WIDE), BF16), square, square, ((total, WIDE, LANES), BF16)],
         [((bands, count * ROWS, LANES), F32)],
         flops=2 * 10**9,
         moved=5 * 2**20,
@@ -225,13 +229,13 @@
     sums[...] = jnp.zeros_like(sums)
 
     def add(s, carry):
-        q = lists[0, s]
+        q = lists[0, 0, s]
         stamp = morph[s].astype(F32)
         for band in range(bands):
             sums[band, q] += amps[first + band, s] * stamp
         return carry
 
-    lax.fori_loop(0, lists.shape[1], add, 0, unroll=4)
+    lax.fori_loop(0, lists.shape[2], add, 0, unroll=4)
 
 
 def home_forward_kernel(bands, sums, first_t, left, total, inner_all):
@@ -336,6 +340,8 @@
     residual, inner_all, left_t, right, keep, send, stacks, sums = refs
     none = NEAR * CAP
     sums[...] = jnp.zeros_like(sums)
+    keep[...] = jnp.zeros_like(keep)
+    send[...] = jnp.zeros_like(send)
     masks, row_masks, packed_low = half_masks(SIDE), half_masks(1), half_masks(ROWS)[0]
     read, rounds = chunk_reader(bands, plan, amps)
     spare = none // 2
@@ -414,7 +420,7 @@
     mine = pl.ds(half_rows(), HALF) if last else pl.ds(0, ROWS)
 
     def gather(s, carry):
-        q = lists[0, s]
+        q = lists[0, 0, s]
         stamp = morph[s].astype(F32)
         grad = jnp.zeros((HALF if last else ROWS, LANES), F32)
         for ref, side in ((back, core), (received, 1 - core)):
@@ -432,7 +438,7 @@
         keep[s] = grad
         return carry
 
-    lax.fori_loop(0, lists.shape[1], gather, 0, unroll=4)
+    lax.fori_loop(0, lists.shape[2], gather, 0, unroll=4)
     for band in range(grad_a.shape[0]):
         rows = sums[core * bands + band] if last else sums[band]
         grad_a[band : band + 1, :] = lane_sums(rows)[:1]
@@ -460,32 +466,10 @@
 def update_kernel(first, last, places, eta_m, slots_ref, eta_a, hots, amps_ref, grad_a, morph, home, *refs):
     grads, out = refs[:NEAR], refs[NEAR:]
     state, amps_out, work = out[0], out[1], out[-1]
-    sources = slots_ref.shape[1]
+    sources = slots_ref.shape[2]
     core = lax.axis_index("band")
     mine = pl.ds(half_rows(), HALF) if last else pl.ds(0, ROWS)
     nears = (core, 2 + core, 1 - core, 3 - core)
-    work[...] = home[...]
-    for ref, near in zip(grads, nears):
-
-        def add(n, carry, ref=ref, near=near):
-            work[places[near, n]] += ref[n, mine, :].astype(F32)
-            return carry
-
-        lax.fori_loop(0, places[NEAR + near, 0], add, 0)
-
-    def step(s, carry):
-        new = jnp.maximum(morph[s, mine, :].astype(F32) - eta_m[0, s] * work[s], 0.0)
-        if last:
-            work[s] = new
-        else:
-            state[s] = new
-            out[2][s] = new.astype(BF16)
-        return carry
-
-    lax.fori_loop(0, sources, step, 0, unroll=8)
-    if last:
-        for r in range(HALF):
-            state[:, r * LANES : (r + 1) * LANES] = work[:, r, :]
     lane = iota((ROWS, LANES), 1) // CAP
     meta = jnp.zeros((ROWS, LANES), F32)
     for ref, near in zip(grads, nears):
@@ -501,23 +485,47 @@
         amps = amps_ref[...]
         total = grad_a[...] + jnp.concatenate(sides, axis=0)
     amps = jnp.maximum(amps - eta_a[...] * total, 0.0)
-    amps_out[...] = amps
     if last:
+        for band in range(bands):
+            amps_out[band] = amps[band : band + 1]
+    else:
+        amps_out[...] = amps
+    work[...] = home[...]
+    for ref, near in zip(grads, nears):
+
+        def add(n, carry, ref=ref, near=near):
+            work[places[near, n]] += ref[n, mine, :].astype(F32)
+            return carry
+
+        lax.fori_loop(0, CAP, add, 0, unroll=8)
+
+    def step(s, carry):
+        new = jnp.maximum(morph[s, mine, :].astype(F32) - eta_m[0, s] * work[s], 0.0)
+        if last:
+            work[s] = new
+        else:
+            state[s] = new
+            out[2][s] = new.astype(BF16)
+        return carry
+
+    lax.fori_loop(0, sources, step, 0, unroll=8)
+    if last:
+        for r in range(HALF):
+            state[:, r * LANES : (r + 1) * LANES] = work[:, r, :]
         return
     stamps, amps_q, messages = out[2], out[3], out[4:6]
     amps_q[...] = amps.astype(BF16).astype(F32)
-    write_messages(messages, slots_ref[...], amps, hots, places, stamps)
-
-
-def call(body, name, operands, scalars, outs, scratch=(), smem_scratch=(), flops=0, moved=0):
+    write_messages(messages, rows_of(slots_ref), amps, hots, places, stamps)
+
+
+def call(body, name, operands, scalars, outs, scratch=(), flops=0, moved=0):
     vmem, smem = pl.BlockSpec(memory_space=pltpu.VMEM), pl.BlockSpec(memory_space=pltpu.SMEM)
     return pl.pallas_call(
         body,
-        out_shape=[jax.ShapeDtypeStruct(shape, dtype) for shape, dtype, _ in outs],
+        out_shape=[jax.ShapeDtypeStruct(shape, dtype) for shape, dtype in outs],
         in_specs=[smem if i < scalars else vmem for i in range(len(operands))],
-        out_specs=[smem if flag else vmem for _, _, flag in outs],
-        scratch_shapes=[pltpu.VMEM(shape, dtype) for shape, dtype in scratch]
-        + [pltpu.SMEM(shape, dtype) for shape, dtype in smem_scratch],
+        out_specs=[vmem] * len(outs),
+        scratch_shapes=[pltpu.VMEM(shape, dtype) for shape, dtype in scratch],
         compiler_params=pltpu.CompilerParams(vmem_limit_bytes=40 * 2**20),
         cost_estimate=pl.CostEstimate(flops=flops, bytes_accessed=moved, transcendentals=0),
         name=name,
@@ -545,7 +553,7 @@
     return lax.ppermute(value, "band", [(0, 1), (1, 0)])
 
 
-def all_tables(psf, num_slots, messages, morph):
+def all_tables(psf, num_slots, messages, sums):
     bands, held = psf.shape[:2]
     lines = lax.axis_size("dec")
     if lax.axis_size("ra") == 4 and 2 * held == num_slots and held % 2 == 0 and lines % 2 == 0:
@@ -554,22 +562,23 @@
         mine = jnp.where(lax.axis_index("dec") % 2 == 0, psf[:, : held // 2], psf[:, held // 2 :])
         far = lax.ppermute(mine, "ra", [(0, 2), (1, 3)])
         here = jnp.where(lax.axis_index("ra") < 2, mine, far)
-        here, *messages = lax.optimization_barrier((here, *messages))
+        here, messages[0] = lax.optimization_barrier((here, messages[0]))
         near = lax.ppermute(here, "ra", along)
-        near, morph, messages[1] = lax.optimization_barrier((near, morph, messages[1]))
+        near, sums = lax.optimization_barrier((near, sums))
         halves = make_tables((here, near), bands)
         others = (lax.ppermute(here, "dec", across), lax.ppermute(near, "dec", across))
-        return make_tables(others, bands, halves), messages, morph
-    return make_tables((lax.all_gather(psf, "ra", axis=1, tiled=True)[:, :num_slots],), bands), messages, morph
+        messages[1], *halves = lax.optimization_barrier((messages[1], *halves))
+        return make_tables(others, bands, halves), messages, sums
+    return make_tables((lax.all_gather(psf, "ra", axis=1, tiled=True)[:, :num_slots],), bands), messages, sums
 
 
 def shards(morphology, sed_amps, slot_lists, morph_step, sed_step, psf_kernels, observed):
     bands, num_slots, sources = sed_amps.shape[2], observed.shape[3], morphology.shape[2]
-    lists, amps = slot_lists[0, 0], sed_amps[0, 0]
+    lists, amps = slot_lists[0, 0][:, None, :], sed_amps[0, 0][:, None, :]
     eta_m, eta_a = morph_step[0], sed_step[0]
     full = morphology[0, 0].reshape(sources, ROWS, LANES)
     seen = observed[0, 0].reshape(bands, num_slots, ROWS, LANES)
-    stamp = ((CAP + 1, ROWS, LANES), BF16, False)
+    stamp = ((CAP + 1, ROWS, LANES), BF16)
     all_stamps = (sources, ROWS, LANES)
     near_all = NEAR * CAP
     chunks = -(-(near_all // GROUP + num_slots) // STRIDE) * STRIDE
@@ -580,8 +589,8 @@
         (lists,),
         0,
         [
-            ((NEAR, LANES, sources), BF16, False),
-            ((2 * NEAR, LANES), jnp.int32, False),
+            ((NEAR, LANES, sources), BF16),
+            ((2 * NEAR, LANES), jnp.int32),
         ],
         moved=2**20,
     )
@@ -590,33 +599,42 @@
         "pack",
         (places, lists, amps, amps_theirs, hots, full),
         1,
-        [stamp] * 2 + [((2 * bands, sources), F32, False)] * 2,
+        [stamp] * 2 + [((2 * bands, sources), F32)] * 2,
         moved=2**20,
     )
-    (first_t, left, left_t, right), messages, morph = all_tables(psf_kernels, num_slots, messages, full)
-    state = full
-    for sweep in range(ITERS):
-        last = sweep == ITERS - 1
-        own = [stepped(messages[0], "ra", 1), stepped(messages[1], "dec", 1)]
-        sums = call(
+    def home_sums(amps_q, morph):
+        return call(
             functools.partial(home_sums_kernel, bands),
             "home_sums",
             (lists, amps_q, morph),
             2,
-            [((bands, num_slots + 1, ROWS, LANES), F32, False)],
+            [((bands, num_slots + 1, ROWS, LANES), F32)],
             moved=4 * 2**20,
         )[0]
+
+    sums = home_sums(amps_q, full)
+    tables, messages, sums = all_tables(psf_kernels, num_slots, messages, sums)
+    first_t, left, left_t, right = tables
+    morph = state = full
+    for sweep in range(ITERS):
+        last = sweep == ITERS - 1
+        own = [stepped(messages[0], "ra", 1), stepped(messages[1], "dec", 1)]
+        if sweep == 0:
+            left, *own = lax.optimization_barrier((left, *own))
+        else:
+            sums = home_sums(amps_q, morph)
         home = call(
             functools.partial(home_forward_kernel, bands),
             "home_forward",
             (sums, first_t, left),
             0,
-            [((bands, num_slots, SIDE, LANES), F32, False)],
+            [((bands, num_slots, SIDE, LANES), F32)],
             [((bands, num_slots, SIDE, LANES), BF16)],
             flops=2 * 10**9,
             moved=4 * 2**20,
         )[0]
-        home, *own = lax.optimization_barrier((home, *own))
+        if sweep > 0:
+            own = [lax.optimization_barrier((home, x))[1] for x in own]
         other = [swapped(x) for x in own]
         order = call(
             functools.partial(order_kernel, num_slots),
@@ -624,8 +642,8 @@
             (*own, *other),
             0,
             [
-                ((8, -(-chunks * GROUP // LANES) * LANES), jnp.int32, False),
-                ((bands, LANES), F32, False),
+                ((8, -(-chunks * GROUP // LANES) * LANES), jnp.int32),
+                ((bands, LANES), F32),
             ],
             moved=2**20,
         )
@@ -635,14 +653,14 @@
             (*order, *own, *other, home, seen, first_t, left),
             2,
             [
-                ((bands, num_slots, SIDE, LANES), BF16, False),
-                ((chunks, bands, SIDE, WIDE), BF16, False),
+                ((bands, num_slots, SIDE, LANES), BF16),
+                ((chunks, bands, SIDE, WIDE), BF16),
             ],
             [((near_all + 1, SIDE, LANES), BF16)] + [((num_slots, SIDE, LANES), F32)] * (2 * bands),
             flops=3 * 10**9,
             moved=8 * 2**20,
         )
-        half_of_near = ((near_all // 2 + 1, ROWS, LANES), BF16, False)
+        half_of_near = ((near_all // 2 + 1, ROWS, LANES), BF16)
         keep, send = call(
             functools.partial(backward_kernel, bands),
             "backward",
@@ -659,14 +677,14 @@
             "home_slots",
             (residual, left_t, right),
             0,
-            [((bands, num_slots + 1, ROWS, LANES), BF16, False)],
+            [((bands, num_slots + 1, ROWS, LANES), BF16)],
             flops=2 * 10**9,
             moved=4 * 2**20,
         )[0]
-        back_received = swapped(back)
-        received, back_received = lax.optimization_barrier((received, back_received))
+        received, back = lax.optimization_barrier((received, back))
         grads = call(reduce_kernel, "reduce", (keep, received), 0, [stamp] * 2, moved=2 * 2**20)
         grads = [stepped(grads[0], "ra", -1), stepped(grads[1], "dec", -1)]
+        back_received = swapped(back)
         bands_here = bands if last else 2 * bands
         part = (sources, HALF, LANES) if last else all_stamps
         home_grad, grad_a = call(
@@ -674,15 +692,16 @@
             "home_gather",
             (lists, amps_q, morph, back, back_received),
             2,
-            [(part, F32, False), ((bands_here, sources), F32, False)],
+            [(part, F32), ((bands_here, sources), F32)],
             [((2 * bands, sources, LANES), F32)],
             moved=4 * 2**20,
         )
-        home_grad, *grads = lax.optimization_barrier((home_grad, *grads))
+        grads = [lax.optimization_barrier((home_grad, x))[1] for x in grads]
         grads += [swapped(x) for x in grads]
-        outs = [((sources, HALF * LANES) if last else all_stamps, F32, False), ((bands_here, sources), F32, False)]
+        outs = [((sources, HALF * LANES) if last else all_stamps, F32)]
+        outs += [((bands, 1, sources) if last else (2 * bands, sources), F32)]
         if not last:
-            outs += [(all_stamps, BF16, False), ((bands_here, sources), F32, False)] + [stamp] * 2
+            outs += [(all_stamps, BF16), ((bands_here, sources), F32)] + [stamp] * 2
         state, amps, *more = call(
             functools.partial(update_kernel, sweep == 0, last),
             "update",
@@ -694,7 +713,7 @@
         )
         if not last:
             morph, amps_q, *messages = more
-    return state[None, None], amps[None, None]
+    return state[None, None], amps.reshape(1, 1, bands, sources)
 
 
 def solution(mesh):

time: 115 us -> 115 us (level)
  Pallas kernels: 51.8 us -> 56.7 us
  starting transfers between devices: 34.7 us -> 30.6 us
  local copies, waits for them, and re-layouts: 3.51 us -> 2.27 us
    pallas_call x22, Pallas kernels: 51.8 us -> 56.7 us  [call(): pl.pallas_call(body, out_shape=[jax.ShapeDtypeStruct(shape, dtype) for sh...]
    ppermute x8, waiting for transfers between devices: 11.8 us -> 15.4 us  [stepped(): return lax.ppermute(value, ('ra', 'dec', 'band'), pairs)]
    ppermute x8, starting transfers between devices: 18.1 us -> 14.6 us  [stepped(): return lax.ppermute(value, ('ra', 'dec', 'band'), pairs)]
    ppermute x13, waiting for transfers between devices: 9.22 us -> 5.8 us  [swapped(): return lax.ppermute(value, 'band', [(0, 1), (1, 0)])]
    unnamed x13 -> x16, local copies, waits for them, and re-layouts: 3.51 us -> 2.27 us
  transfers between devices with their start and end apart: 25 -> 25, of which waited for: 15 -> 15; matrix products, arithmetic and copies ran while one was open for 3% -> 1% of each run, Pallas kernels for 19% -> 19%
where the time goes in v1:
time: 115 us; the launch traced here: 113 us
  Pallas kernels  56.7 us (49%)
  starting transfers between devices  30.6 us (27%)
  waiting for transfers between devices  21.2 us (18%)
  local copies, waits for them, and re-layouts  2.27 us (2%)
  other arithmetic  1.24 us (1%)
    pallas_call x22, Pallas kernels, call(): pl.pallas_call(body, out_shape=[jax.ShapeDtypeStruct(shape, dtype) for sh...  56.7 us
    ppermute x8, waiting for transfers between devices, stepped(): return lax.ppermute(value, ('ra', 'dec', 'band'), pairs)  15.4 us
    ppermute x8, starting transfers between devices, stepped(): return lax.ppermute(value, ('ra', 'dec', 'band'), pairs)  14.6 us
    ppermute x13, starting transfers between devices, swapped(): return lax.ppermute(value, 'band', [(0, 1), (1, 0)])  8.89 us
    ppermute x13, waiting for transfers between devices, swapped(): return lax.ppermute(value, 'band', [(0, 1), (1, 0)])  5.8 us
    ppermute x1, starting transfers between devices, all_tables(): far = lax.ppermute(mine, 'ra', [(0, 2), (1, 3)])  4.22 us
  transfers between devices with their start and end apart: 25, of which 15 were waited for; matrix products, arithmetic and copies ran while one was open for 1% of the time, Pallas kernels for 19%

profile of v1, /device:TPU:5, one launch (start us, length us, event | category | flops | bytes accessed | tf_op | source)
XLA Modules:
  0.0 112.9 jit_solution(13405163703549377659)
XLA Ops:
  1.8 4.2 %collective-permute-start.1 = (bf16[3,4,4096]{2,1,0:T(4,128)(2,1)S(1)}, bf16[3,4,4096]{2,1,0:T(4,128)(2,1)S(1)}, u32[]{:S(2)}, u32[]{:S(2)}) collective-permute-start(bf16[3,4,4096]{2,1,0:T(4,128)(2,1)S(1)} %slice_select_fusion), channel_id=1, source_target_pairs={{0,16},{8,24},{1,17},{9,25},{2,18},{10,26},{3,19},{11,27},{4,20},{... | collective-permute-start | bytes 294920 | tf_op jit(solution)/shard_map/ppermute | solution.py:563
  15.2 2.7 %collective-permute-start.5 = (bf16[33,32,128]{2,1,0:T(8,128)(2,1)S(1)}, bf16[33,32,128]{2,1,0:T(8,128)(2,1)S(1)}, u32[]{:S(2)}, u32[]{:S(2)}) collective-permute-start(bf16[33,32,128]{2,1,0:T(8,128)(2,1)S(1)} %get-tuple-element.83), channel_id=1, source_target_pairs={{0,8},{1,25},{2,10},{3,27},{4,12},{5,29},{6,14},{7,31},{8,16},{9,1... | collective-permute-start | bytes 811016 | tf_op jit(solution)/shard_map/ppermute | solution.py:549
  18.2 2.0 %tables.2 = (bf16[8,64,256]{2,1,0:T(8,128)(2,1)S(1)}, bf16[3,8,64,64]{3,2,1,0:T(8,128)(2,1)S(1)}, bf16[3,8,64,64]{3,2,1,0:T(8,128)(2,1)S(1)}, bf16[8,256,128]{2,1,0:T(8,128)(2,1)S(1)}) custom-call(bf16[3,4,4096]{2,1,0:T(4,128)(2,1)S(1)} %broadcast_select_fusion.refs_0_, bf16[3,4,4096]{2,1,0:T(4,128)(2,1)S(1)} %collective-permute-done.3.refs_1_), custom_call_target="tpu_custom_call" | custom-call | flops 2000000000 | bytes 5242880 | tf_op jit(solution)/shard_map/tables/pallas_call | solution.py:523
  20.2 3.2 %collective-permute-start.6 = (bf16[33,32,128]{2,1,0:T(8,128)(2,1)S(1)}, bf16[33,32,128]{2,1,0:T(8,128)(2,1)S(1)}, u32[]{:S(2)}, u32[]{:S(2)}) collective-permute-start(bf16[33,32,128]{2,1,0:T(8,128)(2,1)S(1)} %get-tuple-element.84), channel_id=1, source_target_pairs={{0,2},{2,4},{3,1},{4,6},{5,3},{7,5},{8,10},{10,12},{11,9},{12,14},... | collective-permute-start | bytes 811016 | tf_op jit(solution)/shard_map/ppermute | solution.py:549
  23.4 2.0 %tables.3 = (bf16[16,64,256]{2,1,0:T(8,128)(2,1)S(1)}, bf16[3,16,64,64]{3,2,1,0:T(8,128)(2,1)S(1)}, bf16[3,16,64,64]{3,2,1,0:T(8,128)(2,1)S(1)}, bf16[16,256,128]{2,1,0:T(8,128)(2,1)S(1)}) custom-call(bf16[3,4,4096]{2,1,0:T(4,128)(2,1)S(1)} %collective-permute-done.2.refs_0_, bf16[3,4,4096]{2,1,0:T(4,128)(2,1)S(1)} %collective-permute-done.4.refs_1_, ...), custom_call_target="tpu_custom_call" | custom-call | flops 2000000000 | bytes 5242880 | tf_op jit(solution)/shard_map/tables/pallas_call | solution.py:523
  25.4 3.4 %collective-permute-done.6.refs_1_ = bf16[33,32,128]{2,1,0:T(8,128)(2,1)S(1)} collective-permute-done((bf16[33,32,128]{2,1,0:T(8,128)(2,1)S(1)}, bf16[33,32,128]{2,1,0:T(8,128)(2,1)S(1)}, u32[]{:S(2)}, u32[]{:S(2)}) %collective-permute-start.6) | collective-permute-done | bytes 270368 | tf_op jit(solution)/shard_map/ppermute | solution.py:549
  28.7 2.3 %collective-permute-start.7 = (bf16[33,32,128]{2,1,0:T(8,128)(2,1)S(1)}, bf16[33,32,128]{2,1,0:T(8,128)(2,1)S(1)}, u32[]{:S(2)}, u32[]{:S(2)}) collective-permute-start(bf16[33,32,128]{2,1,0:T(8,128)(2,1)S(1)} %collective-permute-done.5.refs_0_), channel_id=1, source_target_pairs={{0,1},{1,0},{2,3},{3,2},{4,5},{5,4},{6,7},{7,6},{8,9},{9,8},{10,11... | collective-permute-start | bytes 811016 | tf_op jit(solution)/shard_map/ppermute | solution.py:553
  31.1 2.0 %home_forward.2.refs_4_ = f32[3,16,64,128]{3,2,1,0:T(8,128)S(1)} custom-call(f32[3,17,32,128]{3,2,1,0:T(8,128)S(1)} %home_sums.2.sums, bf16[16,64,256]{2,1,0:T(8,128)(2,1)S(1)} %get-tuple-element.90.first_t.refs_6_, bf16[3,16,64,64]{3,2,1,0:T(8,128)(2,1)S(1)} %get-tuple-element.91.left.refs_7_), custom_call_target="tpu_custom_call" | custom-call | flops 2000000000 | bytes 4194304 | tf_op jit(solution)/shard_map/home_forward/pallas_call | solution.py:523
  33.7 6.9 %forward.2 = (bf16[3,16,64,128]{3,2,1,0:T(8,128)(2,1)S(1)}, bf16[48,3,64,256]{3,2,1,0:T(8,128)(2,1)S(1)}) custom-call(s32[8,256]{1,0:T(8,128)S(1)} %get-tuple-element.87.plan, f32[3,128]{1,0:T(4,128)S(1)} %get-tuple-element.88.amps, bf16[33,32,128]{2,1,0:T(8,128)(2,1)S(1)} %collective-permute-done.5.refs_0_, ...), custom_call_target="tpu_custom_call" | custom-call | flops 3000000000 | bytes 8388608 | tf_op jit(solution)/shard_map/forward/pallas_call | solution.py:523
  40.6 7.1 %backward.2 = (bf16[65,32,128]{2,1,0:T(8,128)(2,1)S(1)}, bf16[65,32,128]{2,1,0:T(8,128)(2,1)S(1)}) custom-call(s32[8,256]{1,0:T(8,128)S(1)} %get-tuple-element.87.plan, f32[3,128]{1,0:T(4,128)S(1)} %get-tuple-element.88.amps, bf16[3,16,64,128]{3,2,1,0:T(8,128)(2,1)S(1)} %get-tuple-element.92.refs_0_.residual, ...), custom_call_target="tpu_custom_call" | custom-call | flops 3000000000 | bytes 8388608 | tf_op jit(solution)/shard_map/backward/pallas_call | solution.py:523
  50.4 1.9 %collective-permute-start.12 = (bf16[33,32,128]{2,1,0:T(8,128)(2,1)S(1)}, bf16[33,32,128]{2,1,0:T(8,128)(2,1)S(1)}, u32[]{:S(2)}, u32[]{:S(2)}) collective-permute-start(bf16[33,32,128]{2,1,0:T(8,128)(2,1)S(1)} %get-tuple-element.104), channel_id=1, source_target_pairs={{1,3},{2,0},{3,5},{4,2},{5,7},{6,4},{9,11},{10,8},{11,13},{12,10},... | collective-permute-start | bytes 811016 | tf_op jit(solution)/shard_map/ppermute | solution.py:549
  53.0 4.2 %home_gather.2 = (f32[128,32,128]{2,1,0:T(8,128)S(1)}, f32[6,128]{1,0:T(8,128)S(1)}) custom-call(s32[5,1,128]{2,1,0:T(1,128)S(1)} %bitcast.26, f32[6,128]{1,0:T(8,128)S(1)} %get-tuple-element.69.amps, bf16[128,32,128]{2,1,0:T(8,128)(2,1)S(1)} %bitcast.19, bf16[3,17,32,128]{3,2,1,0:T(8,128)(2,1)S(1)} %home_slots.2.back, ...), custom_call_target="tpu_custom_call" | custom-call | bytes 4194304 | tf_op jit(solution)/shard_map/home_gather/pallas_call | solution.py:523
  58.8 3.1 %collective-permute-done.11.refs_0_ = bf16[33,32,128]{2,1,0:T(8,128)(2,1)S(1)} collective-permute-done((bf16[33,32,128]{2,1,0:T(8,128)(2,1)S(1)}, bf16[33,32,128]{2,1,0:T(8,128)(2,1)S(1)}, u32[]{:S(2)}, u32[]{:S(2)}) %collective-permute-start.11) | collective-permute-done | bytes 270368 | tf_op jit(solution)/shard_map/ppermute | solution.py:549
  63.8 2.4 %update.2 = (f32[128,32,128]{2,1,0:T(8,128)S(1)}, f32[6,128]{1,0:T(8,128)S(1)}, bf16[128,32,128]{2,1,0:T(8,128)(2,1)S(1)}, f32[6,128]{1,0:T(8,128)S(1)}, bf16[33...) custom-call(s32[8,128]{1,0:T(8,128)S(1)} %get-tuple-element.66.places, f32[1,128]{1,0:T(1,128)S(1)} %bitcast.31, ...), custom_call_target="tpu_custom_call" | custom-call | bytes 3145728 | tf_op jit(solution)/shard_map/update/pallas_call | solution.py:523
  66.2 2.7 %collective-permute-start.16 = (bf16[33,32,128]{2,1,0:T(8,128)(2,1)S(1)}, bf16[33,32,128]{2,1,0:T(8,128)(2,1)S(1)}, u32[]{:S(2)}, u32[]{:S(2)}) collective-permute-start(bf16[33,32,128]{2,1,0:T(8,128)(2,1)S(1)} %get-tuple-element.111), channel_id=1, source_target_pairs={{0,2},{2,4},{3,1},{4,6},{5,3},{7,5},{8,10},{10,12},{11,9},{12,14},... | collective-permute-start | bytes 811016 | tf_op jit(solution)/shard_map/ppermute | solution.py:549
  69.8 1.8 %home_sums.3.sums = f32[3,17,32,128]{3,2,1,0:T(8,128)S(1)} custom-call(s32[5,1,128]{2,1,0:T(1,128)S(1)} %bitcast.28, f32[6,128]{1,0:T(8,128)S(1)} %get-tuple-element.107.amps, bf16[128,32,128]{2,1,0:T(8,128)(2,1)S(1)} %get-tuple-element.108.morph), custom_call_target="tpu_custom_call" | custom-call | bytes 4194304 | tf_op jit(solution)/shard_map/home_sums/pallas_call | solution.py:523
  71.6 2.0 %home_forward.3.refs_4_ = f32[3,16,64,128]{3,2,1,0:T(8,128)S(1)} custom-call(f32[3,17,32,128]{3,2,1,0:T(8,128)S(1)} %home_sums.3.sums, bf16[16,64,256]{2,1,0:T(8,128)(2,1)S(1)} %get-tuple-element.90.first_t.refs_6_, bf16[3,16,64,64]{3,2,1,0:T(8,128)(2,1)S(1)} %get-tuple-element.91.left.refs_7_), custom_call_target="tpu_custom_call" | custom-call | flops 2000000000 | bytes 4194304 | tf_op jit(solution)/shard_map/home_forward/pallas_call | solution.py:523
  76.1 2.0 %collective-permute-start.17 = (bf16[33,32,128]{2,1,0:T(8,128)(2,1)S(1)}, bf16[33,32,128]{2,1,0:T(8,128)(2,1)S(1)}, u32[]{:S(2)}, u32[]{:S(2)}) collective-permute-start(bf16[33,32,128]{2,1,0:T(8,128)(2,1)S(1)} %collective-permute-done.15.refs_0_), channel_id=1, source_target_pairs={{0,1},{1,0},{2,3},{3,2},{4,5},{5,4},{6,7},{7,6},{8,9},{9,8},{10,11... | collective-permute-start | bytes 811016 | tf_op jit(solution)/shard_map/ppermute | solution.py:553
  80.2 6.9 %forward.3 = (bf16[3,16,64,128]{3,2,1,0:T(8,128)(2,1)S(1)}, bf16[48,3,64,256]{3,2,1,0:T(8,128)(2,1)S(1)}) custom-call(s32[8,256]{1,0:T(8,128)S(1)} %get-tuple-element.113.plan, f32[3,128]{1,0:T(4,128)S(1)} %get-tuple-element.114.amps, bf16[33,32,128]{2,1,0:T(8,128)(2,1)S(1)} %collective-permute-done.15.refs_0_, ...), custom_call_target="tpu_custom_call" | custom-call | flops 3000000000 | bytes 8388608 | tf_op jit(solution)/shard_map/forward/pallas_call | solution.py:523
  87.1 7.1 %backward.3 = (bf16[65,32,128]{2,1,0:T(8,128)(2,1)S(1)}, bf16[65,32,128]{2,1,0:T(8,128)(2,1)S(1)}) custom-call(s32[8,256]{1,0:T(8,128)S(1)} %get-tuple-element.113.plan, f32[3,128]{1,0:T(4,128)S(1)} %get-tuple-element.114.amps, bf16[3,16,64,128]{3,2,1,0:T(8,128)(2,1)S(1)} %get-tuple-element.115.refs_0_.residual, ...), custom_call_target="tpu_custom_call" | custom-call | flops 3000000000 | bytes 8388608 | tf_op jit(solution)/shard_map/backward/pallas_call | solution.py:523
  96.7 1.9 %collective-permute-start.22 = (bf16[33,32,128]{2,1,0:T(8,128)(2,1)S(1)}, bf16[33,32,128]{2,1,0:T(8,128)(2,1)S(1)}, u32[]{:S(2)}, u32[]{:S(2)}) collective-permute-start(bf16[33,32,128]{2,1,0:T(8,128)(2,1)S(1)} %get-tuple-element.126), channel_id=1, source_target_pairs={{1,3},{2,0},{3,5},{4,2},{5,7},{6,4},{9,11},{10,8},{11,13},{12,10},... | collective-permute-start | bytes 811016 | tf_op jit(solution)/shard_map/ppermute | solution.py:549
  99.2 2.8 %home_gather.3 = (f32[128,16,128]{2,1,0:T(8,128)S(1)}, f32[3,128]{1,0:T(4,128)S(1)}) custom-call(s32[5,1,128]{2,1,0:T(1,128)S(1)} %bitcast.29, f32[6,128]{1,0:T(8,128)S(1)} %get-tuple-element.107.amps, bf16[128,32,128]{2,1,0:T(8,128)(2,1)S(1)} %get-tuple-element.108.morph, bf16[3,17,32,128]{3,2,1,0:T(8,128)(2,1)S(1)} %home_slots.3.back, ...), custom_call_target="tpu_custom_call" | custom-call | bytes 4194304 | tf_op jit(solution)/shard_map/home_gather/pallas_call | solution.py:523
  102.0 3.5 %collective-permute-done.22.refs_1_ = bf16[33,32,128]{2,1,0:T(8,128)(2,1)S(1)} collective-permute-done((bf16[33,32,128]{2,1,0:T(8,128)(2,1)S(1)}, bf16[33,32,128]{2,1,0:T(8,128)(2,1)S(1)}, u32[]{:S(2)}, u32[]{:S(2)}) %collective-permute-start.22) | collective-permute-done | bytes 270368 | tf_op jit(solution)/shard_map/ppermute | solution.py:549
  109.8 3.2 %update.3 = (f32[128,2048]{1,0:T(8,128)}, f32[3,1,128]{2,1,0:T(1,128)}) custom-call(s32[8,128]{1,0:T(8,128)S(1)} %get-tuple-element.66.places, f32[1,128]{1,0:T(1,128)S(1)} %bitcast.32, s32[5,1,128]{2,1,0:T(1,128)S(1)} %bitcast.30, f32[1,128]{1,0:T(1,128)S(1)} %bitcast.34, bf16[4,128,128]{2,1,0:T(8,128)(2,1)S(1)} %get-tuple-element.67.hots, ...), custom_call_target="tpu_custom_call" | custom-call | bytes 3145728 | tf_op jit(solution)/shard_map/update/pallas_call | solution.py:523
  (66 shorter events, 30.8 us)
Async XLA Ops:
  1.8 8.8 %collective-permute-start.1 = (bf16[3,4,4096]{2,1,0:T(4,128)(2,1)S(1)}, bf16[3,4,4096]{2,1,0:T(4,128)(2,1)S(1)}, u32[]{:S(2)}, u32[]{:S(2)}) collective-permute-start(bf16[3,4,4096]{2,1,0:T(4,128)(2,1)S(1)} %slice_select_fusion), channel_id=1, source_target_pairs={{0,16},{8,24},{1,17},{9,25},{2,18},{10,26},{3,19},{11,27},{4,20},{... | collective-permute-start | bytes 294920 | tf_op jit(solution)/shard_map/ppermute | solution.py:563
  6.0 3.5 %collective-permute-start = (f32[3,1,128]{2,1,0:T(1,128)}, f32[3,1,128]{2,1,0:T(1,128)S(1)}, u32[]{:S(2)}, u32[]{:S(2)}) collective-permute-start(f32[3,1,128]{2,1,0:T(1,128)} %bitcast.35), channel_id=1, source_target_pairs={{0,1},{1,0},{2,3},{3,2},{4,5},{5,4},{6,7},{7,6},{8,9},{9,8},{10,11... | collective-permute-start | bytes 4616 | tf_op jit(solution)/shard_map/ppermute | solution.py:553
  10.7 7.1 %collective-permute-start.3 = (bf16[3,4,4096]{2,1,0:T(4,128)(2,1)S(1)}, bf16[3,4,4096]{2,1,0:T(4,128)(2,1)S(1)}, u32[]{:S(2)}, u32[]{:S(2)}) collective-permute-start(bf16[3,4,4096]{2,1,0:T(4,128)(2,1)S(1)} %broadcast_select_fusion.refs_0_), channel_id=1, source_target_pairs={{0,8},{8,0},{16,24},{24,16},{1,9},{9,1},{17,25},{25,17},{2,10},{10... | collective-permute-start | bytes 294920 | tf_op jit(solution)/shard_map/ppermute | solution.py:566
  13.9 9.4 %collective-permute-start.2 = (bf16[3,4,4096]{2,1,0:T(4,128)(2,1)S(1)}, bf16[3,4,4096]{2,1,0:T(4,128)(2,1)S(1)}, u32[]{:S(2)}, u32[]{:S(2)}) collective-permute-start(bf16[3,4,4096]{2,1,0:T(4,128)(2,1)S(1)} %broadcast_select_fusion.refs_0_), channel_id=1, source_target_pairs={{0,2},{2,0},{4,6},{6,4},{1,3},{3,1},{5,7},{7,5},{8,10},{10,8},{12,... | collective-permute-start | bytes 294920 | tf_op jit(solution)/shard_map/ppermute | solution.py:569
  15.2 10.2 %collective-permute-start.5 = (bf16[33,32,128]{2,1,0:T(8,128)(2,1)S(1)}, bf16[33,32,128]{2,1,0:T(8,128)(2,1)S(1)}, u32[]{:S(2)}, u32[]{:S(2)}) collective-permute-start(bf16[33,32,128]{2,1,0:T(8,128)(2,1)S(1)} %get-tuple-element.83), channel_id=1, source_target_pairs={{0,8},{1,25},{2,10},{3,27},{4,12},{5,29},{6,14},{7,31},{8,16},{9,1... | collective-permute-start | bytes 811016 | tf_op jit(solution)/shard_map/ppermute | solution.py:549
  17.9 5.5 %collective-permute-start.4 = (bf16[3,4,4096]{2,1,0:T(4,128)(2,1)S(1)}, bf16[3,4,4096]{2,1,0:T(4,128)(2,1)S(1)}, u32[]{:S(2)}, u32[]{:S(2)}) collective-permute-start(bf16[3,4,4096]{2,1,0:T(4,128)(2,1)S(1)} %collective-permute-done.3.refs_1_), channel_id=1, source_target_pairs={{0,2},{2,0},{4,6},{6,4},{1,3},{3,1},{5,7},{7,5},{8,10},{10,8},{12,... | collective-permute-start | bytes 294920 | tf_op jit(solution)/shard_map/ppermute | solution.py:569
  20.2 8.6 %collective-permute-start.6 = (bf16[33,32,128]{2,1,0:T(8,128)(2,1)S(1)}, bf16[33,32,128]{2,1,0:T(8,128)(2,1)S(1)}, u32[]{:S(2)}, u32[]{:S(2)}) collective-permute-start(bf16[33,32,128]{2,1,0:T(8,128)(2,1)S(1)} %get-tuple-element.84), channel_id=1, source_target_pairs={{0,2},{2,4},{3,1},{4,6},{5,3},{7,5},{8,10},{10,12},{11,9},{12,14},... | collective-permute-start | bytes 811016 | tf_op jit(solution)/shard_map/ppermute | solution.py:549
  28.7 4.4 %collective-permute-start.7 = (bf16[33,32,128]{2,1,0:T(8,128)(2,1)S(1)}, bf16[33,32,128]{2,1,0:T(8,128)(2,1)S(1)}, u32[]{:S(2)}, u32[]{:S(2)}) collective-permute-start(bf16[33,32,128]{2,1,0:T(8,128)(2,1)S(1)} %collective-permute-done.5.refs_0_), channel_id=1, source_target_pairs={{0,1},{1,0},{2,3},{3,2},{4,5},{5,4},{6,7},{7,6},{8,9},{9,8},{10,11... | collective-permute-start | bytes 811016 | tf_op jit(solution)/shard_map/ppermute | solution.py:553
  31.0 2.1 %collective-permute-start.8 = (bf16[33,32,128]{2,1,0:T(8,128)(2,1)S(1)}, bf16[33,32,128]{2,1,0:T(8,128)(2,1)S(1)}, u32[]{:S(2)}, u32[]{:S(2)}) collective-permute-start(bf16[33,32,128]{2,1,0:T(8,128)(2,1)S(1)} %collective-permute-done.6.refs_1_), channel_id=1, source_target_pairs={{0,1},{1,0},{2,3},{3,2},{4,5},{5,4},{6,7},{7,6},{8,9},{9,8},{10,11... | collective-permute-start | bytes 811016 | tf_op jit(solution)/shard_map/ppermute | solution.py:553
  47.8 2.1 %collective-permute-start.9 = (bf16[65,32,128]{2,1,0:T(8,128)(2,1)S(1)}, bf16[65,32,128]{2,1,0:T(8,128)(2,1)S(1)}, u32[]{:S(2)}, u32[]{:S(2)}) collective-permute-start(bf16[65,32,128]{2,1,0:T(8,128)(2,1)S(1)} %get-tuple-element.96), channel_id=1, source_target_pairs={{0,1},{1,0},{2,3},{3,2},{4,5},{5,4},{6,7},{7,6},{8,9},{9,8},{10,11... | collective-permute-start | bytes 1597448 | tf_op jit(solution)/shard_map/ppermute | solution.py:553
  49.9 3.2 %collective-permute-start.10 = (bf16[3,17,32,128]{3,2,1,0:T(8,128)(2,1)S(1)}, bf16[3,17,32,128]{3,2,1,0:T(8,128)(2,1)S(1)}, u32[]{:S(2)}, u32[]{:S(2)}) collective-permute-start(bf16[3,17,32,128]{3,2,1,0:T(8,128)(2,1)S(1)} %home_slots.2.back), channel_id=1, source_target_pairs={{0,1},{1,0},{2,3},{3,2},{4,5},{5,4},{6,7},{7,6},{8,9},{9,8},{10,11... | collective-permute-start | bytes 1253384 | tf_op jit(solution)/shard_map/ppermute | solution.py:553
  50.4 8.4 %collective-permute-start.12 = (bf16[33,32,128]{2,1,0:T(8,128)(2,1)S(1)}, bf16[33,32,128]{2,1,0:T(8,128)(2,1)S(1)}, u32[]{:S(2)}, u32[]{:S(2)}) collective-permute-start(bf16[33,32,128]{2,1,0:T(8,128)(2,1)S(1)} %get-tuple-element.104), channel_id=1, source_target_pairs={{1,3},{2,0},{3,5},{4,2},{5,7},{6,4},{9,11},{10,8},{11,13},{12,10},... | collective-permute-start | bytes 811016 | tf_op jit(solution)/shard_map/ppermute | solution.py:549
  52.3 9.6 %collective-permute-start.11 = (bf16[33,32,128]{2,1,0:T(8,128)(2,1)S(1)}, bf16[33,32,128]{2,1,0:T(8,128)(2,1)S(1)}, u32[]{:S(2)}, u32[]{:S(2)}) collective-permute-start(bf16[33,32,128]{2,1,0:T(8,128)(2,1)S(1)} %get-tuple-element.102), channel_id=1, source_target_pairs={{0,24},{1,9},{2,26},{3,11},{4,28},{5,13},{6,30},{7,15},{8,0},{9,17... | collective-permute-start | bytes 811016 | tf_op jit(solution)/shard_map/ppermute | solution.py:549
  61.9 1.9 %collective-permute-start.14 = (bf16[33,32,128]{2,1,0:T(8,128)(2,1)S(1)}, bf16[33,32,128]{2,1,0:T(8,128)(2,1)S(1)}, u32[]{:S(2)}, u32[]{:S(2)}) collective-permute-start(bf16[33,32,128]{2,1,0:T(8,128)(2,1)S(1)} %collective-permute-done.12.refs_1_), channel_id=1, source_target_pairs={{0,1},{1,0},{2,3},{3,2},{4,5},{5,4},{6,7},{7,6},{8,9},{9,8},{10,11... | collective-permute-start | bytes 811016 | tf_op jit(solution)/shard_map/ppermute | solution.py:553
  66.2 8.5 %collective-permute-start.16 = (bf16[33,32,128]{2,1,0:T(8,128)(2,1)S(1)}, bf16[33,32,128]{2,1,0:T(8,128)(2,1)S(1)}, u32[]{:S(2)}, u32[]{:S(2)}) collective-permute-start(bf16[33,32,128]{2,1,0:T(8,128)(2,1)S(1)} %get-tuple-element.111), channel_id=1, source_target_pairs={{0,2},{2,4},{3,1},{4,6},{5,3},{7,5},{8,10},{10,12},{11,9},{12,14},... | collective-permute-start | bytes 811016 | tf_op jit(solution)/shard_map/ppermute | solution.py:549
  68.9 7.1 %collective-permute-start.15 = (bf16[33,32,128]{2,1,0:T(8,128)(2,1)S(1)}, bf16[33,32,128]{2,1,0:T(8,128)(2,1)S(1)}, u32[]{:S(2)}, u32[]{:S(2)}) collective-permute-start(bf16[33,32,128]{2,1,0:T(8,128)(2,1)S(1)} %get-tuple-element.109), channel_id=1, source_target_pairs={{0,8},{1,25},{2,10},{3,27},{4,12},{5,29},{6,14},{7,31},{8,16},{9,1... | collective-permute-start | bytes 811016 | tf_op jit(solution)/shard_map/ppermute | solution.py:549
  76.1 3.2 %collective-permute-start.17 = (bf16[33,32,128]{2,1,0:T(8,128)(2,1)S(1)}, bf16[33,32,128]{2,1,0:T(8,128)(2,1)S(1)}, u32[]{:S(2)}, u32[]{:S(2)}) collective-permute-start(bf16[33,32,128]{2,1,0:T(8,128)(2,1)S(1)} %collective-permute-done.15.refs_0_), channel_id=1, source_target_pairs={{0,1},{1,0},{2,3},{3,2},{4,5},{5,4},{6,7},{7,6},{8,9},{9,8},{10,11... | collective-permute-start | bytes 811016 | tf_op jit(solution)/shard_map/ppermute | solution.py:553
  78.1 1.6 %collective-permute-start.18 = (bf16[33,32,128]{2,1,0:T(8,128)(2,1)S(1)}, bf16[33,32,128]{2,1,0:T(8,128)(2,1)S(1)}, u32[]{:S(2)}, u32[]{:S(2)}) collective-permute-start(bf16[33,32,128]{2,1,0:T(8,128)(2,1)S(1)} %collective-permute-done.16.refs_1_), channel_id=1, source_target_pairs={{0,1},{1,0},{2,3},{3,2},{4,5},{5,4},{6,7},{7,6},{8,9},{9,8},{10,11... | collective-permute-start | bytes 811016 | tf_op jit(solution)/shard_map/ppermute | solution.py:553
  94.2 1.9 %collective-permute-start.19 = (bf16[65,32,128]{2,1,0:T(8,128)(2,1)S(1)}, bf16[65,32,128]{2,1,0:T(8,128)(2,1)S(1)}, u32[]{:S(2)}, u32[]{:S(2)}) collective-permute-start(bf16[65,32,128]{2,1,0:T(8,128)(2,1)S(1)} %get-tuple-element.117), channel_id=1, source_target_pairs={{0,1},{1,0},{2,3},{3,2},{4,5},{5,4},{6,7},{7,6},{8,9},{9,8},{10,11... | collective-permute-start | bytes 1597448 | tf_op jit(solution)/shard_map/ppermute | solution.py:553
  96.2 3.0 %collective-permute-start.20 = (bf16[3,17,32,128]{3,2,1,0:T(8,128)(2,1)S(1)}, bf16[3,17,32,128]{3,2,1,0:T(8,128)(2,1)S(1)}, u32[]{:S(2)}, u32[]{:S(2)}) collective-permute-start(bf16[3,17,32,128]{3,2,1,0:T(8,128)(2,1)S(1)} %home_slots.3.back), channel_id=1, source_target_pairs={{0,1},{1,0},{2,3},{3,2},{4,5},{5,4},{6,7},{7,6},{8,9},{9,8},{10,11... | collective-permute-start | bytes 1253384 | tf_op jit(solution)/shard_map/ppermute | solution.py:553
  96.7 8.8 %collective-permute-start.22 = (bf16[33,32,128]{2,1,0:T(8,128)(2,1)S(1)}, bf16[33,32,128]{2,1,0:T(8,128)(2,1)S(1)}, u32[]{:S(2)}, u32[]{:S(2)}) collective-permute-start(bf16[33,32,128]{2,1,0:T(8,128)(2,1)S(1)} %get-tuple-element.126), channel_id=1, source_target_pairs={{1,3},{2,0},{3,5},{4,2},{5,7},{6,4},{9,11},{10,8},{11,13},{12,10},... | collective-permute-start | bytes 811016 | tf_op jit(solution)/shard_map/ppermute | solution.py:549
  98.6 8.3 %collective-permute-start.21 = (bf16[33,32,128]{2,1,0:T(8,128)(2,1)S(1)}, bf16[33,32,128]{2,1,0:T(8,128)(2,1)S(1)}, u32[]{:S(2)}, u32[]{:S(2)}) collective-permute-start(bf16[33,32,128]{2,1,0:T(8,128)(2,1)S(1)} %get-tuple-element.124), channel_id=1, source_target_pairs={{0,24},{1,9},{2,26},{3,11},{4,28},{5,13},{6,30},{7,15},{8,0},{9,17... | collective-permute-start | bytes 811016 | tf_op jit(solution)/shard_map/ppermute | solution.py:549
  106.9 2.5 %collective-permute-start.23 = (bf16[33,32,128]{2,1,0:T(8,128)(2,1)S(1)}, bf16[33,32,128]{2,1,0:T(8,128)(2,1)S(1)}, u32[]{:S(2)}, u32[]{:S(2)}) collective-permute-start(bf16[33,32,128]{2,1,0:T(8,128)(2,1)S(1)} %collective-permute-done.21.refs_0_), channel_id=1, source_target_pairs={{0,1},{1,0},{2,3},{3,2},{4,5},{5,4},{6,7},{7,6},{8,9},{9,8},{10,11... | collective-permute-start | bytes 811016 | tf_op jit(solution)/shard_map/ppermute | solution.py:553
  108.2 1.6 %collective-permute-start.24 = (bf16[33,32,128]{2,1,0:T(8,128)(2,1)S(1)}, bf16[33,32,128]{2,1,0:T(8,128)(2,1)S(1)}, u32[]{:S(2)}, u32[]{:S(2)}) collective-permute-start(bf16[33,32,128]{2,1,0:T(8,128)(2,1)S(1)} %collective-permute-done.22.refs_1_), channel_id=1, source_target_pairs={{0,1},{1,0},{2,3},{3,2},{4,5},{5,4},{6,7},{7,6},{8,9},{9,8},{10,11... | collective-permute-start | bytes 811016 | tf_op jit(solution)/shard_map/ppermute | solution.py:553
  (8 other events, 66.5 us)

commit v2 on v1

--- a/solution.py
+++ b/solution.py
@@ -58,6 +58,12 @@
 def twofold(packed):
     low, flip = half_masks(ROWS)[0], turned(packed)
     return jnp.concatenate([jnp.where(low, packed, flip), jnp.where(low, flip, packed)], axis=0)
+
+
+def rounded(stamp):
+    if stamp.dtype == F32:
+        stamp = jnp.maximum(stamp, 0.0).astype(BF16)
+    return stamp.astype(F32)
 
 
 def half_rows():
@@ -90,14 +96,14 @@
         places[NEAR + near : NEAR + near + 1, :] = count.astype(jnp.int32)
 
 
-def write_messages(messages, slots, amps, hots, places, stamps):
+def write_messages(messages, slots, amps, hots, places, stamp_of):
     first = lax.axis_index("band") == 0
     row = iota((ROWS, slots.shape[1]), 0)
     for turn in range(2):
         near = 2 * turn + lax.axis_index("band")
 
         def pick(n, carry, near=near, turn=turn):
-            messages[turn][n] = stamps[places[near, n]]
+            messages[turn][n] = stamp_of(places[near, n])
             return carry
 
         lax.fori_loop(0, CAP, pick, 0, unroll=8)
@@ -113,22 +119,23 @@
 def pack_kernel(places, slots_ref, amps_mine, amps_theirs, hots, morph, *out):
     messages, amps_out, amps_q = out[:2], out[2], out[3]
     amps = jnp.concatenate(by_core(rows_of(amps_mine), rows_of(amps_theirs)), axis=0)
-    write_messages(messages, rows_of(slots_ref), amps, hots, places, morph)
+    write_messages(messages, rows_of(slots_ref), amps, hots, places, lambda s: morph[s])
     amps_out[...] = amps
     amps_q[...] = amps.astype(BF16).astype(F32)
 
 
-def order_kernel(num_slots, *refs):
-    plan, amps = refs[NEAR:]
-    none = NEAR * CAP
+def order_kernel(num_slots, again, *refs):
+    amps, none = refs[NEAR], NEAR * CAP
     bands = amps.shape[0]
     meta = jnp.zeros((ROWS, LANES), F32)
     for turn in range(2):
         pair = by_core(refs[turn][CAP].astype(F32), refs[2 + turn][CAP].astype(F32))
         for core in range(2):
             meta = meta + pltpu.roll(pair[core], (2 * turn + core) * CAP, 1)
-    slot, kernel = meta[0:1], meta[1:2]
     amps[...] = by_core(meta[2 : 2 + bands], meta[2 + bands : 2 + 2 * bands])[0]
+    if again:
+        return
+    plan, slot, kernel = refs[NEAR + 1], meta[0:1], meta[1:2]
     plan[SLOT_OF : SLOT_OF + 1, :LANES] = jnp.maximum(slot - 1.0, 0.0).astype(jnp.int32)
     live = (slot > 0.0).astype(F32)
     hot = (iota((num_slots, none), 0).astype(F32) == kernel).astype(F32) * live
@@ -230,7 +237,7 @@
 
     def add(s, carry):
         q = lists[0, 0, s]
-        stamp = morph[s].astype(F32)
+        stamp = rounded(morph[s])
         for band in range(bands):
             sums[band, q] += amps[first + band, s] * stamp
         return carry
@@ -238,7 +245,7 @@
     lax.fori_loop(0, lists.shape[2], add, 0, unroll=4)
 
 
-def home_forward_kernel(bands, sums, first_t, left, total, inner_all):
+def home_forward_kernel(bands, sums, observed, first_t, left, total, inner_all):
     num_slots = total.shape[1]
     masks = half_masks(SIDE)
 
@@ -255,7 +262,8 @@
 
     def slot(q, carry):
         for band in range(bands):
-            total[band, q] = jnp.where(masks[band % 2], dot(left[band, q], inner_all[band, q]), 0.0)
+            image = dot(left[band, q], inner_all[band, q]) - twofold(observed[band, q].astype(F32))
+            total[band, q] = jnp.where(masks[band % 2], image, 0.0)
         return carry
 
     lax.fori_loop(0, num_slots, inner_products, 0, unroll=4)
@@ -275,8 +283,8 @@
 
 
 def forward_kernel(bands, plan, amps, *refs):
-    home, observed, first_t, left = refs[NEAR : NEAR + 4]
-    residual, inner_all, stamps, *totals = refs[NEAR + 4 :]
+    home, first_t, left = refs[NEAR : NEAR + 3]
+    residual, inner_all, stamps, *totals = refs[NEAR + 3 :]
     totals = [totals[2 * band : 2 * band + 2] for band in range(bands)]
     num_slots = home.shape[1]
     none = NEAR * CAP
@@ -329,8 +337,7 @@
     def slot(q, carry):
         for band in range(bands):
             model = jnp.where(masks[0], totals[band][0][q], totals[band][1][q])
-            seen = twofold(observed[band, q].astype(F32))
-            residual[band, q] = (model + turned(model) - seen).astype(BF16)
+            residual[band, q] = (model + turned(model)).astype(BF16)
         return carry
 
     lax.fori_loop(0, num_slots, slot, 0, unroll=8)
@@ -415,13 +422,13 @@
     lax.fori_loop(0, num_slots, slot, 0, unroll=8)
 
 
-def home_gather_kernel(bands, last, lists, amps, morph, back, received, keep, grad_a, sums):
+def home_gather_kernel(bands, last, lists, amps, eta_m, morph, back, received, keep, grad_a, sums):
     core = lax.axis_index("band")
     mine = pl.ds(half_rows(), HALF) if last else pl.ds(0, ROWS)
 
     def gather(s, carry):
         q = lists[0, 0, s]
-        stamp = morph[s].astype(F32)
+        stamp = rounded(morph[s])
         grad = jnp.zeros((HALF if last else ROWS, LANES), F32)
         for ref, side in ((back, core), (received, 1 - core)):
             for band in range(bands):
@@ -435,7 +442,7 @@
                     grad = grad + amp * seen
                 along = jnp.sum(seen * stamp, axis=0, keepdims=True)
                 sums[side * bands + band, pl.ds(s, 1), :] = along
-        keep[s] = grad
+        keep[s] = jnp.maximum(morph[s, mine, :].astype(F32), 0.0) - eta_m[0, s] * grad
         return carry
 
     lax.fori_loop(0, lists.shape[2], gather, 0, unroll=4)
@@ -463,10 +470,9 @@
         messages[turn][CAP] = meta.astype(BF16)
 
 
-def update_kernel(first, last, places, eta_m, slots_ref, eta_a, hots, amps_ref, grad_a, morph, home, *refs):
+def update_kernel(last, places, eta_m, slots_ref, eta_a, hots, amps_ref, grad_a, home, *refs):
     grads, out = refs[:NEAR], refs[NEAR:]
-    state, amps_out, work = out[0], out[1], out[-1]
-    sources = slots_ref.shape[2]
+    state, amps_out, work = out[0], out[1], out[-1] if last else out[0]
     core = lax.axis_index("band")
     mine = pl.ds(half_rows(), HALF) if last else pl.ds(0, ROWS)
     nears = (core, 2 + core, 1 - core, 3 - core)
@@ -494,28 +500,23 @@
     for ref, near in zip(grads, nears):
 
         def add(n, carry, ref=ref, near=near):
-            work[places[near, n]] += ref[n, mine, :].astype(F32)
+            s = places[near, n]
+            work[s] -= eta_m[0, s] * ref[n, mine, :].astype(F32)
             return carry
 
         lax.fori_loop(0, CAP, add, 0, unroll=8)
 
-    def step(s, carry):
-        new = jnp.maximum(morph[s, mine, :].astype(F32) - eta_m[0, s] * work[s], 0.0)
-        if last:
-            work[s] = new
-        else:
-            state[s] = new
-            out[2][s] = new.astype(BF16)
-        return carry
-
-    lax.fori_loop(0, sources, step, 0, unroll=8)
     if last:
         for r in range(HALF):
-            state[:, r * LANES : (r + 1) * LANES] = work[:, r, :]
+            state[:, r * LANES : (r + 1) * LANES] = jnp.maximum(work[:, r, :], 0.0)
         return
-    stamps, amps_q, messages = out[2], out[3], out[4:6]
+    amps_q, messages = out[2], out[3:5]
     amps_q[...] = amps.astype(BF16).astype(F32)
-    write_messages(messages, rows_of(slots_ref), amps, hots, places, stamps)
+
+    def stamp_of(s):
+        return jnp.maximum(state[s], 0.0).astype(BF16)
+
+    write_messages(messages, rows_of(slots_ref), amps, hots, places, stamp_of)
 
 
 def call(body, name, operands, scalars, outs, scratch=(), flops=0, moved=0):
@@ -561,13 +562,12 @@
         along = [(0, 1), (1, 0), (2, 3), (3, 2)]
         mine = jnp.where(lax.axis_index("dec") % 2 == 0, psf[:, : held // 2], psf[:, held // 2 :])
         far = lax.ppermute(mine, "ra", [(0, 2), (1, 3)])
+        far, sums = lax.optimization_barrier((far, sums))
         here = jnp.where(lax.axis_index("ra") < 2, mine, far)
         here, messages[0] = lax.optimization_barrier((here, messages[0]))
         near = lax.ppermute(here, "ra", along)
-        near, sums = lax.optimization_barrier((near, sums))
         halves = make_tables((here, near), bands)
         others = (lax.ppermute(here, "dec", across), lax.ppermute(near, "dec", across))
-        messages[1], *halves = lax.optimization_barrier((messages[1], *halves))
         return make_tables(others, bands, halves), messages, sums
     return make_tables((lax.all_gather(psf, "ra", axis=1, tiled=True)[:, :num_slots],), bands), messages, sums
 
@@ -615,7 +615,7 @@
     sums = home_sums(amps_q, full)
     tables, messages, sums = all_tables(psf_kernels, num_slots, messages, sums)
     first_t, left, left_t, right = tables
-    morph = state = full
+    morph, plan = full, None
     for sweep in range(ITERS):
         last = sweep == ITERS - 1
         own = [stepped(messages[0], "ra", 1), stepped(messages[1], "dec", 1)]
@@ -626,7 +626,7 @@
         home = call(
             functools.partial(home_forward_kernel, bands),
             "home_forward",
-            (sums, first_t, left),
+            (sums, seen, first_t, left),
             0,
             [((bands, num_slots, SIDE, LANES), F32)],
             [((bands, num_slots, SIDE, LANES), BF16)],
@@ -636,21 +636,19 @@
         if sweep > 0:
             own = [lax.optimization_barrier((home, x))[1] for x in own]
         other = [swapped(x) for x in own]
-        order = call(
-            functools.partial(order_kernel, num_slots),
+        amps_near, *new_plan = call(
+            functools.partial(order_kernel, num_slots, sweep > 0),
             "order",
             (*own, *other),
             0,
-            [
-                ((8, -(-chunks * GROUP // LANES) * LANES), jnp.int32),
-                ((bands, LANES), F32),
-            ],
+            [((bands, LANES), F32)] + [((8, -(-chunks * GROUP // LANES) * LANES), jnp.int32)] * (sweep == 0),
             moved=2**20,
         )
+        plan = new_plan[0] if new_plan else plan
         residual, inner_all = call(
             functools.partial(forward_kernel, bands),
             "forward",
-            (*order, *own, *other, home, seen, first_t, left),
+            (plan, amps_near, *own, *other, home, first_t, left),
             2,
             [
                 ((bands, num_slots, SIDE, LANES), BF16),
@@ -664,7 +662,7 @@
         keep, send = call(
             functools.partial(backward_kernel, bands),
             "backward",
-            (*order, residual, inner_all, left_t, right),
+            (plan, amps_near, residual, inner_all, left_t, right),
             2,
             [half_of_near] * 2,
             [((chunks, WIDE, WIDE), BF16), ((bands, near_all + 8, LANES), F32)],
@@ -690,8 +688,8 @@
         home_grad, grad_a = call(
             functools.partial(home_gather_kernel, bands, last),
             "home_gather",
-            (lists, amps_q, morph, back, back_received),
-            2,
+            (lists, amps_q, eta_m, morph, back, back_received),
+            3,
             [(part, F32), ((bands_here, sources), F32)],
             [((2 * bands, sources, LANES), F32)],
             moved=4 * 2**20,
@@ -701,18 +699,19 @@
         outs = [((sources, HALF * LANES) if last else all_stamps, F32)]
         outs += [((bands, 1, sources) if last else (2 * bands, sources), F32)]
         if not last:
-            outs += [(all_stamps, BF16), ((bands_here, sources), F32)] + [stamp] * 2
+            outs += [((bands_here, sources), F32)] + [stamp] * 2
         state, amps, *more = call(
-            functools.partial(update_kernel, sweep == 0, last),
+            functools.partial(update_kernel, last),
             "update",
-            (places, eta_m, lists, eta_a, hots, amps, grad_a, state, home_grad, *grads),
+            (places, eta_m, lists, eta_a, hots, amps, grad_a, home_grad, *grads),
             2,
             outs,
-            [(part, F32)],
+            [(part, F32)] if last else (),
             moved=3 * 2**20,
         )
         if not last:
-            morph, amps_q, *messages = more
+            morph = state
+            amps_q, *messages = more
     return state[None, None], amps.reshape(1, 1, bands, sources)
 
 

time: 115 us -> 112 us (0.974)
  Pallas kernels: 56.7 us -> 53.4 us
  waiting for transfers between devices: 21.2 us -> 22.5 us
    ppermute x8, waiting for transfers between devices: 15.4 us -> 11.4 us  [stepped(): return lax.ppermute(value, ('ra', 'dec', 'band'), pairs)]
    ppermute x13, starting transfers between devices: 8.89 us -> 5.44 us  [swapped(): return lax.ppermute(value, 'band', [(0, 1), (1, 0)])]
    pallas_call x22, Pallas kernels: 56.7 us -> 53.4 us  [call(): pl.pallas_call(body, out_shape=[jax.ShapeDtypeStruct(shape, dtype) for sh...]
    ppermute x1, waiting for transfers between devices: 0.01 us -> 3.28 us  [all_tables(): lax.ppermute(here, 'dec', across)]
    ppermute x8, starting transfers between devices: 14.6 us -> 17.8 us  [stepped(): return lax.ppermute(value, ('ra', 'dec', 'band'), pairs)]
    ppermute x1, waiting for transfers between devices: 0.01 us -> 2.11 us  [all_tables(): lax.ppermute(near, 'dec', across)]
  transfers between devices with their start and end apart: 25 -> 25, of which waited for: 15 -> 16; matrix products, arithmetic and copies ran while one was open for 1% -> 1% of each run, Pallas kernels for 19% -> 20%
where the time goes in v2:
time: 112 us; the launch traced here: 111 us
  Pallas kernels  53.4 us (48%)
  starting transfers between devices  30.3 us (27%)
  waiting for transfers between devices  22.5 us (20%)
  local copies, waits for them, and re-layouts  2.29 us (2%)
  other arithmetic  1.21 us (1%)
    pallas_call x22, Pallas kernels, call(): pl.pallas_call(body, out_shape=[jax.ShapeDtypeStruct(shape, dtype) for sh...  53.4 us
    ppermute x8, starting transfers between devices, stepped(): return lax.ppermute(value, ('ra', 'dec', 'band'), pairs)  17.8 us
    ppermute x8, waiting for transfers between devices, stepped(): return lax.ppermute(value, ('ra', 'dec', 'band'), pairs)  11.4 us
    ppermute x13, waiting for transfers between devices, swapped(): return lax.ppermute(value, 'band', [(0, 1), (1, 0)])  5.7 us
    ppermute x13, starting transfers between devices, swapped(): return lax.ppermute(value, 'band', [(0, 1), (1, 0)])  5.44 us
    ppermute x1, starting transfers between devices, all_tables(): far = lax.ppermute(mine, 'ra', [(0, 2), (1, 3)])  4.22 us
    ppermute x1, waiting for transfers between devices, all_tables(): lax.ppermute(here, 'dec', across)  3.28 us
    unnamed x16, local copies, waits for them, and re-layouts  2.29 us
  transfers between devices with their start and end apart: 25, of which 16 were waited for; matrix products, arithmetic and copies ran while one was open for 1% of the time, Pallas kernels for 20%

profile of v2, /device:TPU:5, one launch (start us, length us, event | category | flops | bytes accessed | tf_op | source)
XLA Modules:
  0.0 110.5 jit_solution(9744423240600034674)
XLA Ops:
  1.8 4.2 %collective-permute-start.1 = (bf16[3,4,4096]{2,1,0:T(4,128)(2,1)S(1)}, bf16[3,4,4096]{2,1,0:T(4,128)(2,1)S(1)}, u32[]{:S(2)}, u32[]{:S(2)}) collective-permute-start(bf16[3,4,4096]{2,1,0:T(4,128)(2,1)S(1)} %slice_select_fusion), channel_id=1, source_target_pairs={{0,16},{8,24},{1,17},{9,25},{2,18},{10,26},{3,19},{11,27},{4,20},{... | collective-permute-start | bytes 294920 | tf_op jit(solution)/shard_map/ppermute | solution.py:564
  10.6 1.8 %home_sums.2.sums = f32[3,17,32,128]{3,2,1,0:T(8,128)S(1)} custom-call(s32[5,1,128]{2,1,0:T(1,128)S(1)} %bitcast.24, f32[6,128]{1,0:T(8,128)S(1)} %get-tuple-element.61.amps, bf16[128,32,128]{2,1,0:T(8,128)(2,1)S(1)} %bitcast.18), custom_call_target="tpu_custom_call" | custom-call | bytes 4194304 | tf_op jit(solution)/shard_map/home_sums/pallas_call | solution.py:524
  13.9 3.1 %collective-permute-start.6 = (bf16[33,32,128]{2,1,0:T(8,128)(2,1)S(1)}, bf16[33,32,128]{2,1,0:T(8,128)(2,1)S(1)}, u32[]{:S(2)}, u32[]{:S(2)}) collective-permute-start(bf16[33,32,128]{2,1,0:T(8,128)(2,1)S(1)} %get-tuple-element.71), channel_id=1, source_target_pairs={{0,2},{2,4},{3,1},{4,6},{5,3},{7,5},{8,10},{10,12},{11,9},{12,14},... | collective-permute-start | bytes 811016 | tf_op jit(solution)/shard_map/ppermute | solution.py:550
  19.4 2.0 %tables.2 = (bf16[8,64,256]{2,1,0:T(8,128)(2,1)S(1)}, bf16[3,8,64,64]{3,2,1,0:T(8,128)(2,1)S(1)}, bf16[3,8,64,64]{3,2,1,0:T(8,128)(2,1)S(1)}, bf16[8,256,128]{2,1,0:T(8,128)(2,1)S(1)}) custom-call(bf16[3,4,4096]{2,1,0:T(4,128)(2,1)S(1)} %broadcast_select_fusion.refs_0_, bf16[3,4,4096]{2,1,0:T(4,128)(2,1)S(1)} %collective-permute-done.3.refs_1_), custom_call_target="tpu_custom_call" | custom-call | flops 2000000000 | bytes 5242880 | tf_op jit(solution)/shard_map/tables/pallas_call | solution.py:524
  21.4 3.3 %collective-permute-done.2.refs_0_ = bf16[3,4,4096]{2,1,0:T(4,128)(2,1)S(1)} collective-permute-done((bf16[3,4,4096]{2,1,0:T(4,128)(2,1)S(1)}, bf16[3,4,4096]{2,1,0:T(4,128)(2,1)S(1)}, u32[]{:S(2)}, u32[]{:S(2)}) %collective-permute-start.2) | collective-permute-done | bytes 98336 | tf_op jit(solution)/shard_map/ppermute | solution.py:570
  24.7 2.1 %collective-permute-done.4.refs_1_ = bf16[3,4,4096]{2,1,0:T(4,128)(2,1)S(1)} collective-permute-done((bf16[3,4,4096]{2,1,0:T(4,128)(2,1)S(1)}, bf16[3,4,4096]{2,1,0:T(4,128)(2,1)S(1)}, u32[]{:S(2)}, u32[]{:S(2)}) %collective-permute-start.4) | collective-permute-done | bytes 98336 | tf_op jit(solution)/shard_map/ppermute | solution.py:570
  26.8 2.0 %tables.3 = (bf16[16,64,256]{2,1,0:T(8,128)(2,1)S(1)}, bf16[3,16,64,64]{3,2,1,0:T(8,128)(2,1)S(1)}, bf16[3,16,64,64]{3,2,1,0:T(8,128)(2,1)S(1)}, bf16[16,256,128]{2,1,0:T(8,128)(2,1)S(1)}) custom-call(bf16[3,4,4096]{2,1,0:T(4,128)(2,1)S(1)} %collective-permute-done.2.refs_0_, bf16[3,4,4096]{2,1,0:T(4,128)(2,1)S(1)} %collective-permute-done.4.refs_1_, ...), custom_call_target="tpu_custom_call" | custom-call | flops 2000000000 | bytes 5242880 | tf_op jit(solution)/shard_map/tables/pallas_call | solution.py:524
  30.1 2.0 %home_forward.2.refs_4_ = f32[3,16,64,128]{3,2,1,0:T(8,128)S(1)} custom-call(f32[3,17,32,128]{3,2,1,0:T(8,128)S(1)} %home_sums.2.sums, bf16[3,16,32,128]{3,2,1,0:T(8,128)(2,1)S(1)} %bitcast.20, bf16[16,64,256]{2,1,0:T(8,128)(2,1)S(1)} %get-tuple-element.77.first_t.refs_5_, bf16[3,16,64,64]{3,2,1,0:T(8,128)(2,1)S(1)} %get-tuple-element.78.left.refs_6_), custom_call_target="tpu_custom_call" | custom-call | flops 2000000000 | bytes 4194304 | tf_op jit(solution)/shard_map/home_forward/pallas_call | solution.py:524
  32.7 6.1 %forward.2 = (bf16[3,16,64,128]{3,2,1,0:T(8,128)(2,1)S(1)}, bf16[48,3,64,256]{3,2,1,0:T(8,128)(2,1)S(1)}) custom-call(s32[8,256]{1,0:T(8,128)S(1)} %get-tuple-element.74.plan, f32[3,128]{1,0:T(4,128)S(1)} %get-tuple-element.75.amps, bf16[33,32,128]{2,1,0:T(8,128)(2,1)S(1)} %collective-permute-done.5.refs_0_, ...), custom_call_target="tpu_custom_call" | custom-call | flops 3000000000 | bytes 8388608 | tf_op jit(solution)/shard_map/forward/pallas_call | solution.py:524
  38.9 6.3 %backward.2 = (bf16[65,32,128]{2,1,0:T(8,128)(2,1)S(1)}, bf16[65,32,128]{2,1,0:T(8,128)(2,1)S(1)}) custom-call(s32[8,256]{1,0:T(8,128)S(1)} %get-tuple-element.74.plan, f32[3,128]{1,0:T(4,128)S(1)} %get-tuple-element.75.amps, bf16[3,16,64,128]{3,2,1,0:T(8,128)(2,1)S(1)} %get-tuple-element.79.refs_0_.residual, ...), custom_call_target="tpu_custom_call" | custom-call | flops 3000000000 | bytes 8388608 | tf_op jit(solution)/shard_map/backward/pallas_call | solution.py:524
  47.8 4.1 %collective-permute-start.12 = (bf16[33,32,128]{2,1,0:T(8,128)(2,1)S(1)}, bf16[33,32,128]{2,1,0:T(8,128)(2,1)S(1)}, u32[]{:S(2)}, u32[]{:S(2)}) collective-permute-start(bf16[33,32,128]{2,1,0:T(8,128)(2,1)S(1)} %get-tuple-element.91), channel_id=1, source_target_pairs={{1,3},{2,0},{3,5},{4,2},{5,7},{6,4},{9,11},{10,8},{11,13},{12,10},... | collective-permute-start | bytes 811016 | tf_op jit(solution)/shard_map/ppermute | solution.py:550
  52.1 4.5 %home_gather.2 = (f32[128,32,128]{2,1,0:T(8,128)S(1)}, f32[6,128]{1,0:T(8,128)S(1)}) custom-call(s32[5,1,128]{2,1,0:T(1,128)S(1)} %bitcast.25, f32[6,128]{1,0:T(8,128)S(1)} %get-tuple-element.61.amps, f32[1,128]{1,0:T(1,128)S(1)} %bitcast.30, bf16[128,32,128]{2,1,0:T(8,128)(2,1)S(1)} %bitcast.19, bf16[3,17,32,128]{3,2,1,0:T(8,128)(2,1)S(1)} %home_slots.2.back, ...), custom_call_target="tpu_custom_call" | custom-call | bytes 4194304 | tf_op jit(solution)/shard_map/home_gather/pallas_call | solution.py:524
  61.5 1.9 %update.2 = (f32[128,32,128]{2,1,0:T(8,128)S(1)}, f32[6,128]{1,0:T(8,128)S(1)}, f32[6,128]{1,0:T(8,128)S(1)}, bf16[33,32,128]{2,1,0:T(8,128)(2,1)S(1)}, bf16[33,32,128]{2,1,0:T(8,128)(2,1)S(1)}) custom-call(s32[8,128]{1,0:T(8,128)S(1)} %get-tuple-element.58.places, f32[1,128]{1,0:T(1,128)S(1)} %bitcast.31, s32[5,1,128]{2,1,0:T(1,128)S(1)} %bitcast.26, ...), custom_call_target="tpu_custom_call" | custom-call | bytes 3145728 | tf_op jit(solution)/shard_map/update/pallas_call | solution.py:524
  63.4 4.1 %collective-permute-start.16 = (bf16[33,32,128]{2,1,0:T(8,128)(2,1)S(1)}, bf16[33,32,128]{2,1,0:T(8,128)(2,1)S(1)}, u32[]{:S(2)}, u32[]{:S(2)}) collective-permute-start(bf16[33,32,128]{2,1,0:T(8,128)(2,1)S(1)} %get-tuple-element.98), channel_id=1, source_target_pairs={{0,2},{2,4},{3,1},{4,6},{5,3},{7,5},{8,10},{10,12},{11,9},{12,14},... | collective-permute-start | bytes 811016 | tf_op jit(solution)/shard_map/ppermute | solution.py:550
  68.5 1.8 %home_sums.3.sums = f32[3,17,32,128]{3,2,1,0:T(8,128)S(1)} custom-call(s32[5,1,128]{2,1,0:T(1,128)S(1)} %bitcast.27, f32[6,128]{1,0:T(8,128)S(1)} %get-tuple-element.94.amps, f32[128,32,128]{2,1,0:T(8,128)S(1)} %get-tuple-element.95.morph), custom_call_target="tpu_custom_call" | custom-call | bytes 4194304 | tf_op jit(solution)/shard_map/home_sums/pallas_call | solution.py:524
  70.3 2.0 %home_forward.3.refs_4_ = f32[3,16,64,128]{3,2,1,0:T(8,128)S(1)} custom-call(f32[3,17,32,128]{3,2,1,0:T(8,128)S(1)} %home_sums.3.sums, bf16[3,16,32,128]{3,2,1,0:T(8,128)(2,1)S(1)} %bitcast.21, bf16[16,64,256]{2,1,0:T(8,128)(2,1)S(1)} %get-tuple-element.77.first_t.refs_5_, bf16[3,16,64,64]{3,2,1,0:T(8,128)(2,1)S(1)} %get-tuple-element.78.left.refs_6_), custom_call_target="tpu_custom_call" | custom-call | flops 2000000000 | bytes 4194304 | tf_op jit(solution)/shard_map/home_forward/pallas_call | solution.py:524
  73.5 2.4 %collective-permute-done.15.refs_0_ = bf16[33,32,128]{2,1,0:T(8,128)(2,1)S(1)} collective-permute-done((bf16[33,32,128]{2,1,0:T(8,128)(2,1)S(1)}, bf16[33,32,128]{2,1,0:T(8,128)(2,1)S(1)}, u32[]{:S(2)}, u32[]{:S(2)}) %collective-permute-start.15) | collective-permute-done | bytes 270368 | tf_op jit(solution)/shard_map/ppermute | solution.py:550
  78.0 6.1 %forward.3 = (bf16[3,16,64,128]{3,2,1,0:T(8,128)(2,1)S(1)}, bf16[48,3,64,256]{3,2,1,0:T(8,128)(2,1)S(1)}) custom-call(s32[8,256]{1,0:T(8,128)S(1)} %get-tuple-element.74.plan, f32[3,128]{1,0:T(4,128)S(1)} %order.3.amps, bf16[33,32,128]{2,1,0:T(8,128)(2,1)S(1)} %collective-permute-done.15.refs_0_, bf16[33,32,128]{2,1,0:T(8,128)(2,1)S(1)} %collective-permute-done.16.refs_1_, ...), custom_call_target="tpu_custom_call" | custom-call | flops 3000000000 | bytes 8388608 | tf_op jit(solution)/shard_map/forward/pallas_call | solution.py:524
  84.2 6.5 %backward.3 = (bf16[65,32,128]{2,1,0:T(8,128)(2,1)S(1)}, bf16[65,32,128]{2,1,0:T(8,128)(2,1)S(1)}) custom-call(s32[8,256]{1,0:T(8,128)S(1)} %get-tuple-element.74.plan, f32[3,128]{1,0:T(4,128)S(1)} %order.3.amps, bf16[3,16,64,128]{3,2,1,0:T(8,128)(2,1)S(1)} %get-tuple-element.100.refs_0_.residual, bf16[48,3,64,256]{3,2,1,0:T(8,128)(2,1)S(1)} %get-tuple-element.101.refs_1_, ...), custom_call_target="tpu_custom_call" | custom-call | flops 3000000000 | bytes 8388608 | tf_op jit(solution)/shard_map/backward/pallas_call | solution.py:524
  93.1 2.9 %collective-permute-start.22 = (bf16[33,32,128]{2,1,0:T(8,128)(2,1)S(1)}, bf16[33,32,128]{2,1,0:T(8,128)(2,1)S(1)}, u32[]{:S(2)}, u32[]{:S(2)}) collective-permute-start(bf16[33,32,128]{2,1,0:T(8,128)(2,1)S(1)} %get-tuple-element.110), channel_id=1, source_target_pairs={{1,3},{2,0},{3,5},{4,2},{5,7},{6,4},{9,11},{10,8},{11,13},{12,10},... | collective-permute-start | bytes 811016 | tf_op jit(solution)/shard_map/ppermute | solution.py:550
  97.5 3.0 %home_gather.3 = (f32[128,16,128]{2,1,0:T(8,128)S(1)}, f32[3,128]{1,0:T(4,128)S(1)}) custom-call(s32[5,1,128]{2,1,0:T(1,128)S(1)} %bitcast.28, f32[6,128]{1,0:T(8,128)S(1)} %get-tuple-element.94.amps, f32[1,128]{1,0:T(1,128)S(1)} %bitcast.32, f32[128,32,128]{2,1,0:T(8,128)S(1)} %get-tuple-element.95.morph, bf16[3,17,32,128]{3,2,1,0:T(8,128)(2,1)S(1)} %home_slots.3.back, ...), custom_call_target="tpu_custom_call" | custom-call | bytes 4194304 | tf_op jit(solution)/shard_map/home_gather/pallas_call | solution.py:524
  100.6 3.3 %collective-permute-done.22.refs_1_ = bf16[33,32,128]{2,1,0:T(8,128)(2,1)S(1)} collective-permute-done((bf16[33,32,128]{2,1,0:T(8,128)(2,1)S(1)}, bf16[33,32,128]{2,1,0:T(8,128)(2,1)S(1)}, u32[]{:S(2)}, u32[]{:S(2)}) %collective-permute-start.22) | collective-permute-done | bytes 270368 | tf_op jit(solution)/shard_map/ppermute | solution.py:550
  103.9 1.6 %collective-permute-done.21.refs_0_ = bf16[33,32,128]{2,1,0:T(8,128)(2,1)S(1)} collective-permute-done((bf16[33,32,128]{2,1,0:T(8,128)(2,1)S(1)}, bf16[33,32,128]{2,1,0:T(8,128)(2,1)S(1)}, u32[]{:S(2)}, u32[]{:S(2)}) %collective-permute-start.21) | collective-permute-done | bytes 270368 | tf_op jit(solution)/shard_map/ppermute | solution.py:550
  107.4 3.1 %update.3 = (f32[128,2048]{1,0:T(8,128)}, f32[3,1,128]{2,1,0:T(1,128)}) custom-call(s32[8,128]{1,0:T(8,128)S(1)} %get-tuple-element.58.places, f32[1,128]{1,0:T(1,128)S(1)} %bitcast.33, s32[5,1,128]{2,1,0:T(1,128)S(1)} %bitcast.29, f32[1,128]{1,0:T(1,128)S(1)} %bitcast.35, bf16[4,128,128]{2,1,0:T(8,128)(2,1)S(1)} %get-tuple-element.59.hots, ...), custom_call_target="tpu_custom_call" | custom-call | bytes 3145728 | tf_op jit(solution)/shard_map/update/pallas_call | solution.py:524
  (66 shorter events, 29.1 us)
Async XLA Ops:
  1.8 10.7 %collective-permute-start.1 = (bf16[3,4,4096]{2,1,0:T(4,128)(2,1)S(1)}, bf16[3,4,4096]{2,1,0:T(4,128)(2,1)S(1)}, u32[]{:S(2)}, u32[]{:S(2)}) collective-permute-start(bf16[3,4,4096]{2,1,0:T(4,128)(2,1)S(1)} %slice_select_fusion), channel_id=1, source_target_pairs={{0,16},{8,24},{1,17},{9,25},{2,18},{10,26},{3,19},{11,27},{4,20},{... | collective-permute-start | bytes 294920 | tf_op jit(solution)/shard_map/ppermute | solution.py:564
  6.0 3.5 %collective-permute-start = (f32[3,1,128]{2,1,0:T(1,128)}, f32[3,1,128]{2,1,0:T(1,128)S(1)}, u32[]{:S(2)}, u32[]{:S(2)}) collective-permute-start(f32[3,1,128]{2,1,0:T(1,128)} %bitcast.36), channel_id=1, source_target_pairs={{0,1},{1,0},{2,3},{3,2},{4,5},{5,4},{6,7},{7,6},{8,9},{9,8},{10,11... | collective-permute-start | bytes 4616 | tf_op jit(solution)/shard_map/ppermute | solution.py:554
  12.5 5.7 %collective-permute-start.3 = (bf16[3,4,4096]{2,1,0:T(4,128)(2,1)S(1)}, bf16[3,4,4096]{2,1,0:T(4,128)(2,1)S(1)}, u32[]{:S(2)}, u32[]{:S(2)}) collective-permute-start(bf16[3,4,4096]{2,1,0:T(4,128)(2,1)S(1)} %broadcast_select_fusion.refs_0_), channel_id=1, source_target_pairs={{0,8},{8,0},{16,24},{24,16},{1,9},{9,1},{17,25},{25,17},{2,10},{10... | collective-permute-start | bytes 294920 | tf_op jit(solution)/shard_map/ppermute | solution.py:568
  13.9 14.9 %collective-permute-start.6 = (bf16[33,32,128]{2,1,0:T(8,128)(2,1)S(1)}, bf16[33,32,128]{2,1,0:T(8,128)(2,1)S(1)}, u32[]{:S(2)}, u32[]{:S(2)}) collective-permute-start(bf16[33,32,128]{2,1,0:T(8,128)(2,1)S(1)} %get-tuple-element.71), channel_id=1, source_target_pairs={{0,2},{2,4},{3,1},{4,6},{5,3},{7,5},{8,10},{10,12},{11,9},{12,14},... | collective-permute-start | bytes 811016 | tf_op jit(solution)/shard_map/ppermute | solution.py:550
  17.0 7.6 %collective-permute-start.2 = (bf16[3,4,4096]{2,1,0:T(4,128)(2,1)S(1)}, bf16[3,4,4096]{2,1,0:T(4,128)(2,1)S(1)}, u32[]{:S(2)}, u32[]{:S(2)}) collective-permute-start(bf16[3,4,4096]{2,1,0:T(4,128)(2,1)S(1)} %broadcast_select_fusion.refs_0_), channel_id=1, source_target_pairs={{0,2},{2,0},{4,6},{6,4},{1,3},{3,1},{5,7},{7,5},{8,10},{10,8},{12,... | collective-permute-start | bytes 294920 | tf_op jit(solution)/shard_map/ppermute | solution.py:570
  17.3 11.4 %collective-permute-start.5 = (bf16[33,32,128]{2,1,0:T(8,128)(2,1)S(1)}, bf16[33,32,128]{2,1,0:T(8,128)(2,1)S(1)}, u32[]{:S(2)}, u32[]{:S(2)}) collective-permute-start(bf16[33,32,128]{2,1,0:T(8,128)(2,1)S(1)} %get-tuple-element.70), channel_id=1, source_target_pairs={{0,8},{1,25},{2,10},{3,27},{4,12},{5,29},{6,14},{7,31},{8,16},{9,1... | collective-permute-start | bytes 811016 | tf_op jit(solution)/shard_map/ppermute | solution.py:550
  18.2 8.5 %collective-permute-start.4 = (bf16[3,4,4096]{2,1,0:T(4,128)(2,1)S(1)}, bf16[3,4,4096]{2,1,0:T(4,128)(2,1)S(1)}, u32[]{:S(2)}, u32[]{:S(2)}) collective-permute-start(bf16[3,4,4096]{2,1,0:T(4,128)(2,1)S(1)} %collective-permute-done.3.refs_1_), channel_id=1, source_target_pairs={{0,2},{2,0},{4,6},{6,4},{1,3},{3,1},{5,7},{7,5},{8,10},{10,8},{12,... | collective-permute-start | bytes 294920 | tf_op jit(solution)/shard_map/ppermute | solution.py:570
  28.8 3.4 %collective-permute-start.7 = (bf16[33,32,128]{2,1,0:T(8,128)(2,1)S(1)}, bf16[33,32,128]{2,1,0:T(8,128)(2,1)S(1)}, u32[]{:S(2)}, u32[]{:S(2)}) collective-permute-start(bf16[33,32,128]{2,1,0:T(8,128)(2,1)S(1)} %collective-permute-done.5.refs_0_), channel_id=1, source_target_pairs={{0,1},{1,0},{2,3},{3,2},{4,5},{5,4},{6,7},{7,6},{8,9},{9,8},{10,11... | collective-permute-start | bytes 811016 | tf_op jit(solution)/shard_map/ppermute | solution.py:554
  30.0 2.2 %collective-permute-start.8 = (bf16[33,32,128]{2,1,0:T(8,128)(2,1)S(1)}, bf16[33,32,128]{2,1,0:T(8,128)(2,1)S(1)}, u32[]{:S(2)}, u32[]{:S(2)}) collective-permute-start(bf16[33,32,128]{2,1,0:T(8,128)(2,1)S(1)} %collective-permute-done.6.refs_1_), channel_id=1, source_target_pairs={{0,1},{1,0},{2,3},{3,2},{4,5},{5,4},{6,7},{7,6},{8,9},{9,8},{10,11... | collective-permute-start | bytes 811016 | tf_op jit(solution)/shard_map/ppermute | solution.py:554
  45.3 2.0 %collective-permute-start.9 = (bf16[65,32,128]{2,1,0:T(8,128)(2,1)S(1)}, bf16[65,32,128]{2,1,0:T(8,128)(2,1)S(1)}, u32[]{:S(2)}, u32[]{:S(2)}) collective-permute-start(bf16[65,32,128]{2,1,0:T(8,128)(2,1)S(1)} %get-tuple-element.83), channel_id=1, source_target_pairs={{0,1},{1,0},{2,3},{3,2},{4,5},{5,4},{6,7},{7,6},{8,9},{9,8},{10,11... | collective-permute-start | bytes 1597448 | tf_op jit(solution)/shard_map/ppermute | solution.py:554
  47.3 4.8 %collective-permute-start.10 = (bf16[3,17,32,128]{3,2,1,0:T(8,128)(2,1)S(1)}, bf16[3,17,32,128]{3,2,1,0:T(8,128)(2,1)S(1)}, u32[]{:S(2)}, u32[]{:S(2)}) collective-permute-start(bf16[3,17,32,128]{3,2,1,0:T(8,128)(2,1)S(1)} %home_slots.2.back), channel_id=1, source_target_pairs={{0,1},{1,0},{2,3},{3,2},{4,5},{5,4},{6,7},{7,6},{8,9},{9,8},{10,11... | collective-permute-start | bytes 1253384 | tf_op jit(solution)/shard_map/ppermute | solution.py:554
  47.8 10.4 %collective-permute-start.12 = (bf16[33,32,128]{2,1,0:T(8,128)(2,1)S(1)}, bf16[33,32,128]{2,1,0:T(8,128)(2,1)S(1)}, u32[]{:S(2)}, u32[]{:S(2)}) collective-permute-start(bf16[33,32,128]{2,1,0:T(8,128)(2,1)S(1)} %get-tuple-element.91), channel_id=1, source_target_pairs={{1,3},{2,0},{3,5},{4,2},{5,7},{6,4},{9,11},{10,8},{11,13},{12,10},... | collective-permute-start | bytes 811016 | tf_op jit(solution)/shard_map/ppermute | solution.py:550
  51.9 7.6 %collective-permute-start.11 = (bf16[33,32,128]{2,1,0:T(8,128)(2,1)S(1)}, bf16[33,32,128]{2,1,0:T(8,128)(2,1)S(1)}, u32[]{:S(2)}, u32[]{:S(2)}) collective-permute-start(bf16[33,32,128]{2,1,0:T(8,128)(2,1)S(1)} %get-tuple-element.89), channel_id=1, source_target_pairs={{0,24},{1,9},{2,26},{3,11},{4,28},{5,13},{6,30},{7,15},{8,0},{9,17... | collective-permute-start | bytes 811016 | tf_op jit(solution)/shard_map/ppermute | solution.py:550
  59.5 1.5 %collective-permute-start.13 = (bf16[33,32,128]{2,1,0:T(8,128)(2,1)S(1)}, bf16[33,32,128]{2,1,0:T(8,128)(2,1)S(1)}, u32[]{:S(2)}, u32[]{:S(2)}) collective-permute-start(bf16[33,32,128]{2,1,0:T(8,128)(2,1)S(1)} %collective-permute-done.11.refs_0_), channel_id=1, source_target_pairs={{0,1},{1,0},{2,3},{3,2},{4,5},{5,4},{6,7},{7,6},{8,9},{9,8},{10,11... | collective-permute-start | bytes 811016 | tf_op jit(solution)/shard_map/ppermute | solution.py:554
  59.5 1.9 %collective-permute-start.14 = (bf16[33,32,128]{2,1,0:T(8,128)(2,1)S(1)}, bf16[33,32,128]{2,1,0:T(8,128)(2,1)S(1)}, u32[]{:S(2)}, u32[]{:S(2)}) collective-permute-start(bf16[33,32,128]{2,1,0:T(8,128)(2,1)S(1)} %collective-permute-done.12.refs_1_), channel_id=1, source_target_pairs={{0,1},{1,0},{2,3},{3,2},{4,5},{5,4},{6,7},{7,6},{8,9},{9,8},{10,11... | collective-permute-start | bytes 811016 | tf_op jit(solution)/shard_map/ppermute | solution.py:554
  63.4 10.1 %collective-permute-start.16 = (bf16[33,32,128]{2,1,0:T(8,128)(2,1)S(1)}, bf16[33,32,128]{2,1,0:T(8,128)(2,1)S(1)}, u32[]{:S(2)}, u32[]{:S(2)}) collective-permute-start(bf16[33,32,128]{2,1,0:T(8,128)(2,1)S(1)} %get-tuple-element.98), channel_id=1, source_target_pairs={{0,2},{2,4},{3,1},{4,6},{5,3},{7,5},{8,10},{10,12},{11,9},{12,14},... | collective-permute-start | bytes 811016 | tf_op jit(solution)/shard_map/ppermute | solution.py:550
  67.4 8.4 %collective-permute-start.15 = (bf16[33,32,128]{2,1,0:T(8,128)(2,1)S(1)}, bf16[33,32,128]{2,1,0:T(8,128)(2,1)S(1)}, u32[]{:S(2)}, u32[]{:S(2)}) collective-permute-start(bf16[33,32,128]{2,1,0:T(8,128)(2,1)S(1)} %get-tuple-element.96), channel_id=1, source_target_pairs={{0,8},{1,25},{2,10},{3,27},{4,12},{5,29},{6,14},{7,31},{8,16},{9,1... | collective-permute-start | bytes 811016 | tf_op jit(solution)/shard_map/ppermute | solution.py:550
  75.9 1.7 %collective-permute-start.17 = (bf16[33,32,128]{2,1,0:T(8,128)(2,1)S(1)}, bf16[33,32,128]{2,1,0:T(8,128)(2,1)S(1)}, u32[]{:S(2)}, u32[]{:S(2)}) collective-permute-start(bf16[33,32,128]{2,1,0:T(8,128)(2,1)S(1)} %collective-permute-done.15.refs_0_), channel_id=1, source_target_pairs={{0,1},{1,0},{2,3},{3,2},{4,5},{5,4},{6,7},{7,6},{8,9},{9,8},{10,11... | collective-permute-start | bytes 811016 | tf_op jit(solution)/shard_map/ppermute | solution.py:554
  76.4 1.6 %collective-permute-start.18 = (bf16[33,32,128]{2,1,0:T(8,128)(2,1)S(1)}, bf16[33,32,128]{2,1,0:T(8,128)(2,1)S(1)}, u32[]{:S(2)}, u32[]{:S(2)}) collective-permute-start(bf16[33,32,128]{2,1,0:T(8,128)(2,1)S(1)} %collective-permute-done.16.refs_1_), channel_id=1, source_target_pairs={{0,1},{1,0},{2,3},{3,2},{4,5},{5,4},{6,7},{7,6},{8,9},{9,8},{10,11... | collective-permute-start | bytes 811016 | tf_op jit(solution)/shard_map/ppermute | solution.py:554
  90.7 1.9 %collective-permute-start.19 = (bf16[65,32,128]{2,1,0:T(8,128)(2,1)S(1)}, bf16[65,32,128]{2,1,0:T(8,128)(2,1)S(1)}, u32[]{:S(2)}, u32[]{:S(2)}) collective-permute-start(bf16[65,32,128]{2,1,0:T(8,128)(2,1)S(1)} %get-tuple-element.102), channel_id=1, source_target_pairs={{0,1},{1,0},{2,3},{3,2},{4,5},{5,4},{6,7},{7,6},{8,9},{9,8},{10,11... | collective-permute-start | bytes 1597448 | tf_op jit(solution)/shard_map/ppermute | solution.py:554
  92.6 4.9 %collective-permute-start.20 = (bf16[3,17,32,128]{3,2,1,0:T(8,128)(2,1)S(1)}, bf16[3,17,32,128]{3,2,1,0:T(8,128)(2,1)S(1)}, u32[]{:S(2)}, u32[]{:S(2)}) collective-permute-start(bf16[3,17,32,128]{3,2,1,0:T(8,128)(2,1)S(1)} %home_slots.3.back), channel_id=1, source_target_pairs={{0,1},{1,0},{2,3},{3,2},{4,5},{5,4},{6,7},{7,6},{8,9},{9,8},{10,11... | collective-permute-start | bytes 1253384 | tf_op jit(solution)/shard_map/ppermute | solution.py:554
  93.1 10.8 %collective-permute-start.22 = (bf16[33,32,128]{2,1,0:T(8,128)(2,1)S(1)}, bf16[33,32,128]{2,1,0:T(8,128)(2,1)S(1)}, u32[]{:S(2)}, u32[]{:S(2)}) collective-permute-start(bf16[33,32,128]{2,1,0:T(8,128)(2,1)S(1)} %get-tuple-element.110), channel_id=1, source_target_pairs={{1,3},{2,0},{3,5},{4,2},{5,7},{6,4},{9,11},{10,8},{11,13},{12,10},... | collective-permute-start | bytes 811016 | tf_op jit(solution)/shard_map/ppermute | solution.py:550
  96.0 9.5 %collective-permute-start.21 = (bf16[33,32,128]{2,1,0:T(8,128)(2,1)S(1)}, bf16[33,32,128]{2,1,0:T(8,128)(2,1)S(1)}, u32[]{:S(2)}, u32[]{:S(2)}) collective-permute-start(bf16[33,32,128]{2,1,0:T(8,128)(2,1)S(1)} %get-tuple-element.108), channel_id=1, source_target_pairs={{0,24},{1,9},{2,26},{3,11},{4,28},{5,13},{6,30},{7,15},{8,0},{9,17... | collective-permute-start | bytes 811016 | tf_op jit(solution)/shard_map/ppermute | solution.py:550
  105.5 1.9 %collective-permute-start.24 = (bf16[33,32,128]{2,1,0:T(8,128)(2,1)S(1)}, bf16[33,32,128]{2,1,0:T(8,128)(2,1)S(1)}, u32[]{:S(2)}, u32[]{:S(2)}) collective-permute-start(bf16[33,32,128]{2,1,0:T(8,128)(2,1)S(1)} %collective-permute-done.22.refs_1_), channel_id=1, source_target_pairs={{0,1},{1,0},{2,3},{3,2},{4,5},{5,4},{6,7},{7,6},{8,9},{9,8},{10,11... | collective-permute-start | bytes 811016 | tf_op jit(solution)/shard_map/ppermute | solution.py:554
  (8 other events, 47.5 us)

commit v3 on v2

--- a/solution.py
+++ b/solution.py
@@ -163,7 +163,7 @@
 
 
 def quarter_start(quarter, held):
-    parity, line = lax.axis_index("ra") % 2, lax.axis_index("dec") % 2
+    parity, line = lax.axis_index("ra") % 2, lax.axis_index("dec") // (lax.axis_size("dec") // 2)
     shard = parity if quarter % 2 == 0 else 1 - parity
     half = line if quarter < 2 else 1 - line
     return (2 * shard + half) * held
@@ -192,9 +192,9 @@
     even = (col == 2 * (row % ROWS) + row // ROWS).astype(F32).astype(BF16)
     even_t = (row == 2 * (col % ROWS) + col // ROWS).astype(F32).astype(BF16)
     rest = [jnp.zeros((SIDE * (4 - bands), SIDE), BF16)] if bands < 4 else []
-    for turn, start in enumerate(starts):
-
-        def step(place, carry, turn=turn, start=start):
+
+    def step(place, carry):
+        for turn, start in enumerate(starts):
             k = start + place
             at = pl.multiple_of((turn * held + place) * ROWS, ROWS)
             parts = [twofold(packed[band, pl.ds(at, ROWS), :]).astype(BF16) for band in range(bands)]
@@ -203,16 +203,16 @@
             for band, part in enumerate(parts):
                 rows = slice(band * SIDE, (band + 1) * SIDE)
                 left[band, k] = lefts[rows]
-                left_t[band, k] = dot_nt(eye, lefts[rows]).astype(BF16)
+                left_t[band, k] = dot_nt(even, part[:, :SIDE]).astype(BF16)
                 both = dot(even_t, part).astype(BF16)
                 right[k, rows, :] = both
                 natural.append(both[:, :SIDE])
             if rest:
                 right[k, bands * SIDE :, :] = jnp.zeros((SIDE * (4 - bands), LANES), BF16)
             first_t[k] = dot_nt(eye, jnp.concatenate(natural + rest, axis=0)).astype(BF16)
-            return carry
-
-        lax.fori_loop(0, held, step, 0, unroll=min(held, 4))
+        return carry
+
+    lax.fori_loop(0, held, step, 0, unroll=min(held, 4))
 
 
 def make_tables(shards, bands, earlier=()):
@@ -558,9 +558,9 @@
     bands, held = psf.shape[:2]
     lines = lax.axis_size("dec")
     if lax.axis_size("ra") == 4 and 2 * held == num_slots and held % 2 == 0 and lines % 2 == 0:
-        across = [(i, i + 1 - 2 * (i % 2)) for i in range(lines)]
+        across = [(i, (i + lines // 2) % lines) for i in range(lines)]
         along = [(0, 1), (1, 0), (2, 3), (3, 2)]
-        mine = jnp.where(lax.axis_index("dec") % 2 == 0, psf[:, : held // 2], psf[:, held // 2 :])
+        mine = jnp.where(lax.axis_index("dec") < lines // 2, psf[:, : held // 2], psf[:, held // 2 :])
         far = lax.ppermute(mine, "ra", [(0, 2), (1, 3)])
         far, sums = lax.optimization_barrier((far, sums))
         here = jnp.where(lax.axis_index("ra") < 2, mine, far)

time: 112 us -> 115 us (1.027)
  Pallas kernels: 53.4 us -> 59 us
  starting transfers between devices: 30.3 us -> 24.9 us
  waiting for transfers between devices: 22.5 us -> 25 us
    ppermute x8, starting transfers between devices: 17.8 us -> 10.3 us  [stepped(): return lax.ppermute(value, ('ra', 'dec', 'band'), pairs)]
    pallas_call x22, Pallas kernels: 53.4 us -> 59 us  [call(): pl.pallas_call(body, out_shape=[jax.ShapeDtypeStruct(shape, dtype) for sh...]
    ppermute x8, waiting for transfers between devices: 11.4 us -> 14.4 us  [stepped(): return lax.ppermute(value, ('ra', 'dec', 'band'), pairs)]
    ppermute x1, waiting for transfers between devices: 3.28 us -> 0.76 us  [all_tables(): lax.ppermute(here, 'dec', across)]
    ppermute x13, starting transfers between devices: 5.44 us -> 7.53 us  [swapped(): return lax.ppermute(value, 'band', [(0, 1), (1, 0)])]
    ppermute x1, waiting for transfers between devices: 2.11 us -> 4.15 us  [all_tables(): lax.ppermute(near, 'dec', across)]
where the time goes in v3:
time: 115 us; the launch traced here: 113 us
  Pallas kernels  59 us (51%)
  waiting for transfers between devices  25 us (22%)
  starting transfers between devices  24.9 us (22%)
  local copies, waits for them, and re-layouts  2.29 us (2%)
  other arithmetic  1.21 us (1%)
    pallas_call x22, Pallas kernels, call(): pl.pallas_call(body, out_shape=[jax.ShapeDtypeStruct(shape, dtype) for sh...  59 us
    ppermute x8, waiting for transfers between devices, stepped(): return lax.ppermute(value, ('ra', 'dec', 'band'), pairs)  14.4 us
    ppermute x8, starting transfers between devices, stepped(): return lax.ppermute(value, ('ra', 'dec', 'band'), pairs)  10.3 us
    ppermute x13, starting transfers between devices, swapped(): return lax.ppermute(value, 'band', [(0, 1), (1, 0)])  7.53 us
    ppermute x13, waiting for transfers between devices, swapped(): return lax.ppermute(value, 'band', [(0, 1), (1, 0)])  5.7 us
    ppermute x1, starting transfers between devices, all_tables(): far = lax.ppermute(mine, 'ra', [(0, 2), (1, 3)])  4.22 us
    ppermute x1, waiting for transfers between devices, all_tables(): lax.ppermute(near, 'dec', across)  4.15 us
  transfers between devices with their start and end apart: 25, of which 16 were waited for; matrix products, arithmetic and copies ran while one was open for 1% of the time, Pallas kernels for 20%

profile of v3, /device:TPU:5, one launch (start us, length us, event | category | flops | bytes accessed | tf_op | source)
XLA Modules:
  0.0 113.4 jit_solution(6163578867821094700)
XLA Ops:
  1.8 4.2 %collective-permute-start.1 = (bf16[3,4,4096]{2,1,0:T(4,128)(2,1)S(1)}, bf16[3,4,4096]{2,1,0:T(4,128)(2,1)S(1)}, u32[]{:S(2)}, u32[]{:S(2)}) collective-permute-start(bf16[3,4,4096]{2,1,0:T(4,128)(2,1)S(1)} %slice_select_fusion), channel_id=1, source_target_pairs={{0,16},{8,24},{1,17},{9,25},{2,18},{10,26},{3,19},{11,27},{4,20},{... | collective-permute-start | bytes 294920 | tf_op jit(solution)/shard_map/ppermute | solution.py:564
  10.6 1.9 %home_sums.2.sums = f32[3,17,32,128]{3,2,1,0:T(8,128)S(1)} custom-call(s32[5,1,128]{2,1,0:T(1,128)S(1)} %bitcast.24, f32[6,128]{1,0:T(8,128)S(1)} %get-tuple-element.61.amps, bf16[128,32,128]{2,1,0:T(8,128)(2,1)S(1)} %bitcast.18), custom_call_target="tpu_custom_call" | custom-call | bytes 4194304 | tf_op jit(solution)/shard_map/home_sums/pallas_call | solution.py:524
  13.9 3.1 %collective-permute-start.6 = (bf16[33,32,128]{2,1,0:T(8,128)(2,1)S(1)}, bf16[33,32,128]{2,1,0:T(8,128)(2,1)S(1)}, u32[]{:S(2)}, u32[]{:S(2)}) collective-permute-start(bf16[33,32,128]{2,1,0:T(8,128)(2,1)S(1)} %get-tuple-element.71), channel_id=1, source_target_pairs={{0,2},{2,4},{3,1},{4,6},{5,3},{7,5},{8,10},{10,12},{11,9},{12,14},... | collective-permute-start | bytes 811016 | tf_op jit(solution)/shard_map/ppermute | solution.py:550
  19.4 1.8 %tables.2 = (bf16[8,64,256]{2,1,0:T(8,128)(2,1)S(1)}, bf16[3,8,64,64]{3,2,1,0:T(8,128)(2,1)S(1)}, bf16[3,8,64,64]{3,2,1,0:T(8,128)(2,1)S(1)}, bf16[8,256,128]{2,1,0:T(8,128)(2,1)S(1)}) custom-call(bf16[3,4,4096]{2,1,0:T(4,128)(2,1)S(1)} %broadcast_select_fusion.refs_0_, bf16[3,4,4096]{2,1,0:T(4,128)(2,1)S(1)} %collective-permute-done.3.refs_1_), custom_call_target="tpu_custom_call" | custom-call | flops 2000000000 | bytes 5242880 | tf_op jit(solution)/shard_map/tables/pallas_call | solution.py:524
  21.9 4.2 %collective-permute-done.4.refs_1_ = bf16[3,4,4096]{2,1,0:T(4,128)(2,1)S(1)} collective-permute-done((bf16[3,4,4096]{2,1,0:T(4,128)(2,1)S(1)}, bf16[3,4,4096]{2,1,0:T(4,128)(2,1)S(1)}, u32[]{:S(2)}, u32[]{:S(2)}) %collective-permute-start.4) | collective-permute-done | bytes 98336 | tf_op jit(solution)/shard_map/ppermute | solution.py:570
  26.1 1.8 %tables.3 = (bf16[16,64,256]{2,1,0:T(8,128)(2,1)S(1)}, bf16[3,16,64,64]{3,2,1,0:T(8,128)(2,1)S(1)}, bf16[3,16,64,64]{3,2,1,0:T(8,128)(2,1)S(1)}, bf16[16,256,128]{2,1,0:T(8,128)(2,1)S(1)}) custom-call(bf16[3,4,4096]{2,1,0:T(4,128)(2,1)S(1)} %collective-permute-done.2.refs_0_, bf16[3,4,4096]{2,1,0:T(4,128)(2,1)S(1)} %collective-permute-done.4.refs_1_, ...), custom_call_target="tpu_custom_call" | custom-call | flops 2000000000 | bytes 5242880 | tf_op jit(solution)/shard_map/tables/pallas_call | solution.py:524
  29.4 2.0 %home_forward.2.refs_4_ = f32[3,16,64,128]{3,2,1,0:T(8,128)S(1)} custom-call(f32[3,17,32,128]{3,2,1,0:T(8,128)S(1)} %home_sums.2.sums, bf16[3,16,32,128]{3,2,1,0:T(8,128)(2,1)S(1)} %bitcast.20, bf16[16,64,256]{2,1,0:T(8,128)(2,1)S(1)} %get-tuple-element.77.first_t.refs_5_, bf16[3,16,64,64]{3,2,1,0:T(8,128)(2,1)S(1)} %get-tuple-element.78.left.refs_6_), custom_call_target="tpu_custom_call" | custom-call | flops 2000000000 | bytes 4194304 | tf_op jit(solution)/shard_map/home_forward/pallas_call | solution.py:524
  32.0 7.4 %forward.2 = (bf16[3,16,64,128]{3,2,1,0:T(8,128)(2,1)S(1)}, bf16[48,3,64,256]{3,2,1,0:T(8,128)(2,1)S(1)}) custom-call(s32[8,256]{1,0:T(8,128)S(1)} %get-tuple-element.74.plan, f32[3,128]{1,0:T(4,128)S(1)} %get-tuple-element.75.amps, bf16[33,32,128]{2,1,0:T(8,128)(2,1)S(1)} %collective-permute-done.5.refs_0_, ...), custom_call_target="tpu_custom_call" | custom-call | flops 3000000000 | bytes 8388608 | tf_op jit(solution)/shard_map/forward/pallas_call | solution.py:524
  39.4 7.8 %backward.2 = (bf16[65,32,128]{2,1,0:T(8,128)(2,1)S(1)}, bf16[65,32,128]{2,1,0:T(8,128)(2,1)S(1)}) custom-call(s32[8,256]{1,0:T(8,128)S(1)} %get-tuple-element.74.plan, f32[3,128]{1,0:T(4,128)S(1)} %get-tuple-element.75.amps, bf16[3,16,64,128]{3,2,1,0:T(8,128)(2,1)S(1)} %get-tuple-element.79.refs_0_.residual, ...), custom_call_target="tpu_custom_call" | custom-call | flops 3000000000 | bytes 8388608 | tf_op jit(solution)/shard_map/backward/pallas_call | solution.py:524
  49.8 1.9 %collective-permute-start.12 = (bf16[33,32,128]{2,1,0:T(8,128)(2,1)S(1)}, bf16[33,32,128]{2,1,0:T(8,128)(2,1)S(1)}, u32[]{:S(2)}, u32[]{:S(2)}) collective-permute-start(bf16[33,32,128]{2,1,0:T(8,128)(2,1)S(1)} %get-tuple-element.91), channel_id=1, source_target_pairs={{1,3},{2,0},{3,5},{4,2},{5,7},{6,4},{9,11},{10,8},{11,13},{12,10},... | collective-permute-start | bytes 811016 | tf_op jit(solution)/shard_map/ppermute | solution.py:550
  51.8 4.5 %home_gather.2 = (f32[128,32,128]{2,1,0:T(8,128)S(1)}, f32[6,128]{1,0:T(8,128)S(1)}) custom-call(s32[5,1,128]{2,1,0:T(1,128)S(1)} %bitcast.25, f32[6,128]{1,0:T(8,128)S(1)} %get-tuple-element.61.amps, f32[1,128]{1,0:T(1,128)S(1)} %bitcast.30, bf16[128,32,128]{2,1,0:T(8,128)(2,1)S(1)} %bitcast.19, bf16[3,17,32,128]{3,2,1,0:T(8,128)(2,1)S(1)} %home_slots.2.back, ...), custom_call_target="tpu_custom_call" | custom-call | bytes 4194304 | tf_op jit(solution)/shard_map/home_gather/pallas_call | solution.py:524
  57.9 3.7 %collective-permute-done.11.refs_0_ = bf16[33,32,128]{2,1,0:T(8,128)(2,1)S(1)} collective-permute-done((bf16[33,32,128]{2,1,0:T(8,128)(2,1)S(1)}, bf16[33,32,128]{2,1,0:T(8,128)(2,1)S(1)}, u32[]{:S(2)}, u32[]{:S(2)}) %collective-permute-start.11) | collective-permute-done | bytes 270368 | tf_op jit(solution)/shard_map/ppermute | solution.py:550
  63.6 2.0 %update.2 = (f32[128,32,128]{2,1,0:T(8,128)S(1)}, f32[6,128]{1,0:T(8,128)S(1)}, f32[6,128]{1,0:T(8,128)S(1)}, bf16[33,32,128]{2,1,0:T(8,128)(2,1)S(1)}, bf16[33,32,128]{2,1,0:T(8,128)(2,1)S(1)}) custom-call(s32[8,128]{1,0:T(8,128)S(1)} %get-tuple-element.58.places, f32[1,128]{1,0:T(1,128)S(1)} %bitcast.31, s32[5,1,128]{2,1,0:T(1,128)S(1)} %bitcast.26, ...), custom_call_target="tpu_custom_call" | custom-call | bytes 3145728 | tf_op jit(solution)/shard_map/update/pallas_call | solution.py:524
  65.6 1.9 %collective-permute-start.16 = (bf16[33,32,128]{2,1,0:T(8,128)(2,1)S(1)}, bf16[33,32,128]{2,1,0:T(8,128)(2,1)S(1)}, u32[]{:S(2)}, u32[]{:S(2)}) collective-permute-start(bf16[33,32,128]{2,1,0:T(8,128)(2,1)S(1)} %get-tuple-element.98), channel_id=1, source_target_pairs={{0,2},{2,4},{3,1},{4,6},{5,3},{7,5},{8,10},{10,12},{11,9},{12,14},... | collective-permute-start | bytes 811016 | tf_op jit(solution)/shard_map/ppermute | solution.py:550
  68.0 1.8 %home_sums.3.sums = f32[3,17,32,128]{3,2,1,0:T(8,128)S(1)} custom-call(s32[5,1,128]{2,1,0:T(1,128)S(1)} %bitcast.27, f32[6,128]{1,0:T(8,128)S(1)} %get-tuple-element.94.amps, f32[128,32,128]{2,1,0:T(8,128)S(1)} %get-tuple-element.95.morph), custom_call_target="tpu_custom_call" | custom-call | bytes 4194304 | tf_op jit(solution)/shard_map/home_sums/pallas_call | solution.py:524
  69.9 2.0 %home_forward.3.refs_4_ = f32[3,16,64,128]{3,2,1,0:T(8,128)S(1)} custom-call(f32[3,17,32,128]{3,2,1,0:T(8,128)S(1)} %home_sums.3.sums, bf16[3,16,32,128]{3,2,1,0:T(8,128)(2,1)S(1)} %bitcast.21, bf16[16,64,256]{2,1,0:T(8,128)(2,1)S(1)} %get-tuple-element.77.first_t.refs_5_, bf16[3,16,64,64]{3,2,1,0:T(8,128)(2,1)S(1)} %get-tuple-element.78.left.refs_6_), custom_call_target="tpu_custom_call" | custom-call | flops 2000000000 | bytes 4194304 | tf_op jit(solution)/shard_map/home_forward/pallas_call | solution.py:524
  74.3 2.5 %collective-permute-start.17 = (bf16[33,32,128]{2,1,0:T(8,128)(2,1)S(1)}, bf16[33,32,128]{2,1,0:T(8,128)(2,1)S(1)}, u32[]{:S(2)}, u32[]{:S(2)}) collective-permute-start(bf16[33,32,128]{2,1,0:T(8,128)(2,1)S(1)} %collective-permute-done.15.refs_0_), channel_id=1, source_target_pairs={{0,1},{1,0},{2,3},{3,2},{4,5},{5,4},{6,7},{7,6},{8,9},{9,8},{10,11... | collective-permute-start | bytes 811016 | tf_op jit(solution)/shard_map/ppermute | solution.py:554
  78.5 7.4 %forward.3 = (bf16[3,16,64,128]{3,2,1,0:T(8,128)(2,1)S(1)}, bf16[48,3,64,256]{3,2,1,0:T(8,128)(2,1)S(1)}) custom-call(s32[8,256]{1,0:T(8,128)S(1)} %get-tuple-element.74.plan, f32[3,128]{1,0:T(4,128)S(1)} %order.3.amps, bf16[33,32,128]{2,1,0:T(8,128)(2,1)S(1)} %collective-permute-done.15.refs_0_, bf16[33,32,128]{2,1,0:T(8,128)(2,1)S(1)} %collective-permute-done.16.refs_1_, ...), custom_call_target="tpu_custom_call" | custom-call | flops 3000000000 | bytes 8388608 | tf_op jit(solution)/shard_map/forward/pallas_call | solution.py:524
  85.9 8.1 %backward.3 = (bf16[65,32,128]{2,1,0:T(8,128)(2,1)S(1)}, bf16[65,32,128]{2,1,0:T(8,128)(2,1)S(1)}) custom-call(s32[8,256]{1,0:T(8,128)S(1)} %get-tuple-element.74.plan, f32[3,128]{1,0:T(4,128)S(1)} %order.3.amps, bf16[3,16,64,128]{3,2,1,0:T(8,128)(2,1)S(1)} %get-tuple-element.100.refs_0_.residual, bf16[48,3,64,256]{3,2,1,0:T(8,128)(2,1)S(1)} %get-tuple-element.101.refs_1_, ...), custom_call_target="tpu_custom_call" | custom-call | flops 3000000000 | bytes 8388608 | tf_op jit(solution)/shard_map/backward/pallas_call | solution.py:524
  96.4 1.9 %collective-permute-start.22 = (bf16[33,32,128]{2,1,0:T(8,128)(2,1)S(1)}, bf16[33,32,128]{2,1,0:T(8,128)(2,1)S(1)}, u32[]{:S(2)}, u32[]{:S(2)}) collective-permute-start(bf16[33,32,128]{2,1,0:T(8,128)(2,1)S(1)} %get-tuple-element.110), channel_id=1, source_target_pairs={{1,3},{2,0},{3,5},{4,2},{5,7},{6,4},{9,11},{10,8},{11,13},{12,10},... | collective-permute-start | bytes 811016 | tf_op jit(solution)/shard_map/ppermute | solution.py:550
  98.4 3.0 %home_gather.3 = (f32[128,16,128]{2,1,0:T(8,128)S(1)}, f32[3,128]{1,0:T(4,128)S(1)}) custom-call(s32[5,1,128]{2,1,0:T(1,128)S(1)} %bitcast.28, f32[6,128]{1,0:T(8,128)S(1)} %get-tuple-element.94.amps, f32[1,128]{1,0:T(1,128)S(1)} %bitcast.32, f32[128,32,128]{2,1,0:T(8,128)S(1)} %get-tuple-element.95.morph, bf16[3,17,32,128]{3,2,1,0:T(8,128)(2,1)S(1)} %home_slots.3.back, ...), custom_call_target="tpu_custom_call" | custom-call | bytes 4194304 | tf_op jit(solution)/shard_map/home_gather/pallas_call | solution.py:524
  101.5 3.1 %collective-permute-done.22.refs_1_ = bf16[33,32,128]{2,1,0:T(8,128)(2,1)S(1)} collective-permute-done((bf16[33,32,128]{2,1,0:T(8,128)(2,1)S(1)}, bf16[33,32,128]{2,1,0:T(8,128)(2,1)S(1)}, u32[]{:S(2)}, u32[]{:S(2)}) %collective-permute-start.22) | collective-permute-done | bytes 270368 | tf_op jit(solution)/shard_map/ppermute | solution.py:550
  104.5 3.6 %collective-permute-done.21.refs_0_ = bf16[33,32,128]{2,1,0:T(8,128)(2,1)S(1)} collective-permute-done((bf16[33,32,128]{2,1,0:T(8,128)(2,1)S(1)}, bf16[33,32,128]{2,1,0:T(8,128)(2,1)S(1)}, u32[]{:S(2)}, u32[]{:S(2)}) %collective-permute-start.21) | collective-permute-done | bytes 270368 | tf_op jit(solution)/shard_map/ppermute | solution.py:550
  110.1 3.3 %update.3 = (f32[128,2048]{1,0:T(8,128)}, f32[3,1,128]{2,1,0:T(1,128)}) custom-call(s32[8,128]{1,0:T(8,128)S(1)} %get-tuple-element.58.places, f32[1,128]{1,0:T(1,128)S(1)} %bitcast.33, s32[5,1,128]{2,1,0:T(1,128)S(1)} %bitcast.29, f32[1,128]{1,0:T(1,128)S(1)} %bitcast.35, bf16[4,128,128]{2,1,0:T(8,128)(2,1)S(1)} %get-tuple-element.59.hots, ...), custom_call_target="tpu_custom_call" | custom-call | bytes 3145728 | tf_op jit(solution)/shard_map/update/pallas_call | solution.py:524
  (66 shorter events, 27.2 us)
Async XLA Ops:
  1.8 10.7 %collective-permute-start.1 = (bf16[3,4,4096]{2,1,0:T(4,128)(2,1)S(1)}, bf16[3,4,4096]{2,1,0:T(4,128)(2,1)S(1)}, u32[]{:S(2)}, u32[]{:S(2)}) collective-permute-start(bf16[3,4,4096]{2,1,0:T(4,128)(2,1)S(1)} %slice_select_fusion), channel_id=1, source_target_pairs={{0,16},{8,24},{1,17},{9,25},{2,18},{10,26},{3,19},{11,27},{4,20},{... | collective-permute-start | bytes 294920 | tf_op jit(solution)/shard_map/ppermute | solution.py:564
  6.0 3.5 %collective-permute-start = (f32[3,1,128]{2,1,0:T(1,128)}, f32[3,1,128]{2,1,0:T(1,128)S(1)}, u32[]{:S(2)}, u32[]{:S(2)}) collective-permute-start(f32[3,1,128]{2,1,0:T(1,128)} %bitcast.36), channel_id=1, source_target_pairs={{0,1},{1,0},{2,3},{3,2},{4,5},{5,4},{6,7},{7,6},{8,9},{9,8},{10,11... | collective-permute-start | bytes 4616 | tf_op jit(solution)/shard_map/ppermute | solution.py:554
  12.6 5.4 %collective-permute-start.3 = (bf16[3,4,4096]{2,1,0:T(4,128)(2,1)S(1)}, bf16[3,4,4096]{2,1,0:T(4,128)(2,1)S(1)}, u32[]{:S(2)}, u32[]{:S(2)}) collective-permute-start(bf16[3,4,4096]{2,1,0:T(4,128)(2,1)S(1)} %broadcast_select_fusion.refs_0_), channel_id=1, source_target_pairs={{0,8},{8,0},{16,24},{24,16},{1,9},{9,1},{17,25},{25,17},{2,10},{10... | collective-permute-start | bytes 294920 | tf_op jit(solution)/shard_map/ppermute | solution.py:568
  13.9 14.0 %collective-permute-start.6 = (bf16[33,32,128]{2,1,0:T(8,128)(2,1)S(1)}, bf16[33,32,128]{2,1,0:T(8,128)(2,1)S(1)}, u32[]{:S(2)}, u32[]{:S(2)}) collective-permute-start(bf16[33,32,128]{2,1,0:T(8,128)(2,1)S(1)} %get-tuple-element.71), channel_id=1, source_target_pairs={{0,2},{2,4},{3,1},{4,6},{5,3},{7,5},{8,10},{10,12},{11,9},{12,14},... | collective-permute-start | bytes 811016 | tf_op jit(solution)/shard_map/ppermute | solution.py:550
  17.0 5.0 %collective-permute-start.2 = (bf16[3,4,4096]{2,1,0:T(4,128)(2,1)S(1)}, bf16[3,4,4096]{2,1,0:T(4,128)(2,1)S(1)}, u32[]{:S(2)}, u32[]{:S(2)}) collective-permute-start(bf16[3,4,4096]{2,1,0:T(4,128)(2,1)S(1)} %broadcast_select_fusion.refs_0_), channel_id=1, source_target_pairs={{0,4},{2,6},{4,0},{6,2},{1,5},{3,7},{5,1},{7,3},{8,12},{10,14},{12... | collective-permute-start | bytes 294920 | tf_op jit(solution)/shard_map/ppermute | solution.py:570
  17.1 10.9 %collective-permute-start.5 = (bf16[33,32,128]{2,1,0:T(8,128)(2,1)S(1)}, bf16[33,32,128]{2,1,0:T(8,128)(2,1)S(1)}, u32[]{:S(2)}, u32[]{:S(2)}) collective-permute-start(bf16[33,32,128]{2,1,0:T(8,128)(2,1)S(1)} %get-tuple-element.70), channel_id=1, source_target_pairs={{0,8},{1,25},{2,10},{3,27},{4,12},{5,29},{6,14},{7,31},{8,16},{9,1... | collective-permute-start | bytes 811016 | tf_op jit(solution)/shard_map/ppermute | solution.py:550
  18.0 8.1 %collective-permute-start.4 = (bf16[3,4,4096]{2,1,0:T(4,128)(2,1)S(1)}, bf16[3,4,4096]{2,1,0:T(4,128)(2,1)S(1)}, u32[]{:S(2)}, u32[]{:S(2)}) collective-permute-start(bf16[3,4,4096]{2,1,0:T(4,128)(2,1)S(1)} %collective-permute-done.3.refs_1_), channel_id=1, source_target_pairs={{0,4},{2,6},{4,0},{6,2},{1,5},{3,7},{5,1},{7,3},{8,12},{10,14},{12... | collective-permute-start | bytes 294920 | tf_op jit(solution)/shard_map/ppermute | solution.py:570
  28.0 3.4 %collective-permute-start.7 = (bf16[33,32,128]{2,1,0:T(8,128)(2,1)S(1)}, bf16[33,32,128]{2,1,0:T(8,128)(2,1)S(1)}, u32[]{:S(2)}, u32[]{:S(2)}) collective-permute-start(bf16[33,32,128]{2,1,0:T(8,128)(2,1)S(1)} %collective-permute-done.5.refs_0_), channel_id=1, source_target_pairs={{0,1},{1,0},{2,3},{3,2},{4,5},{5,4},{6,7},{7,6},{8,9},{9,8},{10,11... | collective-permute-start | bytes 811016 | tf_op jit(solution)/shard_map/ppermute | solution.py:554
  29.2 2.2 %collective-permute-start.8 = (bf16[33,32,128]{2,1,0:T(8,128)(2,1)S(1)}, bf16[33,32,128]{2,1,0:T(8,128)(2,1)S(1)}, u32[]{:S(2)}, u32[]{:S(2)}) collective-permute-start(bf16[33,32,128]{2,1,0:T(8,128)(2,1)S(1)} %collective-permute-done.6.refs_1_), channel_id=1, source_target_pairs={{0,1},{1,0},{2,3},{3,2},{4,5},{5,4},{6,7},{7,6},{8,9},{9,8},{10,11... | collective-permute-start | bytes 811016 | tf_op jit(solution)/shard_map/ppermute | solution.py:554
  47.3 2.0 %collective-permute-start.9 = (bf16[65,32,128]{2,1,0:T(8,128)(2,1)S(1)}, bf16[65,32,128]{2,1,0:T(8,128)(2,1)S(1)}, u32[]{:S(2)}, u32[]{:S(2)}) collective-permute-start(bf16[65,32,128]{2,1,0:T(8,128)(2,1)S(1)} %get-tuple-element.83), channel_id=1, source_target_pairs={{0,1},{1,0},{2,3},{3,2},{4,5},{5,4},{6,7},{7,6},{8,9},{9,8},{10,11... | collective-permute-start | bytes 1597448 | tf_op jit(solution)/shard_map/ppermute | solution.py:554
  49.3 2.5 %collective-permute-start.10 = (bf16[3,17,32,128]{3,2,1,0:T(8,128)(2,1)S(1)}, bf16[3,17,32,128]{3,2,1,0:T(8,128)(2,1)S(1)}, u32[]{:S(2)}, u32[]{:S(2)}) collective-permute-start(bf16[3,17,32,128]{3,2,1,0:T(8,128)(2,1)S(1)} %home_slots.2.back), channel_id=1, source_target_pairs={{0,1},{1,0},{2,3},{3,2},{4,5},{5,4},{6,7},{7,6},{8,9},{9,8},{10,11... | collective-permute-start | bytes 1253384 | tf_op jit(solution)/shard_map/ppermute | solution.py:554
  49.8 8.1 %collective-permute-start.12 = (bf16[33,32,128]{2,1,0:T(8,128)(2,1)S(1)}, bf16[33,32,128]{2,1,0:T(8,128)(2,1)S(1)}, u32[]{:S(2)}, u32[]{:S(2)}) collective-permute-start(bf16[33,32,128]{2,1,0:T(8,128)(2,1)S(1)} %get-tuple-element.91), channel_id=1, source_target_pairs={{1,3},{2,0},{3,5},{4,2},{5,7},{6,4},{9,11},{10,8},{11,13},{12,10},... | collective-permute-start | bytes 811016 | tf_op jit(solution)/shard_map/ppermute | solution.py:550
  51.7 9.9 %collective-permute-start.11 = (bf16[33,32,128]{2,1,0:T(8,128)(2,1)S(1)}, bf16[33,32,128]{2,1,0:T(8,128)(2,1)S(1)}, u32[]{:S(2)}, u32[]{:S(2)}) collective-permute-start(bf16[33,32,128]{2,1,0:T(8,128)(2,1)S(1)} %get-tuple-element.89), channel_id=1, source_target_pairs={{0,24},{1,9},{2,26},{3,11},{4,28},{5,13},{6,30},{7,15},{8,0},{9,17... | collective-permute-start | bytes 811016 | tf_op jit(solution)/shard_map/ppermute | solution.py:550
  61.7 1.5 %collective-permute-start.13 = (bf16[33,32,128]{2,1,0:T(8,128)(2,1)S(1)}, bf16[33,32,128]{2,1,0:T(8,128)(2,1)S(1)}, u32[]{:S(2)}, u32[]{:S(2)}) collective-permute-start(bf16[33,32,128]{2,1,0:T(8,128)(2,1)S(1)} %collective-permute-done.11.refs_0_), channel_id=1, source_target_pairs={{0,1},{1,0},{2,3},{3,2},{4,5},{5,4},{6,7},{7,6},{8,9},{9,8},{10,11... | collective-permute-start | bytes 811016 | tf_op jit(solution)/shard_map/ppermute | solution.py:554
  61.7 1.9 %collective-permute-start.14 = (bf16[33,32,128]{2,1,0:T(8,128)(2,1)S(1)}, bf16[33,32,128]{2,1,0:T(8,128)(2,1)S(1)}, u32[]{:S(2)}, u32[]{:S(2)}) collective-permute-start(bf16[33,32,128]{2,1,0:T(8,128)(2,1)S(1)} %collective-permute-done.12.refs_1_), channel_id=1, source_target_pairs={{0,1},{1,0},{2,3},{3,2},{4,5},{5,4},{6,7},{7,6},{8,9},{9,8},{10,11... | collective-permute-start | bytes 811016 | tf_op jit(solution)/shard_map/ppermute | solution.py:554
  65.6 7.9 %collective-permute-start.16 = (bf16[33,32,128]{2,1,0:T(8,128)(2,1)S(1)}, bf16[33,32,128]{2,1,0:T(8,128)(2,1)S(1)}, u32[]{:S(2)}, u32[]{:S(2)}) collective-permute-start(bf16[33,32,128]{2,1,0:T(8,128)(2,1)S(1)} %get-tuple-element.98), channel_id=1, source_target_pairs={{0,2},{2,4},{3,1},{4,6},{5,3},{7,5},{8,10},{10,12},{11,9},{12,14},... | collective-permute-start | bytes 811016 | tf_op jit(solution)/shard_map/ppermute | solution.py:550
  67.6 6.8 %collective-permute-start.15 = (bf16[33,32,128]{2,1,0:T(8,128)(2,1)S(1)}, bf16[33,32,128]{2,1,0:T(8,128)(2,1)S(1)}, u32[]{:S(2)}, u32[]{:S(2)}) collective-permute-start(bf16[33,32,128]{2,1,0:T(8,128)(2,1)S(1)} %get-tuple-element.96), channel_id=1, source_target_pairs={{0,8},{1,25},{2,10},{3,27},{4,12},{5,29},{6,14},{7,31},{8,16},{9,1... | collective-permute-start | bytes 811016 | tf_op jit(solution)/shard_map/ppermute | solution.py:550
  74.3 3.7 %collective-permute-start.17 = (bf16[33,32,128]{2,1,0:T(8,128)(2,1)S(1)}, bf16[33,32,128]{2,1,0:T(8,128)(2,1)S(1)}, u32[]{:S(2)}, u32[]{:S(2)}) collective-permute-start(bf16[33,32,128]{2,1,0:T(8,128)(2,1)S(1)} %collective-permute-done.15.refs_0_), channel_id=1, source_target_pairs={{0,1},{1,0},{2,3},{3,2},{4,5},{5,4},{6,7},{7,6},{8,9},{9,8},{10,11... | collective-permute-start | bytes 811016 | tf_op jit(solution)/shard_map/ppermute | solution.py:554
  76.9 1.6 %collective-permute-start.18 = (bf16[33,32,128]{2,1,0:T(8,128)(2,1)S(1)}, bf16[33,32,128]{2,1,0:T(8,128)(2,1)S(1)}, u32[]{:S(2)}, u32[]{:S(2)}) collective-permute-start(bf16[33,32,128]{2,1,0:T(8,128)(2,1)S(1)} %collective-permute-done.16.refs_1_), channel_id=1, source_target_pairs={{0,1},{1,0},{2,3},{3,2},{4,5},{5,4},{6,7},{7,6},{8,9},{9,8},{10,11... | collective-permute-start | bytes 811016 | tf_op jit(solution)/shard_map/ppermute | solution.py:554
  94.0 1.9 %collective-permute-start.19 = (bf16[65,32,128]{2,1,0:T(8,128)(2,1)S(1)}, bf16[65,32,128]{2,1,0:T(8,128)(2,1)S(1)}, u32[]{:S(2)}, u32[]{:S(2)}) collective-permute-start(bf16[65,32,128]{2,1,0:T(8,128)(2,1)S(1)} %get-tuple-element.102), channel_id=1, source_target_pairs={{0,1},{1,0},{2,3},{3,2},{4,5},{5,4},{6,7},{7,6},{8,9},{9,8},{10,11... | collective-permute-start | bytes 1597448 | tf_op jit(solution)/shard_map/ppermute | solution.py:554
  95.9 2.5 %collective-permute-start.20 = (bf16[3,17,32,128]{3,2,1,0:T(8,128)(2,1)S(1)}, bf16[3,17,32,128]{3,2,1,0:T(8,128)(2,1)S(1)}, u32[]{:S(2)}, u32[]{:S(2)}) collective-permute-start(bf16[3,17,32,128]{3,2,1,0:T(8,128)(2,1)S(1)} %home_slots.3.back), channel_id=1, source_target_pairs={{0,1},{1,0},{2,3},{3,2},{4,5},{5,4},{6,7},{7,6},{8,9},{9,8},{10,11... | collective-permute-start | bytes 1253384 | tf_op jit(solution)/shard_map/ppermute | solution.py:554
  96.4 8.1 %collective-permute-start.22 = (bf16[33,32,128]{2,1,0:T(8,128)(2,1)S(1)}, bf16[33,32,128]{2,1,0:T(8,128)(2,1)S(1)}, u32[]{:S(2)}, u32[]{:S(2)}) collective-permute-start(bf16[33,32,128]{2,1,0:T(8,128)(2,1)S(1)} %get-tuple-element.110), channel_id=1, source_target_pairs={{1,3},{2,0},{3,5},{4,2},{5,7},{6,4},{9,11},{10,8},{11,13},{12,10},... | collective-permute-start | bytes 811016 | tf_op jit(solution)/shard_map/ppermute | solution.py:550
  98.4 9.8 %collective-permute-start.21 = (bf16[33,32,128]{2,1,0:T(8,128)(2,1)S(1)}, bf16[33,32,128]{2,1,0:T(8,128)(2,1)S(1)}, u32[]{:S(2)}, u32[]{:S(2)}) collective-permute-start(bf16[33,32,128]{2,1,0:T(8,128)(2,1)S(1)} %get-tuple-element.108), channel_id=1, source_target_pairs={{0,24},{1,9},{2,26},{3,11},{4,28},{5,13},{6,30},{7,15},{8,0},{9,17... | collective-permute-start | bytes 811016 | tf_op jit(solution)/shard_map/ppermute | solution.py:550
  108.2 1.9 %collective-permute-start.24 = (bf16[33,32,128]{2,1,0:T(8,128)(2,1)S(1)}, bf16[33,32,128]{2,1,0:T(8,128)(2,1)S(1)}, u32[]{:S(2)}, u32[]{:S(2)}) collective-permute-start(bf16[33,32,128]{2,1,0:T(8,128)(2,1)S(1)} %collective-permute-done.22.refs_1_), channel_id=1, source_target_pairs={{0,1},{1,0},{2,3},{3,2},{4,5},{5,4},{6,7},{7,6},{8,9},{9,8},{10,11... | collective-permute-start | bytes 811016 | tf_op jit(solution)/shard_map/ppermute | solution.py:554
  (8 other events, 42.9 us)

commit v4 on v3

--- a/solution.py
+++ b/solution.py
@@ -18,7 +18,7 @@
 ORDER, KERNEL_OF, SLOT_OF, COUNT = range(4)
 NEAR = 4
 GROUP = 4
-STRIDE = 4
+STRIDE = 8
 F32 = jnp.float32
 BF16 = jnp.bfloat16
 
@@ -564,7 +564,7 @@
         far = lax.ppermute(mine, "ra", [(0, 2), (1, 3)])
         far, sums = lax.optimization_barrier((far, sums))
         here = jnp.where(lax.axis_index("ra") < 2, mine, far)
-        here, messages[0] = lax.optimization_barrier((here, messages[0]))
+        here, *messages = lax.optimization_barrier((here, *messages))
         near = lax.ppermute(here, "ra", along)
         halves = make_tables((here, near), bands)
         others = (lax.ppermute(here, "dec", across), lax.ppermute(near, "dec", across))

time: 115 us -> 109 us (0.948); the launches traced: 113 us -> 110 us
  waiting for transfers between devices: 25 us -> 21.8 us
  Pallas kernels: 59 us -> 56.8 us
  starting transfers between devices: 24.9 us -> 26.9 us
    ppermute x8, starting transfers between devices: 10.3 us -> 15.1 us  [stepped(): return lax.ppermute(value, ('ra', 'dec', 'band'), pairs)]
    ppermute x8, waiting for transfers between devices: 14.4 us -> 11.1 us  [stepped(): return lax.ppermute(value, ('ra', 'dec', 'band'), pairs)]
    pallas_call x22, Pallas kernels: 59 us -> 56.8 us  [call(): pl.pallas_call(body, out_shape=[jax.ShapeDtypeStruct(shape, dtype) for sh...]
    ppermute x13, starting transfers between devices: 7.53 us -> 5.86 us  [swapped(): return lax.ppermute(value, 'band', [(0, 1), (1, 0)])]
    ppermute x1, starting transfers between devices: 1.4 us -> 0.07 us  [all_tables(): lax.ppermute(near, 'dec', across)]
  transfers between devices with their start and end apart: 25 -> 25, of which waited for: 16 -> 14; matrix products, arithmetic and copies ran while one was open for 1% -> 1% of each run, Pallas kernels for 20% -> 20%
where the time goes in v4:
time: 109 us; the launch traced here: 110 us
  Pallas kernels  56.8 us (52%)
  starting transfers between devices  26.9 us (25%)
  waiting for transfers between devices  21.8 us (20%)
  local copies, waits for them, and re-layouts  2.29 us (2%)
  other arithmetic  1.21 us (1%)
    pallas_call x22, Pallas kernels, call(): pl.pallas_call(body, out_shape=[jax.ShapeDtypeStruct(shape, dtype) for sh...  56.8 us
    ppermute x8, starting transfers between devices, stepped(): return lax.ppermute(value, ('ra', 'dec', 'band'), pairs)  15.1 us
    ppermute x8, waiting for transfers between devices, stepped(): return lax.ppermute(value, ('ra', 'dec', 'band'), pairs)  11.1 us
    ppermute x13, starting transfers between devices, swapped(): return lax.ppermute(value, 'band', [(0, 1), (1, 0)])  5.86 us
    ppermute x13, waiting for transfers between devices, swapped(): return lax.ppermute(value, 'band', [(0, 1), (1, 0)])  5.72 us
    ppermute x1, waiting for transfers between devices, all_tables(): lax.ppermute(near, 'dec', across)  4.96 us
    ppermute x1, starting transfers between devices, all_tables(): far = lax.ppermute(mine, 'ra', [(0, 2), (1, 3)])  4.22 us
    unnamed x16, local copies, waits for them, and re-layouts  2.29 us
  transfers between devices with their start and end apart: 25, of which 14 were waited for; matrix products, arithmetic and copies ran while one was open for 1% of the time, Pallas kernels for 20%

profile of v4, /device:TPU:5, one launch (start us, length us, event | category | flops | bytes accessed | tf_op | source)
XLA Modules:
  0.0 110.0 jit_solution(17243454317267921100)
XLA Ops:
  1.8 4.2 %collective-permute-start.1 = (bf16[3,4,4096]{2,1,0:T(4,128)(2,1)S(1)}, bf16[3,4,4096]{2,1,0:T(4,128)(2,1)S(1)}, u32[]{:S(2)}, u32[]{:S(2)}) collective-permute-start(bf16[3,4,4096]{2,1,0:T(4,128)(2,1)S(1)} %slice_select_fusion), channel_id=1, source_target_pairs={{0,16},{8,24},{1,17},{9,25},{2,18},{10,26},{3,19},{11,27},{4,20},{... | collective-permute-start | bytes 294920 | tf_op jit(solution)/shard_map/ppermute | solution.py:564
  10.6 1.8 %home_sums.2.sums = f32[3,17,32,128]{3,2,1,0:T(8,128)S(1)} custom-call(s32[5,1,128]{2,1,0:T(1,128)S(1)} %bitcast.24, f32[6,128]{1,0:T(8,128)S(1)} %get-tuple-element.62.amps, bf16[128,32,128]{2,1,0:T(8,128)(2,1)S(1)} %bitcast.18), custom_call_target="tpu_custom_call" | custom-call | bytes 4194304 | tf_op jit(solution)/shard_map/home_sums/pallas_call | solution.py:524
  15.1 4.1 %collective-permute-start.6 = (bf16[33,32,128]{2,1,0:T(8,128)(2,1)S(1)}, bf16[33,32,128]{2,1,0:T(8,128)(2,1)S(1)}, u32[]{:S(2)}, u32[]{:S(2)}) collective-permute-start(bf16[33,32,128]{2,1,0:T(8,128)(2,1)S(1)} %get-tuple-element.73), channel_id=1, source_target_pairs={{0,2},{2,4},{3,1},{4,6},{5,3},{7,5},{8,10},{10,12},{11,9},{12,14},... | collective-permute-start | bytes 811016 | tf_op jit(solution)/shard_map/ppermute | solution.py:550
  19.2 1.8 %tables.2 = (bf16[8,64,256]{2,1,0:T(8,128)(2,1)S(1)}, bf16[3,8,64,64]{3,2,1,0:T(8,128)(2,1)S(1)}, bf16[3,8,64,64]{3,2,1,0:T(8,128)(2,1)S(1)}, bf16[8,256,128]{2,1,0:T(8,128)(2,1)S(1)}) custom-call(bf16[3,4,4096]{2,1,0:T(4,128)(2,1)S(1)} %broadcast_select_fusion.refs_0_, bf16[3,4,4096]{2,1,0:T(4,128)(2,1)S(1)} %collective-permute-done.3.refs_1_), custom_call_target="tpu_custom_call" | custom-call | flops 2000000000 | bytes 5242880 | tf_op jit(solution)/shard_map/tables/pallas_call | solution.py:524
  21.0 5.0 %collective-permute-done.4.refs_1_ = bf16[3,4,4096]{2,1,0:T(4,128)(2,1)S(1)} collective-permute-done((bf16[3,4,4096]{2,1,0:T(4,128)(2,1)S(1)}, bf16[3,4,4096]{2,1,0:T(4,128)(2,1)S(1)}, u32[]{:S(2)}, u32[]{:S(2)}) %collective-permute-start.4) | collective-permute-done | bytes 98336 | tf_op jit(solution)/shard_map/ppermute | solution.py:570
  26.0 1.8 %tables.3 = (bf16[16,64,256]{2,1,0:T(8,128)(2,1)S(1)}, bf16[3,16,64,64]{3,2,1,0:T(8,128)(2,1)S(1)}, bf16[3,16,64,64]{3,2,1,0:T(8,128)(2,1)S(1)}, bf16[16,256,128]{2,1,0:T(8,128)(2,1)S(1)}) custom-call(bf16[3,4,4096]{2,1,0:T(4,128)(2,1)S(1)} %collective-permute-done.2.refs_0_, bf16[3,4,4096]{2,1,0:T(4,128)(2,1)S(1)} %collective-permute-done.4.refs_1_, ...), custom_call_target="tpu_custom_call" | custom-call | flops 2000000000 | bytes 5242880 | tf_op jit(solution)/shard_map/tables/pallas_call | solution.py:524
  28.5 2.0 %home_forward.2.refs_4_ = f32[3,16,64,128]{3,2,1,0:T(8,128)S(1)} custom-call(f32[3,17,32,128]{3,2,1,0:T(8,128)S(1)} %home_sums.2.sums, bf16[3,16,32,128]{3,2,1,0:T(8,128)(2,1)S(1)} %bitcast.20, bf16[16,64,256]{2,1,0:T(8,128)(2,1)S(1)} %get-tuple-element.79.first_t.refs_5_, bf16[3,16,64,64]{3,2,1,0:T(8,128)(2,1)S(1)} %get-tuple-element.80.left.refs_6_), custom_call_target="tpu_custom_call" | custom-call | flops 2000000000 | bytes 4194304 | tf_op jit(solution)/shard_map/home_forward/pallas_call | solution.py:524
  31.1 6.3 %forward.2 = (bf16[3,16,64,128]{3,2,1,0:T(8,128)(2,1)S(1)}, bf16[48,3,64,256]{3,2,1,0:T(8,128)(2,1)S(1)}) custom-call(s32[8,256]{1,0:T(8,128)S(1)} %get-tuple-element.76.plan, f32[3,128]{1,0:T(4,128)S(1)} %get-tuple-element.77.amps, bf16[33,32,128]{2,1,0:T(8,128)(2,1)S(1)} %collective-permute-done.5.refs_0_, ...), custom_call_target="tpu_custom_call" | custom-call | flops 3000000000 | bytes 8388608 | tf_op jit(solution)/shard_map/forward/pallas_call | solution.py:524
  37.5 8.0 %backward.2 = (bf16[65,32,128]{2,1,0:T(8,128)(2,1)S(1)}, bf16[65,32,128]{2,1,0:T(8,128)(2,1)S(1)}) custom-call(s32[8,256]{1,0:T(8,128)S(1)} %get-tuple-element.76.plan, f32[3,128]{1,0:T(4,128)S(1)} %get-tuple-element.77.amps, bf16[3,16,64,128]{3,2,1,0:T(8,128)(2,1)S(1)} %get-tuple-element.81.refs_0_.residual, ...), custom_call_target="tpu_custom_call" | custom-call | flops 3000000000 | bytes 8388608 | tf_op jit(solution)/shard_map/backward/pallas_call | solution.py:524
  48.0 1.9 %collective-permute-start.12 = (bf16[33,32,128]{2,1,0:T(8,128)(2,1)S(1)}, bf16[33,32,128]{2,1,0:T(8,128)(2,1)S(1)}, u32[]{:S(2)}, u32[]{:S(2)}) collective-permute-start(bf16[33,32,128]{2,1,0:T(8,128)(2,1)S(1)} %get-tuple-element.93), channel_id=1, source_target_pairs={{1,3},{2,0},{3,5},{4,2},{5,7},{6,4},{9,11},{10,8},{11,13},{12,10},... | collective-permute-start | bytes 811016 | tf_op jit(solution)/shard_map/ppermute | solution.py:550
  51.4 4.5 %home_gather.2 = (f32[128,32,128]{2,1,0:T(8,128)S(1)}, f32[6,128]{1,0:T(8,128)S(1)}) custom-call(s32[5,1,128]{2,1,0:T(1,128)S(1)} %bitcast.25, f32[6,128]{1,0:T(8,128)S(1)} %get-tuple-element.62.amps, f32[1,128]{1,0:T(1,128)S(1)} %bitcast.30, bf16[128,32,128]{2,1,0:T(8,128)(2,1)S(1)} %bitcast.19, bf16[3,17,32,128]{3,2,1,0:T(8,128)(2,1)S(1)} %home_slots.2.back, ...), custom_call_target="tpu_custom_call" | custom-call | bytes 4194304 | tf_op jit(solution)/shard_map/home_gather/pallas_call | solution.py:524
  56.1 3.5 %collective-permute-done.11.refs_0_ = bf16[33,32,128]{2,1,0:T(8,128)(2,1)S(1)} collective-permute-done((bf16[33,32,128]{2,1,0:T(8,128)(2,1)S(1)}, bf16[33,32,128]{2,1,0:T(8,128)(2,1)S(1)}, u32[]{:S(2)}, u32[]{:S(2)}) %collective-permute-start.11) | collective-permute-done | bytes 270368 | tf_op jit(solution)/shard_map/ppermute | solution.py:550
  61.5 1.9 %update.2 = (f32[128,32,128]{2,1,0:T(8,128)S(1)}, f32[6,128]{1,0:T(8,128)S(1)}, f32[6,128]{1,0:T(8,128)S(1)}, bf16[33,32,128]{2,1,0:T(8,128)(2,1)S(1)}, bf16[33,32,128]{2,1,0:T(8,128)(2,1)S(1)}) custom-call(s32[8,128]{1,0:T(8,128)S(1)} %get-tuple-element.59.places, f32[1,128]{1,0:T(1,128)S(1)} %bitcast.31, s32[5,1,128]{2,1,0:T(1,128)S(1)} %bitcast.26, ...), custom_call_target="tpu_custom_call" | custom-call | bytes 3145728 | tf_op jit(solution)/shard_map/update/pallas_call | solution.py:524
  63.5 1.9 %collective-permute-start.16 = (bf16[33,32,128]{2,1,0:T(8,128)(2,1)S(1)}, bf16[33,32,128]{2,1,0:T(8,128)(2,1)S(1)}, u32[]{:S(2)}, u32[]{:S(2)}) collective-permute-start(bf16[33,32,128]{2,1,0:T(8,128)(2,1)S(1)} %get-tuple-element.100), channel_id=1, source_target_pairs={{0,2},{2,4},{3,1},{4,6},{5,3},{7,5},{8,10},{10,12},{11,9},{12,14},... | collective-permute-start | bytes 811016 | tf_op jit(solution)/shard_map/ppermute | solution.py:550
  65.4 2.3 %collective-permute-start.15 = (bf16[33,32,128]{2,1,0:T(8,128)(2,1)S(1)}, bf16[33,32,128]{2,1,0:T(8,128)(2,1)S(1)}, u32[]{:S(2)}, u32[]{:S(2)}) collective-permute-start(bf16[33,32,128]{2,1,0:T(8,128)(2,1)S(1)} %get-tuple-element.98), channel_id=1, source_target_pairs={{0,8},{1,25},{2,10},{3,27},{4,12},{5,29},{6,14},{7,31},{8,16},{9,1... | collective-permute-start | bytes 811016 | tf_op jit(solution)/shard_map/ppermute | solution.py:550
  69.5 2.0 %home_forward.3.refs_4_ = f32[3,16,64,128]{3,2,1,0:T(8,128)S(1)} custom-call(f32[3,17,32,128]{3,2,1,0:T(8,128)S(1)} %home_sums.3.sums, bf16[3,16,32,128]{3,2,1,0:T(8,128)(2,1)S(1)} %bitcast.21, bf16[16,64,256]{2,1,0:T(8,128)(2,1)S(1)} %get-tuple-element.79.first_t.refs_5_, bf16[3,16,64,64]{3,2,1,0:T(8,128)(2,1)S(1)} %get-tuple-element.80.left.refs_6_), custom_call_target="tpu_custom_call" | custom-call | flops 2000000000 | bytes 4194304 | tf_op jit(solution)/shard_map/home_forward/pallas_call | solution.py:524
  71.5 2.0 %collective-permute-done.15.refs_0_ = bf16[33,32,128]{2,1,0:T(8,128)(2,1)S(1)} collective-permute-done((bf16[33,32,128]{2,1,0:T(8,128)(2,1)S(1)}, bf16[33,32,128]{2,1,0:T(8,128)(2,1)S(1)}, u32[]{:S(2)}, u32[]{:S(2)}) %collective-permute-start.15) | collective-permute-done | bytes 270368 | tf_op jit(solution)/shard_map/ppermute | solution.py:550
  76.9 6.5 %forward.3 = (bf16[3,16,64,128]{3,2,1,0:T(8,128)(2,1)S(1)}, bf16[48,3,64,256]{3,2,1,0:T(8,128)(2,1)S(1)}) custom-call(s32[8,256]{1,0:T(8,128)S(1)} %get-tuple-element.76.plan, f32[3,128]{1,0:T(4,128)S(1)} %order.3.amps, bf16[33,32,128]{2,1,0:T(8,128)(2,1)S(1)} %collective-permute-done.15.refs_0_, bf16[33,32,128]{2,1,0:T(8,128)(2,1)S(1)} %collective-permute-done.16.refs_1_, ...), custom_call_target="tpu_custom_call" | custom-call | flops 3000000000 | bytes 8388608 | tf_op jit(solution)/shard_map/forward/pallas_call | solution.py:524
  83.4 8.1 %backward.3 = (bf16[65,32,128]{2,1,0:T(8,128)(2,1)S(1)}, bf16[65,32,128]{2,1,0:T(8,128)(2,1)S(1)}) custom-call(s32[8,256]{1,0:T(8,128)S(1)} %get-tuple-element.76.plan, f32[3,128]{1,0:T(4,128)S(1)} %order.3.amps, bf16[3,16,64,128]{3,2,1,0:T(8,128)(2,1)S(1)} %get-tuple-element.102.refs_0_.residual, bf16[48,3,64,256]{3,2,1,0:T(8,128)(2,1)S(1)} %get-tuple-element.103.refs_1_, ...), custom_call_target="tpu_custom_call" | custom-call | flops 3000000000 | bytes 8388608 | tf_op jit(solution)/shard_map/backward/pallas_call | solution.py:524
  93.9 1.9 %collective-permute-start.22 = (bf16[33,32,128]{2,1,0:T(8,128)(2,1)S(1)}, bf16[33,32,128]{2,1,0:T(8,128)(2,1)S(1)}, u32[]{:S(2)}, u32[]{:S(2)}) collective-permute-start(bf16[33,32,128]{2,1,0:T(8,128)(2,1)S(1)} %get-tuple-element.112), channel_id=1, source_target_pairs={{1,3},{2,0},{3,5},{4,2},{5,7},{6,4},{9,11},{10,8},{11,13},{12,10},... | collective-permute-start | bytes 811016 | tf_op jit(solution)/shard_map/ppermute | solution.py:550
  96.4 3.0 %home_gather.3 = (f32[128,16,128]{2,1,0:T(8,128)S(1)}, f32[3,128]{1,0:T(4,128)S(1)}) custom-call(s32[5,1,128]{2,1,0:T(1,128)S(1)} %bitcast.28, f32[6,128]{1,0:T(8,128)S(1)} %get-tuple-element.96.amps, f32[1,128]{1,0:T(1,128)S(1)} %bitcast.32, f32[128,32,128]{2,1,0:T(8,128)S(1)} %get-tuple-element.97.morph, bf16[3,17,32,128]{3,2,1,0:T(8,128)(2,1)S(1)} %home_slots.3.back, ...), custom_call_target="tpu_custom_call" | custom-call | bytes 4194304 | tf_op jit(solution)/shard_map/home_gather/pallas_call | solution.py:524
  99.4 2.6 %collective-permute-done.22.refs_1_ = bf16[33,32,128]{2,1,0:T(8,128)(2,1)S(1)} collective-permute-done((bf16[33,32,128]{2,1,0:T(8,128)(2,1)S(1)}, bf16[33,32,128]{2,1,0:T(8,128)(2,1)S(1)}, u32[]{:S(2)}, u32[]{:S(2)}) %collective-permute-start.22) | collective-permute-done | bytes 270368 | tf_op jit(solution)/shard_map/ppermute | solution.py:550
  102.0 2.9 %collective-permute-done.21.refs_0_ = bf16[33,32,128]{2,1,0:T(8,128)(2,1)S(1)} collective-permute-done((bf16[33,32,128]{2,1,0:T(8,128)(2,1)S(1)}, bf16[33,32,128]{2,1,0:T(8,128)(2,1)S(1)}, u32[]{:S(2)}, u32[]{:S(2)}) %collective-permute-start.21) | collective-permute-done | bytes 270368 | tf_op jit(solution)/shard_map/ppermute | solution.py:550
  106.9 3.1 %update.3 = (f32[128,2048]{1,0:T(8,128)}, f32[3,1,128]{2,1,0:T(1,128)}) custom-call(s32[8,128]{1,0:T(8,128)S(1)} %get-tuple-element.59.places, f32[1,128]{1,0:T(1,128)S(1)} %bitcast.33, s32[5,1,128]{2,1,0:T(1,128)S(1)} %bitcast.29, f32[1,128]{1,0:T(1,128)S(1)} %bitcast.35, bf16[4,128,128]{2,1,0:T(8,128)(2,1)S(1)} %get-tuple-element.60.hots, ...), custom_call_target="tpu_custom_call" | custom-call | bytes 3145728 | tf_op jit(solution)/shard_map/update/pallas_call | solution.py:524
  (66 shorter events, 25.7 us)
Async XLA Ops:
  1.8 10.6 %collective-permute-start.1 = (bf16[3,4,4096]{2,1,0:T(4,128)(2,1)S(1)}, bf16[3,4,4096]{2,1,0:T(4,128)(2,1)S(1)}, u32[]{:S(2)}, u32[]{:S(2)}) collective-permute-start(bf16[3,4,4096]{2,1,0:T(4,128)(2,1)S(1)} %slice_select_fusion), channel_id=1, source_target_pairs={{0,16},{8,24},{1,17},{9,25},{2,18},{10,26},{3,19},{11,27},{4,20},{... | collective-permute-start | bytes 294920 | tf_op jit(solution)/shard_map/ppermute | solution.py:564
  6.0 3.5 %collective-permute-start = (f32[3,1,128]{2,1,0:T(1,128)}, f32[3,1,128]{2,1,0:T(1,128)S(1)}, u32[]{:S(2)}, u32[]{:S(2)}) collective-permute-start(f32[3,1,128]{2,1,0:T(1,128)} %bitcast.36), channel_id=1, source_target_pairs={{0,1},{1,0},{2,3},{3,2},{4,5},{5,4},{6,7},{7,6},{8,9},{9,8},{10,11... | collective-permute-start | bytes 4616 | tf_op jit(solution)/shard_map/ppermute | solution.py:554
  12.5 6.6 %collective-permute-start.3 = (bf16[3,4,4096]{2,1,0:T(4,128)(2,1)S(1)}, bf16[3,4,4096]{2,1,0:T(4,128)(2,1)S(1)}, u32[]{:S(2)}, u32[]{:S(2)}) collective-permute-start(bf16[3,4,4096]{2,1,0:T(4,128)(2,1)S(1)} %broadcast_select_fusion.refs_0_), channel_id=1, source_target_pairs={{0,8},{8,0},{16,24},{24,16},{1,9},{9,1},{17,25},{25,17},{2,10},{10... | collective-permute-start | bytes 294920 | tf_op jit(solution)/shard_map/ppermute | solution.py:568
  13.9 7.1 %collective-permute-start.2 = (bf16[3,4,4096]{2,1,0:T(4,128)(2,1)S(1)}, bf16[3,4,4096]{2,1,0:T(4,128)(2,1)S(1)}, u32[]{:S(2)}, u32[]{:S(2)}) collective-permute-start(bf16[3,4,4096]{2,1,0:T(4,128)(2,1)S(1)} %broadcast_select_fusion.refs_0_), channel_id=1, source_target_pairs={{0,4},{2,6},{4,0},{6,2},{1,5},{3,7},{5,1},{7,3},{8,12},{10,14},{12... | collective-permute-start | bytes 294920 | tf_op jit(solution)/shard_map/ppermute | solution.py:570
  14.1 13.7 %collective-permute-start.5 = (bf16[33,32,128]{2,1,0:T(8,128)(2,1)S(1)}, bf16[33,32,128]{2,1,0:T(8,128)(2,1)S(1)}, u32[]{:S(2)}, u32[]{:S(2)}) collective-permute-start(bf16[33,32,128]{2,1,0:T(8,128)(2,1)S(1)} %get-tuple-element.72), channel_id=1, source_target_pairs={{0,8},{1,25},{2,10},{3,27},{4,12},{5,29},{6,14},{7,31},{8,16},{9,1... | collective-permute-start | bytes 811016 | tf_op jit(solution)/shard_map/ppermute | solution.py:550
  15.1 12.8 %collective-permute-start.6 = (bf16[33,32,128]{2,1,0:T(8,128)(2,1)S(1)}, bf16[33,32,128]{2,1,0:T(8,128)(2,1)S(1)}, u32[]{:S(2)}, u32[]{:S(2)}) collective-permute-start(bf16[33,32,128]{2,1,0:T(8,128)(2,1)S(1)} %get-tuple-element.73), channel_id=1, source_target_pairs={{0,2},{2,4},{3,1},{4,6},{5,3},{7,5},{8,10},{10,12},{11,9},{12,14},... | collective-permute-start | bytes 811016 | tf_op jit(solution)/shard_map/ppermute | solution.py:550
  19.1 6.9 %collective-permute-start.4 = (bf16[3,4,4096]{2,1,0:T(4,128)(2,1)S(1)}, bf16[3,4,4096]{2,1,0:T(4,128)(2,1)S(1)}, u32[]{:S(2)}, u32[]{:S(2)}) collective-permute-start(bf16[3,4,4096]{2,1,0:T(4,128)(2,1)S(1)} %collective-permute-done.3.refs_1_), channel_id=1, source_target_pairs={{0,4},{2,6},{4,0},{6,2},{1,5},{3,7},{5,1},{7,3},{8,12},{10,14},{12... | collective-permute-start | bytes 294920 | tf_op jit(solution)/shard_map/ppermute | solution.py:570
  27.9 2.7 %collective-permute-start.7 = (bf16[33,32,128]{2,1,0:T(8,128)(2,1)S(1)}, bf16[33,32,128]{2,1,0:T(8,128)(2,1)S(1)}, u32[]{:S(2)}, u32[]{:S(2)}) collective-permute-start(bf16[33,32,128]{2,1,0:T(8,128)(2,1)S(1)} %collective-permute-done.5.refs_0_), channel_id=1, source_target_pairs={{0,1},{1,0},{2,3},{3,2},{4,5},{5,4},{6,7},{7,6},{8,9},{9,8},{10,11... | collective-permute-start | bytes 811016 | tf_op jit(solution)/shard_map/ppermute | solution.py:554
  28.3 2.3 %collective-permute-start.8 = (bf16[33,32,128]{2,1,0:T(8,128)(2,1)S(1)}, bf16[33,32,128]{2,1,0:T(8,128)(2,1)S(1)}, u32[]{:S(2)}, u32[]{:S(2)}) collective-permute-start(bf16[33,32,128]{2,1,0:T(8,128)(2,1)S(1)} %collective-permute-done.6.refs_1_), channel_id=1, source_target_pairs={{0,1},{1,0},{2,3},{3,2},{4,5},{5,4},{6,7},{7,6},{8,9},{9,8},{10,11... | collective-permute-start | bytes 811016 | tf_op jit(solution)/shard_map/ppermute | solution.py:554
  45.5 2.0 %collective-permute-start.9 = (bf16[65,32,128]{2,1,0:T(8,128)(2,1)S(1)}, bf16[65,32,128]{2,1,0:T(8,128)(2,1)S(1)}, u32[]{:S(2)}, u32[]{:S(2)}) collective-permute-start(bf16[65,32,128]{2,1,0:T(8,128)(2,1)S(1)} %get-tuple-element.85), channel_id=1, source_target_pairs={{0,1},{1,0},{2,3},{3,2},{4,5},{5,4},{6,7},{7,6},{8,9},{9,8},{10,11... | collective-permute-start | bytes 1597448 | tf_op jit(solution)/shard_map/ppermute | solution.py:554
  47.5 3.9 %collective-permute-start.10 = (bf16[3,17,32,128]{3,2,1,0:T(8,128)(2,1)S(1)}, bf16[3,17,32,128]{3,2,1,0:T(8,128)(2,1)S(1)}, u32[]{:S(2)}, u32[]{:S(2)}) collective-permute-start(bf16[3,17,32,128]{3,2,1,0:T(8,128)(2,1)S(1)} %home_slots.2.back), channel_id=1, source_target_pairs={{0,1},{1,0},{2,3},{3,2},{4,5},{5,4},{6,7},{7,6},{8,9},{9,8},{10,11... | collective-permute-start | bytes 1253384 | tf_op jit(solution)/shard_map/ppermute | solution.py:554
  48.0 8.1 %collective-permute-start.12 = (bf16[33,32,128]{2,1,0:T(8,128)(2,1)S(1)}, bf16[33,32,128]{2,1,0:T(8,128)(2,1)S(1)}, u32[]{:S(2)}, u32[]{:S(2)}) collective-permute-start(bf16[33,32,128]{2,1,0:T(8,128)(2,1)S(1)} %get-tuple-element.93), channel_id=1, source_target_pairs={{1,3},{2,0},{3,5},{4,2},{5,7},{6,4},{9,11},{10,8},{11,13},{12,10},... | collective-permute-start | bytes 811016 | tf_op jit(solution)/shard_map/ppermute | solution.py:550
  49.9 9.7 %collective-permute-start.11 = (bf16[33,32,128]{2,1,0:T(8,128)(2,1)S(1)}, bf16[33,32,128]{2,1,0:T(8,128)(2,1)S(1)}, u32[]{:S(2)}, u32[]{:S(2)}) collective-permute-start(bf16[33,32,128]{2,1,0:T(8,128)(2,1)S(1)} %get-tuple-element.91), channel_id=1, source_target_pairs={{0,24},{1,9},{2,26},{3,11},{4,28},{5,13},{6,30},{7,15},{8,0},{9,17... | collective-permute-start | bytes 811016 | tf_op jit(solution)/shard_map/ppermute | solution.py:550
  59.6 1.5 %collective-permute-start.13 = (bf16[33,32,128]{2,1,0:T(8,128)(2,1)S(1)}, bf16[33,32,128]{2,1,0:T(8,128)(2,1)S(1)}, u32[]{:S(2)}, u32[]{:S(2)}) collective-permute-start(bf16[33,32,128]{2,1,0:T(8,128)(2,1)S(1)} %collective-permute-done.11.refs_0_), channel_id=1, source_target_pairs={{0,1},{1,0},{2,3},{3,2},{4,5},{5,4},{6,7},{7,6},{8,9},{9,8},{10,11... | collective-permute-start | bytes 811016 | tf_op jit(solution)/shard_map/ppermute | solution.py:554
  59.6 1.9 %collective-permute-start.14 = (bf16[33,32,128]{2,1,0:T(8,128)(2,1)S(1)}, bf16[33,32,128]{2,1,0:T(8,128)(2,1)S(1)}, u32[]{:S(2)}, u32[]{:S(2)}) collective-permute-start(bf16[33,32,128]{2,1,0:T(8,128)(2,1)S(1)} %collective-permute-done.12.refs_1_), channel_id=1, source_target_pairs={{0,1},{1,0},{2,3},{3,2},{4,5},{5,4},{6,7},{7,6},{8,9},{9,8},{10,11... | collective-permute-start | bytes 811016 | tf_op jit(solution)/shard_map/ppermute | solution.py:554
  63.5 8.1 %collective-permute-start.16 = (bf16[33,32,128]{2,1,0:T(8,128)(2,1)S(1)}, bf16[33,32,128]{2,1,0:T(8,128)(2,1)S(1)}, u32[]{:S(2)}, u32[]{:S(2)}) collective-permute-start(bf16[33,32,128]{2,1,0:T(8,128)(2,1)S(1)} %get-tuple-element.100), channel_id=1, source_target_pairs={{0,2},{2,4},{3,1},{4,6},{5,3},{7,5},{8,10},{10,12},{11,9},{12,14},... | collective-permute-start | bytes 811016 | tf_op jit(solution)/shard_map/ppermute | solution.py:550
  65.4 8.1 %collective-permute-start.15 = (bf16[33,32,128]{2,1,0:T(8,128)(2,1)S(1)}, bf16[33,32,128]{2,1,0:T(8,128)(2,1)S(1)}, u32[]{:S(2)}, u32[]{:S(2)}) collective-permute-start(bf16[33,32,128]{2,1,0:T(8,128)(2,1)S(1)} %get-tuple-element.98), channel_id=1, source_target_pairs={{0,8},{1,25},{2,10},{3,27},{4,12},{5,29},{6,14},{7,31},{8,16},{9,1... | collective-permute-start | bytes 811016 | tf_op jit(solution)/shard_map/ppermute | solution.py:550
  73.5 2.9 %collective-permute-start.17 = (bf16[33,32,128]{2,1,0:T(8,128)(2,1)S(1)}, bf16[33,32,128]{2,1,0:T(8,128)(2,1)S(1)}, u32[]{:S(2)}, u32[]{:S(2)}) collective-permute-start(bf16[33,32,128]{2,1,0:T(8,128)(2,1)S(1)} %collective-permute-done.15.refs_0_), channel_id=1, source_target_pairs={{0,1},{1,0},{2,3},{3,2},{4,5},{5,4},{6,7},{7,6},{8,9},{9,8},{10,11... | collective-permute-start | bytes 811016 | tf_op jit(solution)/shard_map/ppermute | solution.py:554
  75.2 1.6 %collective-permute-start.18 = (bf16[33,32,128]{2,1,0:T(8,128)(2,1)S(1)}, bf16[33,32,128]{2,1,0:T(8,128)(2,1)S(1)}, u32[]{:S(2)}, u32[]{:S(2)}) collective-permute-start(bf16[33,32,128]{2,1,0:T(8,128)(2,1)S(1)} %collective-permute-done.16.refs_1_), channel_id=1, source_target_pairs={{0,1},{1,0},{2,3},{3,2},{4,5},{5,4},{6,7},{7,6},{8,9},{9,8},{10,11... | collective-permute-start | bytes 811016 | tf_op jit(solution)/shard_map/ppermute | solution.py:554
  91.5 1.9 %collective-permute-start.19 = (bf16[65,32,128]{2,1,0:T(8,128)(2,1)S(1)}, bf16[65,32,128]{2,1,0:T(8,128)(2,1)S(1)}, u32[]{:S(2)}, u32[]{:S(2)}) collective-permute-start(bf16[65,32,128]{2,1,0:T(8,128)(2,1)S(1)} %get-tuple-element.104), channel_id=1, source_target_pairs={{0,1},{1,0},{2,3},{3,2},{4,5},{5,4},{6,7},{7,6},{8,9},{9,8},{10,11... | collective-permute-start | bytes 1597448 | tf_op jit(solution)/shard_map/ppermute | solution.py:554
  93.4 3.0 %collective-permute-start.20 = (bf16[3,17,32,128]{3,2,1,0:T(8,128)(2,1)S(1)}, bf16[3,17,32,128]{3,2,1,0:T(8,128)(2,1)S(1)}, u32[]{:S(2)}, u32[]{:S(2)}) collective-permute-start(bf16[3,17,32,128]{3,2,1,0:T(8,128)(2,1)S(1)} %home_slots.3.back), channel_id=1, source_target_pairs={{0,1},{1,0},{2,3},{3,2},{4,5},{5,4},{6,7},{7,6},{8,9},{9,8},{10,11... | collective-permute-start | bytes 1253384 | tf_op jit(solution)/shard_map/ppermute | solution.py:554
  93.9 8.1 %collective-permute-start.22 = (bf16[33,32,128]{2,1,0:T(8,128)(2,1)S(1)}, bf16[33,32,128]{2,1,0:T(8,128)(2,1)S(1)}, u32[]{:S(2)}, u32[]{:S(2)}) collective-permute-start(bf16[33,32,128]{2,1,0:T(8,128)(2,1)S(1)} %get-tuple-element.112), channel_id=1, source_target_pairs={{1,3},{2,0},{3,5},{4,2},{5,7},{6,4},{9,11},{10,8},{11,13},{12,10},... | collective-permute-start | bytes 811016 | tf_op jit(solution)/shard_map/ppermute | solution.py:550
  95.9 9.1 %collective-permute-start.21 = (bf16[33,32,128]{2,1,0:T(8,128)(2,1)S(1)}, bf16[33,32,128]{2,1,0:T(8,128)(2,1)S(1)}, u32[]{:S(2)}, u32[]{:S(2)}) collective-permute-start(bf16[33,32,128]{2,1,0:T(8,128)(2,1)S(1)} %get-tuple-element.110), channel_id=1, source_target_pairs={{0,24},{1,9},{2,26},{3,11},{4,28},{5,13},{6,30},{7,15},{8,0},{9,17... | collective-permute-start | bytes 811016 | tf_op jit(solution)/shard_map/ppermute | solution.py:550
  105.2 1.7 %collective-permute-start.24 = (bf16[33,32,128]{2,1,0:T(8,128)(2,1)S(1)}, bf16[33,32,128]{2,1,0:T(8,128)(2,1)S(1)}, u32[]{:S(2)}, u32[]{:S(2)}) collective-permute-start(bf16[33,32,128]{2,1,0:T(8,128)(2,1)S(1)} %collective-permute-done.22.refs_1_), channel_id=1, source_target_pairs={{0,1},{1,0},{2,3},{3,2},{4,5},{5,4},{6,7},{7,6},{8,9},{9,8},{10,11... | collective-permute-start | bytes 811016 | tf_op jit(solution)/shard_map/ppermute | solution.py:554
  (8 other events, 44.6 us)

commit v5 on v4

--- a/solution.py
+++ b/solution.py
@@ -390,7 +390,8 @@
     def gradients(turn, carry):
         for c in [STRIDE * turn + i for i in range(STRIDE)]:
             k, members, _, _ = read(c)
-            grads = dot(stacks[c], right[k])
+            depth = bands * SIDE
+            grads = dot(stacks[c, :, :depth], right[k, :depth, :])
             for u, v in enumerate(members):
                 top = grads[u * SIDE : u * SIDE + ROWS]
                 low = grads[u * SIDE + ROWS : (u + 1) * SIDE]
@@ -564,8 +565,9 @@
         far = lax.ppermute(mine, "ra", [(0, 2), (1, 3)])
         far, sums = lax.optimization_barrier((far, sums))
         here = jnp.where(lax.axis_index("ra") < 2, mine, far)
-        here, *messages = lax.optimization_barrier((here, *messages))
+        here, messages[0] = lax.optimization_barrier((here, messages[0]))
         near = lax.ppermute(here, "ra", along)
+        near, messages[1] = lax.optimization_barrier((near, messages[1]))
         halves = make_tables((here, near), bands)
         others = (lax.ppermute(here, "dec", across), lax.ppermute(near, "dec", across))
         return make_tables(others, bands, halves), messages, sums

time: 109 us -> 110 us (level); the launches traced: 110 us -> 109 us
  starting transfers between devices: 26.9 us -> 31.8 us
  Pallas kernels: 56.8 us -> 52.8 us
  waiting for transfers between devices: 21.8 us -> 19.6 us
    ppermute x1, waiting for transfers between devices: 4.96 us -> 0.01 us  [all_tables(): lax.ppermute(near, 'dec', across)]
    ppermute x13, starting transfers between devices: 5.86 us -> 10.1 us  [swapped(): return lax.ppermute(value, 'band', [(0, 1), (1, 0)])]
    pallas_call x22, Pallas kernels: 56.8 us -> 52.8 us  [call(): pl.pallas_call(body, out_shape=[jax.ShapeDtypeStruct(shape, dtype) for sh...]
    ppermute x1, waiting for transfers between devices: 0.01 us -> 1.98 us  [all_tables(): near = lax.ppermute(here, 'ra', along)]
  transfers between devices with their start and end apart: 25 -> 25, of which waited for: 14 -> 15; matrix products, arithmetic and copies ran while one was open for 1% -> 1% of each run, Pallas kernels for 20% -> 21%
where the time goes in v5:
time: 110 us; the launch traced here: 109 us
  Pallas kernels  52.8 us (48%)
  starting transfers between devices  31.8 us (29%)
  waiting for transfers between devices  19.6 us (18%)
  local copies, waits for them, and re-layouts  2.3 us (2%)
  other arithmetic  1.21 us (1%)
    pallas_call x22, Pallas kernels, call(): pl.pallas_call(body, out_shape=[jax.ShapeDtypeStruct(shape, dtype) for sh...  52.8 us
    ppermute x8, starting transfers between devices, stepped(): return lax.ppermute(value, ('ra', 'dec', 'band'), pairs)  15.7 us
    ppermute x8, waiting for transfers between devices, stepped(): return lax.ppermute(value, ('ra', 'dec', 'band'), pairs)  11.6 us
    ppermute x13, starting transfers between devices, swapped(): return lax.ppermute(value, 'band', [(0, 1), (1, 0)])  10.1 us
    ppermute x13, waiting for transfers between devices, swapped(): return lax.ppermute(value, 'band', [(0, 1), (1, 0)])  5.96 us
    ppermute x1, starting transfers between devices, all_tables(): far = lax.ppermute(mine, 'ra', [(0, 2), (1, 3)])  4.22 us
    unnamed x16, local copies, waits for them, and re-layouts  2.3 us
  transfers between devices with their start and end apart: 25, of which 15 were waited for; matrix products, arithmetic and copies ran while one was open for 1% of the time, Pallas kernels for 21%

profile of v5, /device:TPU:5, one launch (start us, length us, event | category | flops | bytes accessed | tf_op | source)
XLA Modules:
  0.0 108.6 jit_solution(17743809349554982238)
XLA Ops:
  1.8 4.2 %collective-permute-start.1 = (bf16[3,4,4096]{2,1,0:T(4,128)(2,1)S(1)}, bf16[3,4,4096]{2,1,0:T(4,128)(2,1)S(1)}, u32[]{:S(2)}, u32[]{:S(2)}) collective-permute-start(bf16[3,4,4096]{2,1,0:T(4,128)(2,1)S(1)} %slice_select_fusion), channel_id=1, source_target_pairs={{0,16},{8,24},{1,17},{9,25},{2,18},{10,26},{3,19},{11,27},{4,20},{... | collective-permute-start | bytes 294920 | tf_op jit(solution)/shard_map/ppermute | solution.py:565
  10.6 1.8 %home_sums.2.sums = f32[3,17,32,128]{3,2,1,0:T(8,128)S(1)} custom-call(s32[5,1,128]{2,1,0:T(1,128)S(1)} %bitcast.24, f32[6,128]{1,0:T(8,128)S(1)} %get-tuple-element.63.amps, bf16[128,32,128]{2,1,0:T(8,128)(2,1)S(1)} %bitcast.18), custom_call_target="tpu_custom_call" | custom-call | bytes 4194304 | tf_op jit(solution)/shard_map/home_sums/pallas_call | solution.py:525
  15.1 2.0 %collective-permute-done.3.refs_1_ = bf16[3,4,4096]{2,1,0:T(4,128)(2,1)S(1)} collective-permute-done((bf16[3,4,4096]{2,1,0:T(4,128)(2,1)S(1)}, bf16[3,4,4096]{2,1,0:T(4,128)(2,1)S(1)}, u32[]{:S(2)}, u32[]{:S(2)}) %collective-permute-start.3) | collective-permute-done | bytes 98336 | tf_op jit(solution)/shard_map/ppermute | solution.py:569
  17.3 4.1 %collective-permute-start.6 = (bf16[33,32,128]{2,1,0:T(8,128)(2,1)S(1)}, bf16[33,32,128]{2,1,0:T(8,128)(2,1)S(1)}, u32[]{:S(2)}, u32[]{:S(2)}) collective-permute-start(bf16[33,32,128]{2,1,0:T(8,128)(2,1)S(1)} %get-tuple-element.75), channel_id=1, source_target_pairs={{0,2},{2,4},{3,1},{4,6},{5,3},{7,5},{8,10},{10,12},{11,9},{12,14},... | collective-permute-start | bytes 811016 | tf_op jit(solution)/shard_map/ppermute | solution.py:551
  23.2 1.8 %tables.3 = (bf16[16,64,256]{2,1,0:T(8,128)(2,1)S(1)}, bf16[3,16,64,64]{3,2,1,0:T(8,128)(2,1)S(1)}, bf16[3,16,64,64]{3,2,1,0:T(8,128)(2,1)S(1)}, bf16[16,256,128]{2,1,0:T(8,128)(2,1)S(1)}) custom-call(bf16[3,4,4096]{2,1,0:T(4,128)(2,1)S(1)} %collective-permute-done.2.refs_0_, bf16[3,4,4096]{2,1,0:T(4,128)(2,1)S(1)} %collective-permute-done.4.refs_1_, ...), custom_call_target="tpu_custom_call" | custom-call | flops 2000000000 | bytes 5242880 | tf_op jit(solution)/shard_map/tables/pallas_call | solution.py:525
  25.0 2.1 %collective-permute-done.6.refs_1_ = bf16[33,32,128]{2,1,0:T(8,128)(2,1)S(1)} collective-permute-done((bf16[33,32,128]{2,1,0:T(8,128)(2,1)S(1)}, bf16[33,32,128]{2,1,0:T(8,128)(2,1)S(1)}, u32[]{:S(2)}, u32[]{:S(2)}) %collective-permute-start.6) | collective-permute-done | bytes 270368 | tf_op jit(solution)/shard_map/ppermute | solution.py:551
  27.1 1.9 %collective-permute-start.7 = (bf16[33,32,128]{2,1,0:T(8,128)(2,1)S(1)}, bf16[33,32,128]{2,1,0:T(8,128)(2,1)S(1)}, u32[]{:S(2)}, u32[]{:S(2)}) collective-permute-start(bf16[33,32,128]{2,1,0:T(8,128)(2,1)S(1)} %collective-permute-done.5.refs_0_), channel_id=1, source_target_pairs={{0,1},{1,0},{2,3},{3,2},{4,5},{5,4},{6,7},{7,6},{8,9},{9,8},{10,11... | collective-permute-start | bytes 811016 | tf_op jit(solution)/shard_map/ppermute | solution.py:555
  29.1 2.0 %home_forward.2.refs_4_ = f32[3,16,64,128]{3,2,1,0:T(8,128)S(1)} custom-call(f32[3,17,32,128]{3,2,1,0:T(8,128)S(1)} %home_sums.2.sums, bf16[3,16,32,128]{3,2,1,0:T(8,128)(2,1)S(1)} %bitcast.20, bf16[16,64,256]{2,1,0:T(8,128)(2,1)S(1)} %get-tuple-element.81.first_t.refs_5_, bf16[3,16,64,64]{3,2,1,0:T(8,128)(2,1)S(1)} %get-tuple-element.82.left.refs_6_), custom_call_target="tpu_custom_call" | custom-call | flops 2000000000 | bytes 4194304 | tf_op jit(solution)/shard_map/home_forward/pallas_call | solution.py:525
  31.7 5.4 %forward.2 = (bf16[3,16,64,128]{3,2,1,0:T(8,128)(2,1)S(1)}, bf16[48,3,64,256]{3,2,1,0:T(8,128)(2,1)S(1)}) custom-call(s32[8,256]{1,0:T(8,128)S(1)} %get-tuple-element.78.plan, f32[3,128]{1,0:T(4,128)S(1)} %get-tuple-element.79.amps, bf16[33,32,128]{2,1,0:T(8,128)(2,1)S(1)} %collective-permute-done.5.refs_0_, ...), custom_call_target="tpu_custom_call" | custom-call | flops 3000000000 | bytes 8388608 | tf_op jit(solution)/shard_map/forward/pallas_call | solution.py:525
  37.1 6.7 %backward.2 = (bf16[65,32,128]{2,1,0:T(8,128)(2,1)S(1)}, bf16[65,32,128]{2,1,0:T(8,128)(2,1)S(1)}) custom-call(s32[8,256]{1,0:T(8,128)S(1)} %get-tuple-element.78.plan, f32[3,128]{1,0:T(4,128)S(1)} %get-tuple-element.79.amps, bf16[3,16,64,128]{3,2,1,0:T(8,128)(2,1)S(1)} %get-tuple-element.83.refs_0_.residual, ...), custom_call_target="tpu_custom_call" | custom-call | flops 3000000000 | bytes 8388608 | tf_op jit(solution)/shard_map/backward/pallas_call | solution.py:525
  46.5 1.9 %collective-permute-start.12 = (bf16[33,32,128]{2,1,0:T(8,128)(2,1)S(1)}, bf16[33,32,128]{2,1,0:T(8,128)(2,1)S(1)}, u32[]{:S(2)}, u32[]{:S(2)}) collective-permute-start(bf16[33,32,128]{2,1,0:T(8,128)(2,1)S(1)} %get-tuple-element.95), channel_id=1, source_target_pairs={{1,3},{2,0},{3,5},{4,2},{5,7},{6,4},{9,11},{10,8},{11,13},{12,10},... | collective-permute-start | bytes 811016 | tf_op jit(solution)/shard_map/ppermute | solution.py:551
  48.4 2.6 %collective-permute-start.11 = (bf16[33,32,128]{2,1,0:T(8,128)(2,1)S(1)}, bf16[33,32,128]{2,1,0:T(8,128)(2,1)S(1)}, u32[]{:S(2)}, u32[]{:S(2)}) collective-permute-start(bf16[33,32,128]{2,1,0:T(8,128)(2,1)S(1)} %get-tuple-element.93), channel_id=1, source_target_pairs={{0,24},{1,9},{2,26},{3,11},{4,28},{5,13},{6,30},{7,15},{8,0},{9,17... | collective-permute-start | bytes 811016 | tf_op jit(solution)/shard_map/ppermute | solution.py:551
  51.0 4.5 %home_gather.2 = (f32[128,32,128]{2,1,0:T(8,128)S(1)}, f32[6,128]{1,0:T(8,128)S(1)}) custom-call(s32[5,1,128]{2,1,0:T(1,128)S(1)} %bitcast.25, f32[6,128]{1,0:T(8,128)S(1)} %get-tuple-element.63.amps, f32[1,128]{1,0:T(1,128)S(1)} %bitcast.30, bf16[128,32,128]{2,1,0:T(8,128)(2,1)S(1)} %bitcast.19, bf16[3,17,32,128]{3,2,1,0:T(8,128)(2,1)S(1)} %home_slots.2.back, ...), custom_call_target="tpu_custom_call" | custom-call | bytes 4194304 | tf_op jit(solution)/shard_map/home_gather/pallas_call | solution.py:525
  60.8 2.0 %update.2 = (f32[128,32,128]{2,1,0:T(8,128)S(1)}, f32[6,128]{1,0:T(8,128)S(1)}, f32[6,128]{1,0:T(8,128)S(1)}, bf16[33,32,128]{2,1,0:T(8,128)(2,1)S(1)}, bf16[33,32,128]{2,1,0:T(8,128)(2,1)S(1)}) custom-call(s32[8,128]{1,0:T(8,128)S(1)} %get-tuple-element.60.places, f32[1,128]{1,0:T(1,128)S(1)} %bitcast.31, s32[5,1,128]{2,1,0:T(1,128)S(1)} %bitcast.26, ...), custom_call_target="tpu_custom_call" | custom-call | bytes 3145728 | tf_op jit(solution)/shard_map/update/pallas_call | solution.py:525
  62.9 1.9 %collective-permute-start.16 = (bf16[33,32,128]{2,1,0:T(8,128)(2,1)S(1)}, bf16[33,32,128]{2,1,0:T(8,128)(2,1)S(1)}, u32[]{:S(2)}, u32[]{:S(2)}) collective-permute-start(bf16[33,32,128]{2,1,0:T(8,128)(2,1)S(1)} %get-tuple-element.102), channel_id=1, source_target_pairs={{0,2},{2,4},{3,1},{4,6},{5,3},{7,5},{8,10},{10,12},{11,9},{12,14},... | collective-permute-start | bytes 811016 | tf_op jit(solution)/shard_map/ppermute | solution.py:551
  64.8 2.3 %collective-permute-start.15 = (bf16[33,32,128]{2,1,0:T(8,128)(2,1)S(1)}, bf16[33,32,128]{2,1,0:T(8,128)(2,1)S(1)}, u32[]{:S(2)}, u32[]{:S(2)}) collective-permute-start(bf16[33,32,128]{2,1,0:T(8,128)(2,1)S(1)} %get-tuple-element.100), channel_id=1, source_target_pairs={{0,8},{1,25},{2,10},{3,27},{4,12},{5,29},{6,14},{7,31},{8,16},{9,1... | collective-permute-start | bytes 811016 | tf_op jit(solution)/shard_map/ppermute | solution.py:551
  69.0 2.0 %home_forward.3.refs_4_ = f32[3,16,64,128]{3,2,1,0:T(8,128)S(1)} custom-call(f32[3,17,32,128]{3,2,1,0:T(8,128)S(1)} %home_sums.3.sums, bf16[3,16,32,128]{3,2,1,0:T(8,128)(2,1)S(1)} %bitcast.21, bf16[16,64,256]{2,1,0:T(8,128)(2,1)S(1)} %get-tuple-element.81.first_t.refs_5_, bf16[3,16,64,64]{3,2,1,0:T(8,128)(2,1)S(1)} %get-tuple-element.82.left.refs_6_), custom_call_target="tpu_custom_call" | custom-call | flops 2000000000 | bytes 4194304 | tf_op jit(solution)/shard_map/home_forward/pallas_call | solution.py:525
  71.9 2.7 %collective-permute-start.17 = (bf16[33,32,128]{2,1,0:T(8,128)(2,1)S(1)}, bf16[33,32,128]{2,1,0:T(8,128)(2,1)S(1)}, u32[]{:S(2)}, u32[]{:S(2)}) collective-permute-start(bf16[33,32,128]{2,1,0:T(8,128)(2,1)S(1)} %collective-permute-done.15.refs_0_), channel_id=1, source_target_pairs={{0,1},{1,0},{2,3},{3,2},{4,5},{5,4},{6,7},{7,6},{8,9},{9,8},{10,11... | collective-permute-start | bytes 811016 | tf_op jit(solution)/shard_map/ppermute | solution.py:555
  76.2 5.6 %forward.3 = (bf16[3,16,64,128]{3,2,1,0:T(8,128)(2,1)S(1)}, bf16[48,3,64,256]{3,2,1,0:T(8,128)(2,1)S(1)}) custom-call(s32[8,256]{1,0:T(8,128)S(1)} %get-tuple-element.78.plan, f32[3,128]{1,0:T(4,128)S(1)} %order.3.amps, bf16[33,32,128]{2,1,0:T(8,128)(2,1)S(1)} %collective-permute-done.15.refs_0_, bf16[33,32,128]{2,1,0:T(8,128)(2,1)S(1)} %collective-permute-done.16.refs_1_, ...), custom_call_target="tpu_custom_call" | custom-call | flops 3000000000 | bytes 8388608 | tf_op jit(solution)/shard_map/forward/pallas_call | solution.py:525
  81.8 6.8 %backward.3 = (bf16[65,32,128]{2,1,0:T(8,128)(2,1)S(1)}, bf16[65,32,128]{2,1,0:T(8,128)(2,1)S(1)}) custom-call(s32[8,256]{1,0:T(8,128)S(1)} %get-tuple-element.78.plan, f32[3,128]{1,0:T(4,128)S(1)} %order.3.amps, bf16[3,16,64,128]{3,2,1,0:T(8,128)(2,1)S(1)} %get-tuple-element.104.refs_0_.residual, bf16[48,3,64,256]{3,2,1,0:T(8,128)(2,1)S(1)} %get-tuple-element.105.refs_1_, ...), custom_call_target="tpu_custom_call" | custom-call | flops 3000000000 | bytes 8388608 | tf_op jit(solution)/shard_map/backward/pallas_call | solution.py:525
  91.1 1.9 %collective-permute-start.22 = (bf16[33,32,128]{2,1,0:T(8,128)(2,1)S(1)}, bf16[33,32,128]{2,1,0:T(8,128)(2,1)S(1)}, u32[]{:S(2)}, u32[]{:S(2)}) collective-permute-start(bf16[33,32,128]{2,1,0:T(8,128)(2,1)S(1)} %get-tuple-element.114), channel_id=1, source_target_pairs={{1,3},{2,0},{3,5},{4,2},{5,7},{6,4},{9,11},{10,8},{11,13},{12,10},... | collective-permute-start | bytes 811016 | tf_op jit(solution)/shard_map/ppermute | solution.py:551
  93.1 3.0 %home_gather.3 = (f32[128,16,128]{2,1,0:T(8,128)S(1)}, f32[3,128]{1,0:T(4,128)S(1)}) custom-call(s32[5,1,128]{2,1,0:T(1,128)S(1)} %bitcast.28, f32[6,128]{1,0:T(8,128)S(1)} %get-tuple-element.98.amps, f32[1,128]{1,0:T(1,128)S(1)} %bitcast.32, f32[128,32,128]{2,1,0:T(8,128)S(1)} %get-tuple-element.99.morph, bf16[3,17,32,128]{3,2,1,0:T(8,128)(2,1)S(1)} %home_slots.3.back, ...), custom_call_target="tpu_custom_call" | custom-call | bytes 4194304 | tf_op jit(solution)/shard_map/home_gather/pallas_call | solution.py:525
  96.1 5.5 %collective-permute-done.22.refs_1_ = bf16[33,32,128]{2,1,0:T(8,128)(2,1)S(1)} collective-permute-done((bf16[33,32,128]{2,1,0:T(8,128)(2,1)S(1)}, bf16[33,32,128]{2,1,0:T(8,128)(2,1)S(1)}, u32[]{:S(2)}, u32[]{:S(2)}) %collective-permute-start.22) | collective-permute-done | bytes 270368 | tf_op jit(solution)/shard_map/ppermute | solution.py:551
  105.4 3.2 %update.3 = (f32[128,2048]{1,0:T(8,128)}, f32[3,1,128]{2,1,0:T(1,128)}) custom-call(s32[8,128]{1,0:T(8,128)S(1)} %get-tuple-element.60.places, f32[1,128]{1,0:T(1,128)S(1)} %bitcast.33, s32[5,1,128]{2,1,0:T(1,128)S(1)} %bitcast.29, f32[1,128]{1,0:T(1,128)S(1)} %bitcast.35, bf16[4,128,128]{2,1,0:T(8,128)(2,1)S(1)} %get-tuple-element.61.hots, ...), custom_call_target="tpu_custom_call" | custom-call | bytes 3145728 | tf_op jit(solution)/shard_map/update/pallas_call | solution.py:525
  (66 shorter events, 29.5 us)
Async XLA Ops:
  1.8 10.7 %collective-permute-start.1 = (bf16[3,4,4096]{2,1,0:T(4,128)(2,1)S(1)}, bf16[3,4,4096]{2,1,0:T(4,128)(2,1)S(1)}, u32[]{:S(2)}, u32[]{:S(2)}) collective-permute-start(bf16[3,4,4096]{2,1,0:T(4,128)(2,1)S(1)} %slice_select_fusion), channel_id=1, source_target_pairs={{0,16},{8,24},{1,17},{9,25},{2,18},{10,26},{3,19},{11,27},{4,20},{... | collective-permute-start | bytes 294920 | tf_op jit(solution)/shard_map/ppermute | solution.py:565
  6.0 3.5 %collective-permute-start = (f32[3,1,128]{2,1,0:T(1,128)}, f32[3,1,128]{2,1,0:T(1,128)S(1)}, u32[]{:S(2)}, u32[]{:S(2)}) collective-permute-start(f32[3,1,128]{2,1,0:T(1,128)} %bitcast.36), channel_id=1, source_target_pairs={{0,1},{1,0},{2,3},{3,2},{4,5},{5,4},{6,7},{7,6},{8,9},{9,8},{10,11... | collective-permute-start | bytes 4616 | tf_op jit(solution)/shard_map/ppermute | solution.py:555
  12.6 4.5 %collective-permute-start.3 = (bf16[3,4,4096]{2,1,0:T(4,128)(2,1)S(1)}, bf16[3,4,4096]{2,1,0:T(4,128)(2,1)S(1)}, u32[]{:S(2)}, u32[]{:S(2)}) collective-permute-start(bf16[3,4,4096]{2,1,0:T(4,128)(2,1)S(1)} %broadcast_select_fusion.refs_0_), channel_id=1, source_target_pairs={{0,8},{8,0},{16,24},{24,16},{1,9},{9,1},{17,25},{25,17},{2,10},{10... | collective-permute-start | bytes 294920 | tf_op jit(solution)/shard_map/ppermute | solution.py:569
  13.9 9.2 %collective-permute-start.2 = (bf16[3,4,4096]{2,1,0:T(4,128)(2,1)S(1)}, bf16[3,4,4096]{2,1,0:T(4,128)(2,1)S(1)}, u32[]{:S(2)}, u32[]{:S(2)}) collective-permute-start(bf16[3,4,4096]{2,1,0:T(4,128)(2,1)S(1)} %broadcast_select_fusion.refs_0_), channel_id=1, source_target_pairs={{0,4},{2,6},{4,0},{6,2},{1,5},{3,7},{5,1},{7,3},{8,12},{10,14},{12... | collective-permute-start | bytes 294920 | tf_op jit(solution)/shard_map/ppermute | solution.py:572
  14.2 10.9 %collective-permute-start.5 = (bf16[33,32,128]{2,1,0:T(8,128)(2,1)S(1)}, bf16[33,32,128]{2,1,0:T(8,128)(2,1)S(1)}, u32[]{:S(2)}, u32[]{:S(2)}) collective-permute-start(bf16[33,32,128]{2,1,0:T(8,128)(2,1)S(1)} %get-tuple-element.74), channel_id=1, source_target_pairs={{0,8},{1,25},{2,10},{3,27},{4,12},{5,29},{6,14},{7,31},{8,16},{9,1... | collective-permute-start | bytes 811016 | tf_op jit(solution)/shard_map/ppermute | solution.py:551
  17.0 6.1 %collective-permute-start.4 = (bf16[3,4,4096]{2,1,0:T(4,128)(2,1)S(1)}, bf16[3,4,4096]{2,1,0:T(4,128)(2,1)S(1)}, u32[]{:S(2)}, u32[]{:S(2)}) collective-permute-start(bf16[3,4,4096]{2,1,0:T(4,128)(2,1)S(1)} %collective-permute-done.3.refs_1_), channel_id=1, source_target_pairs={{0,4},{2,6},{4,0},{6,2},{1,5},{3,7},{5,1},{7,3},{8,12},{10,14},{12... | collective-permute-start | bytes 294920 | tf_op jit(solution)/shard_map/ppermute | solution.py:572
  17.3 9.8 %collective-permute-start.6 = (bf16[33,32,128]{2,1,0:T(8,128)(2,1)S(1)}, bf16[33,32,128]{2,1,0:T(8,128)(2,1)S(1)}, u32[]{:S(2)}, u32[]{:S(2)}) collective-permute-start(bf16[33,32,128]{2,1,0:T(8,128)(2,1)S(1)} %get-tuple-element.75), channel_id=1, source_target_pairs={{0,2},{2,4},{3,1},{4,6},{5,3},{7,5},{8,10},{10,12},{11,9},{12,14},... | collective-permute-start | bytes 811016 | tf_op jit(solution)/shard_map/ppermute | solution.py:551
  27.1 4.0 %collective-permute-start.7 = (bf16[33,32,128]{2,1,0:T(8,128)(2,1)S(1)}, bf16[33,32,128]{2,1,0:T(8,128)(2,1)S(1)}, u32[]{:S(2)}, u32[]{:S(2)}) collective-permute-start(bf16[33,32,128]{2,1,0:T(8,128)(2,1)S(1)} %collective-permute-done.5.refs_0_), channel_id=1, source_target_pairs={{0,1},{1,0},{2,3},{3,2},{4,5},{5,4},{6,7},{7,6},{8,9},{9,8},{10,11... | collective-permute-start | bytes 811016 | tf_op jit(solution)/shard_map/ppermute | solution.py:555
  29.0 2.1 %collective-permute-start.8 = (bf16[33,32,128]{2,1,0:T(8,128)(2,1)S(1)}, bf16[33,32,128]{2,1,0:T(8,128)(2,1)S(1)}, u32[]{:S(2)}, u32[]{:S(2)}) collective-permute-start(bf16[33,32,128]{2,1,0:T(8,128)(2,1)S(1)} %collective-permute-done.6.refs_1_), channel_id=1, source_target_pairs={{0,1},{1,0},{2,3},{3,2},{4,5},{5,4},{6,7},{7,6},{8,9},{9,8},{10,11... | collective-permute-start | bytes 811016 | tf_op jit(solution)/shard_map/ppermute | solution.py:555
  43.9 2.1 %collective-permute-start.9 = (bf16[65,32,128]{2,1,0:T(8,128)(2,1)S(1)}, bf16[65,32,128]{2,1,0:T(8,128)(2,1)S(1)}, u32[]{:S(2)}, u32[]{:S(2)}) collective-permute-start(bf16[65,32,128]{2,1,0:T(8,128)(2,1)S(1)} %get-tuple-element.87), channel_id=1, source_target_pairs={{0,1},{1,0},{2,3},{3,2},{4,5},{5,4},{6,7},{7,6},{8,9},{9,8},{10,11... | collective-permute-start | bytes 1597448 | tf_op jit(solution)/shard_map/ppermute | solution.py:555
  46.0 5.0 %collective-permute-start.10 = (bf16[3,17,32,128]{3,2,1,0:T(8,128)(2,1)S(1)}, bf16[3,17,32,128]{3,2,1,0:T(8,128)(2,1)S(1)}, u32[]{:S(2)}, u32[]{:S(2)}) collective-permute-start(bf16[3,17,32,128]{3,2,1,0:T(8,128)(2,1)S(1)} %home_slots.2.back), channel_id=1, source_target_pairs={{0,1},{1,0},{2,3},{3,2},{4,5},{5,4},{6,7},{7,6},{8,9},{9,8},{10,11... | collective-permute-start | bytes 1253384 | tf_op jit(solution)/shard_map/ppermute | solution.py:555
  46.5 10.2 %collective-permute-start.12 = (bf16[33,32,128]{2,1,0:T(8,128)(2,1)S(1)}, bf16[33,32,128]{2,1,0:T(8,128)(2,1)S(1)}, u32[]{:S(2)}, u32[]{:S(2)}) collective-permute-start(bf16[33,32,128]{2,1,0:T(8,128)(2,1)S(1)} %get-tuple-element.95), channel_id=1, source_target_pairs={{1,3},{2,0},{3,5},{4,2},{5,7},{6,4},{9,11},{10,8},{11,13},{12,10},... | collective-permute-start | bytes 811016 | tf_op jit(solution)/shard_map/ppermute | solution.py:551
  48.4 9.6 %collective-permute-start.11 = (bf16[33,32,128]{2,1,0:T(8,128)(2,1)S(1)}, bf16[33,32,128]{2,1,0:T(8,128)(2,1)S(1)}, u32[]{:S(2)}, u32[]{:S(2)}) collective-permute-start(bf16[33,32,128]{2,1,0:T(8,128)(2,1)S(1)} %get-tuple-element.93), channel_id=1, source_target_pairs={{0,24},{1,9},{2,26},{3,11},{4,28},{5,13},{6,30},{7,15},{8,0},{9,17... | collective-permute-start | bytes 811016 | tf_op jit(solution)/shard_map/ppermute | solution.py:551
  58.0 2.4 %collective-permute-start.13 = (bf16[33,32,128]{2,1,0:T(8,128)(2,1)S(1)}, bf16[33,32,128]{2,1,0:T(8,128)(2,1)S(1)}, u32[]{:S(2)}, u32[]{:S(2)}) collective-permute-start(bf16[33,32,128]{2,1,0:T(8,128)(2,1)S(1)} %collective-permute-done.11.refs_0_), channel_id=1, source_target_pairs={{0,1},{1,0},{2,3},{3,2},{4,5},{5,4},{6,7},{7,6},{8,9},{9,8},{10,11... | collective-permute-start | bytes 811016 | tf_op jit(solution)/shard_map/ppermute | solution.py:555
  59.3 1.6 %collective-permute-start.14 = (bf16[33,32,128]{2,1,0:T(8,128)(2,1)S(1)}, bf16[33,32,128]{2,1,0:T(8,128)(2,1)S(1)}, u32[]{:S(2)}, u32[]{:S(2)}) collective-permute-start(bf16[33,32,128]{2,1,0:T(8,128)(2,1)S(1)} %collective-permute-done.12.refs_1_), channel_id=1, source_target_pairs={{0,1},{1,0},{2,3},{3,2},{4,5},{5,4},{6,7},{7,6},{8,9},{9,8},{10,11... | collective-permute-start | bytes 811016 | tf_op jit(solution)/shard_map/ppermute | solution.py:555
  62.9 8.2 %collective-permute-start.16 = (bf16[33,32,128]{2,1,0:T(8,128)(2,1)S(1)}, bf16[33,32,128]{2,1,0:T(8,128)(2,1)S(1)}, u32[]{:S(2)}, u32[]{:S(2)}) collective-permute-start(bf16[33,32,128]{2,1,0:T(8,128)(2,1)S(1)} %get-tuple-element.102), channel_id=1, source_target_pairs={{0,2},{2,4},{3,1},{4,6},{5,3},{7,5},{8,10},{10,12},{11,9},{12,14},... | collective-permute-start | bytes 811016 | tf_op jit(solution)/shard_map/ppermute | solution.py:551
  64.8 7.1 %collective-permute-start.15 = (bf16[33,32,128]{2,1,0:T(8,128)(2,1)S(1)}, bf16[33,32,128]{2,1,0:T(8,128)(2,1)S(1)}, u32[]{:S(2)}, u32[]{:S(2)}) collective-permute-start(bf16[33,32,128]{2,1,0:T(8,128)(2,1)S(1)} %get-tuple-element.100), channel_id=1, source_target_pairs={{0,8},{1,25},{2,10},{3,27},{4,12},{5,29},{6,14},{7,31},{8,16},{9,1... | collective-permute-start | bytes 811016 | tf_op jit(solution)/shard_map/ppermute | solution.py:551
  71.9 3.9 %collective-permute-start.17 = (bf16[33,32,128]{2,1,0:T(8,128)(2,1)S(1)}, bf16[33,32,128]{2,1,0:T(8,128)(2,1)S(1)}, u32[]{:S(2)}, u32[]{:S(2)}) collective-permute-start(bf16[33,32,128]{2,1,0:T(8,128)(2,1)S(1)} %collective-permute-done.15.refs_0_), channel_id=1, source_target_pairs={{0,1},{1,0},{2,3},{3,2},{4,5},{5,4},{6,7},{7,6},{8,9},{9,8},{10,11... | collective-permute-start | bytes 811016 | tf_op jit(solution)/shard_map/ppermute | solution.py:555
  74.6 1.6 %collective-permute-start.18 = (bf16[33,32,128]{2,1,0:T(8,128)(2,1)S(1)}, bf16[33,32,128]{2,1,0:T(8,128)(2,1)S(1)}, u32[]{:S(2)}, u32[]{:S(2)}) collective-permute-start(bf16[33,32,128]{2,1,0:T(8,128)(2,1)S(1)} %collective-permute-done.16.refs_1_), channel_id=1, source_target_pairs={{0,1},{1,0},{2,3},{3,2},{4,5},{5,4},{6,7},{7,6},{8,9},{9,8},{10,11... | collective-permute-start | bytes 811016 | tf_op jit(solution)/shard_map/ppermute | solution.py:555
  88.6 1.9 %collective-permute-start.19 = (bf16[65,32,128]{2,1,0:T(8,128)(2,1)S(1)}, bf16[65,32,128]{2,1,0:T(8,128)(2,1)S(1)}, u32[]{:S(2)}, u32[]{:S(2)}) collective-permute-start(bf16[65,32,128]{2,1,0:T(8,128)(2,1)S(1)} %get-tuple-element.106), channel_id=1, source_target_pairs={{0,1},{1,0},{2,3},{3,2},{4,5},{5,4},{6,7},{7,6},{8,9},{9,8},{10,11... | collective-permute-start | bytes 1597448 | tf_op jit(solution)/shard_map/ppermute | solution.py:555
  90.6 2.5 %collective-permute-start.20 = (bf16[3,17,32,128]{3,2,1,0:T(8,128)(2,1)S(1)}, bf16[3,17,32,128]{3,2,1,0:T(8,128)(2,1)S(1)}, u32[]{:S(2)}, u32[]{:S(2)}) collective-permute-start(bf16[3,17,32,128]{3,2,1,0:T(8,128)(2,1)S(1)} %home_slots.3.back), channel_id=1, source_target_pairs={{0,1},{1,0},{2,3},{3,2},{4,5},{5,4},{6,7},{7,6},{8,9},{9,8},{10,11... | collective-permute-start | bytes 1253384 | tf_op jit(solution)/shard_map/ppermute | solution.py:555
  91.1 10.5 %collective-permute-start.22 = (bf16[33,32,128]{2,1,0:T(8,128)(2,1)S(1)}, bf16[33,32,128]{2,1,0:T(8,128)(2,1)S(1)}, u32[]{:S(2)}, u32[]{:S(2)}) collective-permute-start(bf16[33,32,128]{2,1,0:T(8,128)(2,1)S(1)} %get-tuple-element.114), channel_id=1, source_target_pairs={{1,3},{2,0},{3,5},{4,2},{5,7},{6,4},{9,11},{10,8},{11,13},{12,10},... | collective-permute-start | bytes 811016 | tf_op jit(solution)/shard_map/ppermute | solution.py:551
  93.0 9.3 %collective-permute-start.21 = (bf16[33,32,128]{2,1,0:T(8,128)(2,1)S(1)}, bf16[33,32,128]{2,1,0:T(8,128)(2,1)S(1)}, u32[]{:S(2)}, u32[]{:S(2)}) collective-permute-start(bf16[33,32,128]{2,1,0:T(8,128)(2,1)S(1)} %get-tuple-element.112), channel_id=1, source_target_pairs={{0,24},{1,9},{2,26},{3,11},{4,28},{5,13},{6,30},{7,15},{8,0},{9,17... | collective-permute-start | bytes 811016 | tf_op jit(solution)/shard_map/ppermute | solution.py:551
  102.3 2.7 %collective-permute-start.23 = (bf16[33,32,128]{2,1,0:T(8,128)(2,1)S(1)}, bf16[33,32,128]{2,1,0:T(8,128)(2,1)S(1)}, u32[]{:S(2)}, u32[]{:S(2)}) collective-permute-start(bf16[33,32,128]{2,1,0:T(8,128)(2,1)S(1)} %collective-permute-done.21.refs_0_), channel_id=1, source_target_pairs={{0,1},{1,0},{2,3},{3,2},{4,5},{5,4},{6,7},{7,6},{8,9},{9,8},{10,11... | collective-permute-start | bytes 811016 | tf_op jit(solution)/shard_map/ppermute | solution.py:555
  (8 other events, 51.2 us)

commit v6 on v5

--- a/solution.py
+++ b/solution.py
@@ -555,7 +555,7 @@
     return lax.ppermute(value, "band", [(0, 1), (1, 0)])
 
 
-def all_tables(psf, num_slots, messages, sums):
+def all_tables(psf, num_slots, stamps, sums):
     bands, held = psf.shape[:2]
     lines = lax.axis_size("dec")
     if lax.axis_size("ra") == 4 and 2 * held == num_slots and held % 2 == 0 and lines % 2 == 0:
@@ -565,13 +565,13 @@
         far = lax.ppermute(mine, "ra", [(0, 2), (1, 3)])
         far, sums = lax.optimization_barrier((far, sums))
         here = jnp.where(lax.axis_index("ra") < 2, mine, far)
-        here, messages[0] = lax.optimization_barrier((here, messages[0]))
+        here_across = lax.ppermute(here, "dec", across)
+        here, *stamps = lax.optimization_barrier((here, *stamps))
         near = lax.ppermute(here, "ra", along)
-        near, messages[1] = lax.optimization_barrier((near, messages[1]))
         halves = make_tables((here, near), bands)
-        others = (lax.ppermute(here, "dec", across), lax.ppermute(near, "dec", across))
-        return make_tables(others, bands, halves), messages, sums
-    return make_tables((lax.all_gather(psf, "ra", axis=1, tiled=True)[:, :num_slots],), bands), messages, sums
+        others = (here_across, lax.ppermute(near, "dec", across))
+        return make_tables(others, bands, halves), stamps, sums
+    return make_tables((lax.all_gather(psf, "ra", axis=1, tiled=True)[:, :num_slots],), bands), stamps, sums
 
 
 def shards(morphology, sed_amps, slot_lists, morph_step, sed_step, psf_kernels, observed):
@@ -615,15 +615,14 @@
         )[0]
 
     sums = home_sums(amps_q, full)
-    tables, messages, sums = all_tables(psf_kernels, num_slots, messages, sums)
+    own = [stepped(messages[0], "ra", 1), stepped(messages[1], "dec", 1)]
+    tables, own, sums = all_tables(psf_kernels, num_slots, own, sums)
     first_t, left, left_t, right = tables
     morph, plan = full, None
     for sweep in range(ITERS):
         last = sweep == ITERS - 1
-        own = [stepped(messages[0], "ra", 1), stepped(messages[1], "dec", 1)]
-        if sweep == 0:
-            left, *own = lax.optimization_barrier((left, *own))
-        else:
+        if sweep > 0:
+            own = [stepped(messages[0], "ra", 1), stepped(messages[1], "dec", 1)]
             sums = home_sums(amps_q, morph)
         home = call(
             functools.partial(home_forward_kernel, bands),

time: 110 us -> 114 us (1.036)
  waiting for transfers between devices: 19.6 us -> 23.8 us
    ppermute x8, waiting for transfers between devices: 11.6 us -> 16.5 us  [stepped(): return lax.ppermute(value, ('ra', 'dec', 'band'), pairs)]
    ppermute x1, waiting for transfers between devices: 1.98 us -> 0.01 us  [all_tables(): near = lax.ppermute(here, 'ra', along)]
    ppermute x8, starting transfers between devices: 15.7 us -> 14 us  [stepped(): return lax.ppermute(value, ('ra', 'dec', 'band'), pairs)]
    ppermute x2, waiting for transfers between devices: 0.01 us -> 1.38 us  [the longest x1 1.38 us: all_tables(): others = (here_across, lax.ppermute(near, 'dec', across))]
    ppermute x2, starting transfers between devices: 0.49 us -> 1.66 us  [the longest x1 1.59 us: all_tables(): others = (here_across, lax.ppermute(near, 'dec', across))]
  transfers between devices with their start and end apart: 25 -> 25, of which waited for: 15 -> 13; matrix products, arithmetic and copies ran while one was open for 1% -> 1% of each run, Pallas kernels for 21% -> 20%
where the time goes in v6:
time: 114 us; the launch traced here: 113 us
  Pallas kernels  52.7 us (46%)
  starting transfers between devices  32 us (28%)
  waiting for transfers between devices  23.8 us (21%)
  local copies, waits for them, and re-layouts  2.3 us (2%)
  other arithmetic  1.21 us (1%)
    pallas_call x22, Pallas kernels, call(): pl.pallas_call(body, out_shape=[jax.ShapeDtypeStruct(shape, dtype) for sh...  52.7 us
    ppermute x8, waiting for transfers between devices, stepped(): return lax.ppermute(value, ('ra', 'dec', 'band'), pairs)  16.5 us
    ppermute x8, starting transfers between devices, stepped(): return lax.ppermute(value, ('ra', 'dec', 'band'), pairs)  14 us
    ppermute x13, starting transfers between devices, swapped(): return lax.ppermute(value, 'band', [(0, 1), (1, 0)])  10.1 us
    ppermute x13, waiting for transfers between devices, swapped(): return lax.ppermute(value, 'band', [(0, 1), (1, 0)])  5.91 us
    ppermute x1, starting transfers between devices, all_tables(): far = lax.ppermute(mine, 'ra', [(0, 2), (1, 3)])  4.22 us
    unnamed x16, local copies, waits for them, and re-layouts  2.3 us
  transfers between devices with their start and end apart: 25, of which 13 were waited for; matrix products, arithmetic and copies ran while one was open for 1% of the time, Pallas kernels for 20%

profile of v6, /device:TPU:5, one launch (start us, length us, event | category | flops | bytes accessed | tf_op | source)
XLA Modules:
  0.0 112.9 jit_solution(16991945639052128302)
XLA Ops:
  1.8 4.2 %collective-permute-start.1 = (bf16[3,4,4096]{2,1,0:T(4,128)(2,1)S(1)}, bf16[3,4,4096]{2,1,0:T(4,128)(2,1)S(1)}, u32[]{:S(2)}, u32[]{:S(2)}) collective-permute-start(bf16[3,4,4096]{2,1,0:T(4,128)(2,1)S(1)} %slice_select_fusion), channel_id=1, source_target_pairs={{0,16},{8,24},{1,17},{9,25},{2,18},{10,26},{3,19},{11,27},{4,20},{... | collective-permute-start | bytes 294920 | tf_op jit(solution)/shard_map/ppermute | solution.py:565
  10.7 3.1 %collective-permute-start.3 = (bf16[33,32,128]{2,1,0:T(8,128)(2,1)S(1)}, bf16[33,32,128]{2,1,0:T(8,128)(2,1)S(1)}, u32[]{:S(2)}, u32[]{:S(2)}) collective-permute-start(bf16[33,32,128]{2,1,0:T(8,128)(2,1)S(1)} %get-tuple-element.62), channel_id=1, source_target_pairs={{0,2},{2,4},{3,1},{4,6},{5,3},{7,5},{8,10},{10,12},{11,9},{12,14},... | collective-permute-start | bytes 811016 | tf_op jit(solution)/shard_map/ppermute | solution.py:551
  15.7 3.4 %collective-permute-done.2.refs_0_ = bf16[33,32,128]{2,1,0:T(8,128)(2,1)S(1)} collective-permute-done((bf16[33,32,128]{2,1,0:T(8,128)(2,1)S(1)}, bf16[33,32,128]{2,1,0:T(8,128)(2,1)S(1)}, u32[]{:S(2)}, u32[]{:S(2)}) %collective-permute-start.2) | collective-permute-done | bytes 270368 | tf_op jit(solution)/shard_map/ppermute | solution.py:551
  19.1 2.0 %collective-permute-start.7 = (bf16[3,4,4096]{2,1,0:T(4,128)(2,1)S(1)}, bf16[3,4,4096]{2,1,0:T(4,128)(2,1)S(1)}, u32[]{:S(2)}, u32[]{:S(2)}) collective-permute-start(bf16[3,4,4096]{2,1,0:T(4,128)(2,1)S(1)} %broadcast_select_fusion.refs_0_), channel_id=1, source_target_pairs={{0,8},{8,0},{16,24},{24,16},{1,9},{9,1},{17,25},{25,17},{2,10},{10... | collective-permute-start | bytes 294920 | tf_op jit(solution)/shard_map/ppermute | solution.py:570
  21.3 2.0 %collective-permute-start.4 = (bf16[33,32,128]{2,1,0:T(8,128)(2,1)S(1)}, bf16[33,32,128]{2,1,0:T(8,128)(2,1)S(1)}, u32[]{:S(2)}, u32[]{:S(2)}) collective-permute-start(bf16[33,32,128]{2,1,0:T(8,128)(2,1)S(1)} %collective-permute-done.2.refs_0_), channel_id=1, source_target_pairs={{0,1},{1,0},{2,3},{3,2},{4,5},{5,4},{6,7},{7,6},{8,9},{9,8},{10,11... | collective-permute-start | bytes 811016 | tf_op jit(solution)/shard_map/ppermute | solution.py:555
  28.2 1.8 %tables.3 = (bf16[16,64,256]{2,1,0:T(8,128)(2,1)S(1)}, bf16[3,16,64,64]{3,2,1,0:T(8,128)(2,1)S(1)}, bf16[3,16,64,64]{3,2,1,0:T(8,128)(2,1)S(1)}, bf16[16,256,128]{2,1,0:T(8,128)(2,1)S(1)}) custom-call(bf16[3,4,4096]{2,1,0:T(4,128)(2,1)S(1)} %collective-permute-done.6.refs_0_, bf16[3,4,4096]{2,1,0:T(4,128)(2,1)S(1)} %collective-permute-done.8.refs_1_, ...), custom_call_target="tpu_custom_call" | custom-call | flops 2000000000 | bytes 5242880 | tf_op jit(solution)/shard_map/tables/pallas_call | solution.py:525
  30.0 2.0 %home_forward.2.refs_4_ = f32[3,16,64,128]{3,2,1,0:T(8,128)S(1)} custom-call(f32[3,17,32,128]{3,2,1,0:T(8,128)S(1)} %home_sums.2.sums, bf16[3,16,32,128]{3,2,1,0:T(8,128)(2,1)S(1)} %bitcast.20, bf16[16,64,256]{2,1,0:T(8,128)(2,1)S(1)} %get-tuple-element.73.first_t.refs_5_, bf16[3,16,64,64]{3,2,1,0:T(8,128)(2,1)S(1)} %get-tuple-element.74.left.refs_6_), custom_call_target="tpu_custom_call" | custom-call | flops 2000000000 | bytes 4194304 | tf_op jit(solution)/shard_map/home_forward/pallas_call | solution.py:525
  32.6 5.4 %forward.2 = (bf16[3,16,64,128]{3,2,1,0:T(8,128)(2,1)S(1)}, bf16[48,3,64,256]{3,2,1,0:T(8,128)(2,1)S(1)}) custom-call(s32[8,256]{1,0:T(8,128)S(1)} %get-tuple-element.65.plan, f32[3,128]{1,0:T(4,128)S(1)} %get-tuple-element.66.amps, bf16[33,32,128]{2,1,0:T(8,128)(2,1)S(1)} %collective-permute-done.2.refs_0_, ...), custom_call_target="tpu_custom_call" | custom-call | flops 3000000000 | bytes 8388608 | tf_op jit(solution)/shard_map/forward/pallas_call | solution.py:525
  38.0 6.8 %backward.2 = (bf16[65,32,128]{2,1,0:T(8,128)(2,1)S(1)}, bf16[65,32,128]{2,1,0:T(8,128)(2,1)S(1)}) custom-call(s32[8,256]{1,0:T(8,128)S(1)} %get-tuple-element.65.plan, f32[3,128]{1,0:T(4,128)S(1)} %get-tuple-element.66.amps, bf16[3,16,64,128]{3,2,1,0:T(8,128)(2,1)S(1)} %get-tuple-element.75.refs_0_.residual, ...), custom_call_target="tpu_custom_call" | custom-call | flops 3000000000 | bytes 8388608 | tf_op jit(solution)/shard_map/backward/pallas_call | solution.py:525
  44.9 2.6 %collective-permute-start.9 = (bf16[65,32,128]{2,1,0:T(8,128)(2,1)S(1)}, bf16[65,32,128]{2,1,0:T(8,128)(2,1)S(1)}, u32[]{:S(2)}, u32[]{:S(2)}) collective-permute-start(bf16[65,32,128]{2,1,0:T(8,128)(2,1)S(1)} %get-tuple-element.79), channel_id=1, source_target_pairs={{0,1},{1,0},{2,3},{3,2},{4,5},{5,4},{6,7},{7,6},{8,9},{9,8},{10,11... | collective-permute-start | bytes 1597448 | tf_op jit(solution)/shard_map/ppermute | solution.py:555
  49.5 1.9 %collective-permute-start.12 = (bf16[33,32,128]{2,1,0:T(8,128)(2,1)S(1)}, bf16[33,32,128]{2,1,0:T(8,128)(2,1)S(1)}, u32[]{:S(2)}, u32[]{:S(2)}) collective-permute-start(bf16[33,32,128]{2,1,0:T(8,128)(2,1)S(1)} %get-tuple-element.87), channel_id=1, source_target_pairs={{1,3},{2,0},{3,5},{4,2},{5,7},{6,4},{9,11},{10,8},{11,13},{12,10},... | collective-permute-start | bytes 811016 | tf_op jit(solution)/shard_map/ppermute | solution.py:551
  52.9 4.5 %home_gather.2 = (f32[128,32,128]{2,1,0:T(8,128)S(1)}, f32[6,128]{1,0:T(8,128)S(1)}) custom-call(s32[5,1,128]{2,1,0:T(1,128)S(1)} %bitcast.25, f32[6,128]{1,0:T(8,128)S(1)} %get-tuple-element.59.amps, f32[1,128]{1,0:T(1,128)S(1)} %bitcast.30, bf16[128,32,128]{2,1,0:T(8,128)(2,1)S(1)} %bitcast.19, bf16[3,17,32,128]{3,2,1,0:T(8,128)(2,1)S(1)} %home_slots.2.back, ...), custom_call_target="tpu_custom_call" | custom-call | bytes 4194304 | tf_op jit(solution)/shard_map/home_gather/pallas_call | solution.py:525
  57.4 4.0 %collective-permute-done.12.refs_1_ = bf16[33,32,128]{2,1,0:T(8,128)(2,1)S(1)} collective-permute-done((bf16[33,32,128]{2,1,0:T(8,128)(2,1)S(1)}, bf16[33,32,128]{2,1,0:T(8,128)(2,1)S(1)}, u32[]{:S(2)}, u32[]{:S(2)}) %collective-permute-start.12) | collective-permute-done | bytes 270368 | tf_op jit(solution)/shard_map/ppermute | solution.py:551
  63.9 2.0 %update.2 = (f32[128,32,128]{2,1,0:T(8,128)S(1)}, f32[6,128]{1,0:T(8,128)S(1)}, f32[6,128]{1,0:T(8,128)S(1)}, bf16[33,32,128]{2,1,0:T(8,128)(2,1)S(1)}, bf16[33,32,128]{2,1,0:T(8,128)(2,1)S(1)}) custom-call(s32[8,128]{1,0:T(8,128)S(1)} %get-tuple-element.56.places, f32[1,128]{1,0:T(1,128)S(1)} %bitcast.31, s32[5,1,128]{2,1,0:T(1,128)S(1)} %bitcast.26, ...), custom_call_target="tpu_custom_call" | custom-call | bytes 3145728 | tf_op jit(solution)/shard_map/update/pallas_call | solution.py:525
  65.9 4.2 %collective-permute-start.16 = (bf16[33,32,128]{2,1,0:T(8,128)(2,1)S(1)}, bf16[33,32,128]{2,1,0:T(8,128)(2,1)S(1)}, u32[]{:S(2)}, u32[]{:S(2)}) collective-permute-start(bf16[33,32,128]{2,1,0:T(8,128)(2,1)S(1)} %get-tuple-element.94), channel_id=1, source_target_pairs={{0,2},{2,4},{3,1},{4,6},{5,3},{7,5},{8,10},{10,12},{11,9},{12,14},... | collective-permute-start | bytes 811016 | tf_op jit(solution)/shard_map/ppermute | solution.py:551
  73.2 2.0 %home_forward.3.refs_4_ = f32[3,16,64,128]{3,2,1,0:T(8,128)S(1)} custom-call(f32[3,17,32,128]{3,2,1,0:T(8,128)S(1)} %home_sums.3.sums, bf16[3,16,32,128]{3,2,1,0:T(8,128)(2,1)S(1)} %bitcast.21, bf16[16,64,256]{2,1,0:T(8,128)(2,1)S(1)} %get-tuple-element.73.first_t.refs_5_, bf16[3,16,64,64]{3,2,1,0:T(8,128)(2,1)S(1)} %get-tuple-element.74.left.refs_6_), custom_call_target="tpu_custom_call" | custom-call | flops 2000000000 | bytes 4194304 | tf_op jit(solution)/shard_map/home_forward/pallas_call | solution.py:525
  75.2 3.2 %collective-permute-done.15.refs_0_ = bf16[33,32,128]{2,1,0:T(8,128)(2,1)S(1)} collective-permute-done((bf16[33,32,128]{2,1,0:T(8,128)(2,1)S(1)}, bf16[33,32,128]{2,1,0:T(8,128)(2,1)S(1)}, u32[]{:S(2)}, u32[]{:S(2)}) %collective-permute-start.15) | collective-permute-done | bytes 270368 | tf_op jit(solution)/shard_map/ppermute | solution.py:551
  80.5 5.6 %forward.3 = (bf16[3,16,64,128]{3,2,1,0:T(8,128)(2,1)S(1)}, bf16[48,3,64,256]{3,2,1,0:T(8,128)(2,1)S(1)}) custom-call(s32[8,256]{1,0:T(8,128)S(1)} %get-tuple-element.65.plan, f32[3,128]{1,0:T(4,128)S(1)} %order.3.amps, bf16[33,32,128]{2,1,0:T(8,128)(2,1)S(1)} %collective-permute-done.15.refs_0_, bf16[33,32,128]{2,1,0:T(8,128)(2,1)S(1)} %collective-permute-done.16.refs_1_, ...), custom_call_target="tpu_custom_call" | custom-call | flops 3000000000 | bytes 8388608 | tf_op jit(solution)/shard_map/forward/pallas_call | solution.py:525
  86.1 6.8 %backward.3 = (bf16[65,32,128]{2,1,0:T(8,128)(2,1)S(1)}, bf16[65,32,128]{2,1,0:T(8,128)(2,1)S(1)}) custom-call(s32[8,256]{1,0:T(8,128)S(1)} %get-tuple-element.65.plan, f32[3,128]{1,0:T(4,128)S(1)} %order.3.amps, bf16[3,16,64,128]{3,2,1,0:T(8,128)(2,1)S(1)} %get-tuple-element.96.refs_0_.residual, bf16[48,3,64,256]{3,2,1,0:T(8,128)(2,1)S(1)} %get-tuple-element.97.refs_1_, ...), custom_call_target="tpu_custom_call" | custom-call | flops 3000000000 | bytes 8388608 | tf_op jit(solution)/shard_map/backward/pallas_call | solution.py:525
  95.4 1.9 %collective-permute-start.22 = (bf16[33,32,128]{2,1,0:T(8,128)(2,1)S(1)}, bf16[33,32,128]{2,1,0:T(8,128)(2,1)S(1)}, u32[]{:S(2)}, u32[]{:S(2)}) collective-permute-start(bf16[33,32,128]{2,1,0:T(8,128)(2,1)S(1)} %get-tuple-element.106), channel_id=1, source_target_pairs={{1,3},{2,0},{3,5},{4,2},{5,7},{6,4},{9,11},{10,8},{11,13},{12,10},... | collective-permute-start | bytes 811016 | tf_op jit(solution)/shard_map/ppermute | solution.py:551
  97.4 3.0 %home_gather.3 = (f32[128,16,128]{2,1,0:T(8,128)S(1)}, f32[3,128]{1,0:T(4,128)S(1)}) custom-call(s32[5,1,128]{2,1,0:T(1,128)S(1)} %bitcast.28, f32[6,128]{1,0:T(8,128)S(1)} %get-tuple-element.90.amps, f32[1,128]{1,0:T(1,128)S(1)} %bitcast.32, f32[128,32,128]{2,1,0:T(8,128)S(1)} %get-tuple-element.91.morph, bf16[3,17,32,128]{3,2,1,0:T(8,128)(2,1)S(1)} %home_slots.3.back, ...), custom_call_target="tpu_custom_call" | custom-call | bytes 4194304 | tf_op jit(solution)/shard_map/home_gather/pallas_call | solution.py:525
  100.4 5.9 %collective-permute-done.22.refs_1_ = bf16[33,32,128]{2,1,0:T(8,128)(2,1)S(1)} collective-permute-done((bf16[33,32,128]{2,1,0:T(8,128)(2,1)S(1)}, bf16[33,32,128]{2,1,0:T(8,128)(2,1)S(1)}, u32[]{:S(2)}, u32[]{:S(2)}) %collective-permute-start.22) | collective-permute-done | bytes 270368 | tf_op jit(solution)/shard_map/ppermute | solution.py:551
  106.3 1.8 %collective-permute-start.23 = (bf16[33,32,128]{2,1,0:T(8,128)(2,1)S(1)}, bf16[33,32,128]{2,1,0:T(8,128)(2,1)S(1)}, u32[]{:S(2)}, u32[]{:S(2)}) collective-permute-start(bf16[33,32,128]{2,1,0:T(8,128)(2,1)S(1)} %collective-permute-done.21.refs_0_), channel_id=1, source_target_pairs={{0,1},{1,0},{2,3},{3,2},{4,5},{5,4},{6,7},{7,6},{8,9},{9,8},{10,11... | collective-permute-start | bytes 811016 | tf_op jit(solution)/shard_map/ppermute | solution.py:555
  109.7 3.2 %update.3 = (f32[128,2048]{1,0:T(8,128)}, f32[3,1,128]{2,1,0:T(1,128)}) custom-call(s32[8,128]{1,0:T(8,128)S(1)} %get-tuple-element.56.places, f32[1,128]{1,0:T(1,128)S(1)} %bitcast.33, s32[5,1,128]{2,1,0:T(1,128)S(1)} %bitcast.29, f32[1,128]{1,0:T(1,128)S(1)} %bitcast.35, bf16[4,128,128]{2,1,0:T(8,128)(2,1)S(1)} %get-tuple-element.57.hots, ...), custom_call_target="tpu_custom_call" | custom-call | bytes 3145728 | tf_op jit(solution)/shard_map/update/pallas_call | solution.py:525
  (66 shorter events, 28.5 us)
Async XLA Ops:
  1.8 13.9 %collective-permute-start.1 = (bf16[3,4,4096]{2,1,0:T(4,128)(2,1)S(1)}, bf16[3,4,4096]{2,1,0:T(4,128)(2,1)S(1)}, u32[]{:S(2)}, u32[]{:S(2)}) collective-permute-start(bf16[3,4,4096]{2,1,0:T(4,128)(2,1)S(1)} %slice_select_fusion), channel_id=1, source_target_pairs={{0,16},{8,24},{1,17},{9,25},{2,18},{10,26},{3,19},{11,27},{4,20},{... | collective-permute-start | bytes 294920 | tf_op jit(solution)/shard_map/ppermute | solution.py:565
  6.0 3.5 %collective-permute-start = (f32[3,1,128]{2,1,0:T(1,128)}, f32[3,1,128]{2,1,0:T(1,128)S(1)}, u32[]{:S(2)}, u32[]{:S(2)}) collective-permute-start(f32[3,1,128]{2,1,0:T(1,128)} %bitcast.36), channel_id=1, source_target_pairs={{0,1},{1,0},{2,3},{3,2},{4,5},{5,4},{6,7},{7,6},{8,9},{9,8},{10,11... | collective-permute-start | bytes 4616 | tf_op jit(solution)/shard_map/ppermute | solution.py:555
  10.6 8.5 %collective-permute-start.2 = (bf16[33,32,128]{2,1,0:T(8,128)(2,1)S(1)}, bf16[33,32,128]{2,1,0:T(8,128)(2,1)S(1)}, u32[]{:S(2)}, u32[]{:S(2)}) collective-permute-start(bf16[33,32,128]{2,1,0:T(8,128)(2,1)S(1)} %get-tuple-element.61), channel_id=1, source_target_pairs={{0,8},{1,25},{2,10},{3,27},{4,12},{5,29},{6,14},{7,31},{8,16},{9,1... | collective-permute-start | bytes 811016 | tf_op jit(solution)/shard_map/ppermute | solution.py:551
  10.7 8.4 %collective-permute-start.3 = (bf16[33,32,128]{2,1,0:T(8,128)(2,1)S(1)}, bf16[33,32,128]{2,1,0:T(8,128)(2,1)S(1)}, u32[]{:S(2)}, u32[]{:S(2)}) collective-permute-start(bf16[33,32,128]{2,1,0:T(8,128)(2,1)S(1)} %get-tuple-element.62), channel_id=1, source_target_pairs={{0,2},{2,4},{3,1},{4,6},{5,3},{7,5},{8,10},{10,12},{11,9},{12,14},... | collective-permute-start | bytes 811016 | tf_op jit(solution)/shard_map/ppermute | solution.py:551
  19.1 4.3 %collective-permute-start.7 = (bf16[3,4,4096]{2,1,0:T(4,128)(2,1)S(1)}, bf16[3,4,4096]{2,1,0:T(4,128)(2,1)S(1)}, u32[]{:S(2)}, u32[]{:S(2)}) collective-permute-start(bf16[3,4,4096]{2,1,0:T(4,128)(2,1)S(1)} %broadcast_select_fusion.refs_0_), channel_id=1, source_target_pairs={{0,8},{8,0},{16,24},{24,16},{1,9},{9,1},{17,25},{25,17},{2,10},{10... | collective-permute-start | bytes 294920 | tf_op jit(solution)/shard_map/ppermute | solution.py:570
  21.2 5.6 %collective-permute-start.6 = (bf16[3,4,4096]{2,1,0:T(4,128)(2,1)S(1)}, bf16[3,4,4096]{2,1,0:T(4,128)(2,1)S(1)}, u32[]{:S(2)}, u32[]{:S(2)}) collective-permute-start(bf16[3,4,4096]{2,1,0:T(4,128)(2,1)S(1)} %broadcast_select_fusion.refs_0_), channel_id=1, source_target_pairs={{0,4},{2,6},{4,0},{6,2},{1,5},{3,7},{5,1},{7,3},{8,12},{10,14},{12... | collective-permute-start | bytes 294920 | tf_op jit(solution)/shard_map/ppermute | solution.py:568
  21.3 10.7 %collective-permute-start.4 = (bf16[33,32,128]{2,1,0:T(8,128)(2,1)S(1)}, bf16[33,32,128]{2,1,0:T(8,128)(2,1)S(1)}, u32[]{:S(2)}, u32[]{:S(2)}) collective-permute-start(bf16[33,32,128]{2,1,0:T(8,128)(2,1)S(1)} %collective-permute-done.2.refs_0_), channel_id=1, source_target_pairs={{0,1},{1,0},{2,3},{3,2},{4,5},{5,4},{6,7},{7,6},{8,9},{9,8},{10,11... | collective-permute-start | bytes 811016 | tf_op jit(solution)/shard_map/ppermute | solution.py:555
  23.3 8.7 %collective-permute-start.5 = (bf16[33,32,128]{2,1,0:T(8,128)(2,1)S(1)}, bf16[33,32,128]{2,1,0:T(8,128)(2,1)S(1)}, u32[]{:S(2)}, u32[]{:S(2)}) collective-permute-start(bf16[33,32,128]{2,1,0:T(8,128)(2,1)S(1)} %collective-permute-done.3.refs_1_), channel_id=1, source_target_pairs={{0,1},{1,0},{2,3},{3,2},{4,5},{5,4},{6,7},{7,6},{8,9},{9,8},{10,11... | collective-permute-start | bytes 811016 | tf_op jit(solution)/shard_map/ppermute | solution.py:555
  23.4 4.8 %collective-permute-start.8 = (bf16[3,4,4096]{2,1,0:T(4,128)(2,1)S(1)}, bf16[3,4,4096]{2,1,0:T(4,128)(2,1)S(1)}, u32[]{:S(2)}, u32[]{:S(2)}) collective-permute-start(bf16[3,4,4096]{2,1,0:T(4,128)(2,1)S(1)} %collective-permute-done.7.refs_1_), channel_id=1, source_target_pairs={{0,4},{2,6},{4,0},{6,2},{1,5},{3,7},{5,1},{7,3},{8,12},{10,14},{12... | collective-permute-start | bytes 294920 | tf_op jit(solution)/shard_map/ppermute | solution.py:572
  44.9 4.1 %collective-permute-start.9 = (bf16[65,32,128]{2,1,0:T(8,128)(2,1)S(1)}, bf16[65,32,128]{2,1,0:T(8,128)(2,1)S(1)}, u32[]{:S(2)}, u32[]{:S(2)}) collective-permute-start(bf16[65,32,128]{2,1,0:T(8,128)(2,1)S(1)} %get-tuple-element.79), channel_id=1, source_target_pairs={{0,1},{1,0},{2,3},{3,2},{4,5},{5,4},{6,7},{7,6},{8,9},{9,8},{10,11... | collective-permute-start | bytes 1597448 | tf_op jit(solution)/shard_map/ppermute | solution.py:555
  49.0 3.8 %collective-permute-start.10 = (bf16[3,17,32,128]{3,2,1,0:T(8,128)(2,1)S(1)}, bf16[3,17,32,128]{3,2,1,0:T(8,128)(2,1)S(1)}, u32[]{:S(2)}, u32[]{:S(2)}) collective-permute-start(bf16[3,17,32,128]{3,2,1,0:T(8,128)(2,1)S(1)} %home_slots.2.back), channel_id=1, source_target_pairs={{0,1},{1,0},{2,3},{3,2},{4,5},{5,4},{6,7},{7,6},{8,9},{9,8},{10,11... | collective-permute-start | bytes 1253384 | tf_op jit(solution)/shard_map/ppermute | solution.py:555
  49.5 11.9 %collective-permute-start.12 = (bf16[33,32,128]{2,1,0:T(8,128)(2,1)S(1)}, bf16[33,32,128]{2,1,0:T(8,128)(2,1)S(1)}, u32[]{:S(2)}, u32[]{:S(2)}) collective-permute-start(bf16[33,32,128]{2,1,0:T(8,128)(2,1)S(1)} %get-tuple-element.87), channel_id=1, source_target_pairs={{1,3},{2,0},{3,5},{4,2},{5,7},{6,4},{9,11},{10,8},{11,13},{12,10},... | collective-permute-start | bytes 811016 | tf_op jit(solution)/shard_map/ppermute | solution.py:551
  51.5 10.0 %collective-permute-start.11 = (bf16[33,32,128]{2,1,0:T(8,128)(2,1)S(1)}, bf16[33,32,128]{2,1,0:T(8,128)(2,1)S(1)}, u32[]{:S(2)}, u32[]{:S(2)}) collective-permute-start(bf16[33,32,128]{2,1,0:T(8,128)(2,1)S(1)} %get-tuple-element.85), channel_id=1, source_target_pairs={{0,24},{1,9},{2,26},{3,11},{4,28},{5,13},{6,30},{7,15},{8,0},{9,17... | collective-permute-start | bytes 811016 | tf_op jit(solution)/shard_map/ppermute | solution.py:551
  61.4 2.0 %collective-permute-start.13 = (bf16[33,32,128]{2,1,0:T(8,128)(2,1)S(1)}, bf16[33,32,128]{2,1,0:T(8,128)(2,1)S(1)}, u32[]{:S(2)}, u32[]{:S(2)}) collective-permute-start(bf16[33,32,128]{2,1,0:T(8,128)(2,1)S(1)} %collective-permute-done.11.refs_0_), channel_id=1, source_target_pairs={{0,1},{1,0},{2,3},{3,2},{4,5},{5,4},{6,7},{7,6},{8,9},{9,8},{10,11... | collective-permute-start | bytes 811016 | tf_op jit(solution)/shard_map/ppermute | solution.py:555
  62.3 1.6 %collective-permute-start.14 = (bf16[33,32,128]{2,1,0:T(8,128)(2,1)S(1)}, bf16[33,32,128]{2,1,0:T(8,128)(2,1)S(1)}, u32[]{:S(2)}, u32[]{:S(2)}) collective-permute-start(bf16[33,32,128]{2,1,0:T(8,128)(2,1)S(1)} %collective-permute-done.12.refs_1_), channel_id=1, source_target_pairs={{0,1},{1,0},{2,3},{3,2},{4,5},{5,4},{6,7},{7,6},{8,9},{9,8},{10,11... | collective-permute-start | bytes 811016 | tf_op jit(solution)/shard_map/ppermute | solution.py:555
  65.9 9.3 %collective-permute-start.16 = (bf16[33,32,128]{2,1,0:T(8,128)(2,1)S(1)}, bf16[33,32,128]{2,1,0:T(8,128)(2,1)S(1)}, u32[]{:S(2)}, u32[]{:S(2)}) collective-permute-start(bf16[33,32,128]{2,1,0:T(8,128)(2,1)S(1)} %get-tuple-element.94), channel_id=1, source_target_pairs={{0,2},{2,4},{3,1},{4,6},{5,3},{7,5},{8,10},{10,12},{11,9},{12,14},... | collective-permute-start | bytes 811016 | tf_op jit(solution)/shard_map/ppermute | solution.py:551
  70.0 8.4 %collective-permute-start.15 = (bf16[33,32,128]{2,1,0:T(8,128)(2,1)S(1)}, bf16[33,32,128]{2,1,0:T(8,128)(2,1)S(1)}, u32[]{:S(2)}, u32[]{:S(2)}) collective-permute-start(bf16[33,32,128]{2,1,0:T(8,128)(2,1)S(1)} %get-tuple-element.92), channel_id=1, source_target_pairs={{0,8},{1,25},{2,10},{3,27},{4,12},{5,29},{6,14},{7,31},{8,16},{9,1... | collective-permute-start | bytes 811016 | tf_op jit(solution)/shard_map/ppermute | solution.py:551
  78.4 1.6 %collective-permute-start.17 = (bf16[33,32,128]{2,1,0:T(8,128)(2,1)S(1)}, bf16[33,32,128]{2,1,0:T(8,128)(2,1)S(1)}, u32[]{:S(2)}, u32[]{:S(2)}) collective-permute-start(bf16[33,32,128]{2,1,0:T(8,128)(2,1)S(1)} %collective-permute-done.15.refs_0_), channel_id=1, source_target_pairs={{0,1},{1,0},{2,3},{3,2},{4,5},{5,4},{6,7},{7,6},{8,9},{9,8},{10,11... | collective-permute-start | bytes 811016 | tf_op jit(solution)/shard_map/ppermute | solution.py:555
  92.9 2.0 %collective-permute-start.19 = (bf16[65,32,128]{2,1,0:T(8,128)(2,1)S(1)}, bf16[65,32,128]{2,1,0:T(8,128)(2,1)S(1)}, u32[]{:S(2)}, u32[]{:S(2)}) collective-permute-start(bf16[65,32,128]{2,1,0:T(8,128)(2,1)S(1)} %get-tuple-element.98), channel_id=1, source_target_pairs={{0,1},{1,0},{2,3},{3,2},{4,5},{5,4},{6,7},{7,6},{8,9},{9,8},{10,11... | collective-permute-start | bytes 1597448 | tf_op jit(solution)/shard_map/ppermute | solution.py:555
  94.9 2.5 %collective-permute-start.20 = (bf16[3,17,32,128]{3,2,1,0:T(8,128)(2,1)S(1)}, bf16[3,17,32,128]{3,2,1,0:T(8,128)(2,1)S(1)}, u32[]{:S(2)}, u32[]{:S(2)}) collective-permute-start(bf16[3,17,32,128]{3,2,1,0:T(8,128)(2,1)S(1)} %home_slots.3.back), channel_id=1, source_target_pairs={{0,1},{1,0},{2,3},{3,2},{4,5},{5,4},{6,7},{7,6},{8,9},{9,8},{10,11... | collective-permute-start | bytes 1253384 | tf_op jit(solution)/shard_map/ppermute | solution.py:555
  95.4 10.9 %collective-permute-start.22 = (bf16[33,32,128]{2,1,0:T(8,128)(2,1)S(1)}, bf16[33,32,128]{2,1,0:T(8,128)(2,1)S(1)}, u32[]{:S(2)}, u32[]{:S(2)}) collective-permute-start(bf16[33,32,128]{2,1,0:T(8,128)(2,1)S(1)} %get-tuple-element.106), channel_id=1, source_target_pairs={{1,3},{2,0},{3,5},{4,2},{5,7},{6,4},{9,11},{10,8},{11,13},{12,10},... | collective-permute-start | bytes 811016 | tf_op jit(solution)/shard_map/ppermute | solution.py:551
  97.3 9.0 %collective-permute-start.21 = (bf16[33,32,128]{2,1,0:T(8,128)(2,1)S(1)}, bf16[33,32,128]{2,1,0:T(8,128)(2,1)S(1)}, u32[]{:S(2)}, u32[]{:S(2)}) collective-permute-start(bf16[33,32,128]{2,1,0:T(8,128)(2,1)S(1)} %get-tuple-element.104), channel_id=1, source_target_pairs={{0,24},{1,9},{2,26},{3,11},{4,28},{5,13},{6,30},{7,15},{8,0},{9,17... | collective-permute-start | bytes 811016 | tf_op jit(solution)/shard_map/ppermute | solution.py:551
  106.3 3.0 %collective-permute-start.23 = (bf16[33,32,128]{2,1,0:T(8,128)(2,1)S(1)}, bf16[33,32,128]{2,1,0:T(8,128)(2,1)S(1)}, u32[]{:S(2)}, u32[]{:S(2)}) collective-permute-start(bf16[33,32,128]{2,1,0:T(8,128)(2,1)S(1)} %collective-permute-done.21.refs_0_), channel_id=1, source_target_pairs={{0,1},{1,0},{2,3},{3,2},{4,5},{5,4},{6,7},{7,6},{8,9},{9,8},{10,11... | collective-permute-start | bytes 811016 | tf_op jit(solution)/shard_map/ppermute | solution.py:555
  108.1 1.6 %collective-permute-start.24 = (bf16[33,32,128]{2,1,0:T(8,128)(2,1)S(1)}, bf16[33,32,128]{2,1,0:T(8,128)(2,1)S(1)}, u32[]{:S(2)}, u32[]{:S(2)}) collective-permute-start(bf16[33,32,128]{2,1,0:T(8,128)(2,1)S(1)} %collective-permute-done.22.refs_1_), channel_id=1, source_target_pairs={{0,1},{1,0},{2,3},{3,2},{4,5},{5,4},{6,7},{7,6},{8,9},{9,8},{10,11... | collective-permute-start | bytes 811016 | tf_op jit(solution)/shard_map/ppermute | solution.py:555
  (8 other events, 61.9 us)
